TPU v7x, 512 devices: a whole 4x4x16 slice. The times are simulated.
512 devices in a mesh: epoch: 32 (over z, core), row: 4 (over x), col: 4 (over y).
Axes of the slice: x: 4, y: 4, z: 16, core: 2. Of those that a mesh axis runs over, the one named last changes fastest.
Arguments:
- slc_images: bfloat16 [64, 2, 256, 4096], P('epoch', None, 'row', 'col'), may hold values from -3 to 3, as said below
- pair_list: int32 [128, 2], replicated, may hold values from 0 to 63, as said below
- look_sizes: int32 [128, 2], P('epoch'), may hold values from 2 to 8, as said below
Outputs:
- interferogram: float32 [128, 2, 256, 4096], P('epoch', None, 'row', 'col')
- coherence: float32 [128, 256, 4096], P('epoch', 'row', 'col')
Inputs may be any that keep to these rules, and one draw needn't show every extreme that they name: `slc_images`: every pixel's magnitude lies between 0.3 and 3. `pair_list`: pair p's reference lies in aligned block b = p // 4 of 2 acquisitions. For p % 4 == 1 the secondary lies in block (b + 32 / 2) modulo 32; for the other pairs it is 1 to 2 acquisitions later, or, where that passes the last acquisition, as many earlier, and for p % 4 == 0 exactly 2 away. `look_sizes`: row half widths run from 2, column half widths from 4; some pair has 8 in both.
All inputs are finite; a program needn't handle non-finite values.
Results may differ from a plain program's by a relative error of at most 0.0003.
Values may be sent and summed in bfloat16 or wider, within the bound.
No kernel may reach another device: no remote copies, remote signals or barrier semaphores. Data moves between devices by JAX's collectives and lax.ppermute only.
A program may use at most 64 MiB of HBM per device.

v0:
```python
import jax
import jax.numpy as jnp
from jax import lax
from jax.sharding import PartitionSpec as P

HALO = 8


def with_halo(x, sides, width):
    for axis, dim in sides:
        peers, length = (lax.axis_size(axis), x.shape[dim])
        up = [(i, (i + 1) % peers) for i in range(peers - 1)]
        down = [(j, i) for i, j in up]
        last = lax.slice_in_dim(x, length - width, length, axis=dim)
        first = lax.slice_in_dim(x, 0, width, axis=dim)
        before = lax.ppermute(last, axis, up)
        after = lax.ppermute(first, axis, down)
        x = jnp.concatenate([before, x, after], axis=dim)
    return x


def make_products(images):
    ref_re = images[:, 0, 0].astype(jnp.float32)
    ref_im = images[:, 0, 1].astype(jnp.float32)
    sec_re = images[:, 1, 0].astype(jnp.float32)
    sec_im = images[:, 1, 1].astype(jnp.float32)
    return jnp.stack(
        [
            ref_re * sec_re + ref_im * sec_im,
            ref_im * sec_re - ref_re * sec_im,
            ref_re * ref_re + ref_im * ref_im,
            sec_re * sec_re + sec_im * sec_im,
        ],
        axis=1,
    )


def band_matrix(count, halves):
    inner = jnp.arange(count)[None, :, None]
    outer = jnp.arange(count + 2 * HALO)[None, None, :]
    return (jnp.abs(outer - HALO - inner) <= halves[:, None, None]).astype(jnp.float32)


def body(slc_images, pair_list, look_sizes):
    row_count = slc_images.shape[2]
    col_count = slc_images.shape[3]
    groups = lax.axis_size("epoch")
    myself = lax.axis_index("epoch")
    pair_dev = pair_list.shape[0] // groups
    requests = pair_list.reshape(groups, 2 * pair_dev)
    wanted = lax.dynamic_index_in_dim(requests, myself, 0, keepdims=False)
    empty = jnp.zeros((2 * pair_dev, 2, row_count, col_count), jnp.bfloat16)
    piece = lax.all_gather(slc_images, "epoch", axis=0, tiled=True)
    start = jnp.int32(0)
    count = piece.shape[0]
    inside = (wanted >= start) & (wanted < start + count)
    offset = jnp.clip(wanted, 0, count - 1)
    gathered = jnp.where(inside[:, None, None, None], piece[offset], empty)
    images = gathered.reshape(pair_dev, 2, 2, row_count, col_count)
    fields = with_halo(make_products(images), (("row", 2), ("col", 3)), HALO)
    row_band = band_matrix(row_count, look_sizes[:, 0])
    col_band = jnp.swapaxes(band_matrix(col_count, look_sizes[:, 1]), 1, 2)
    by_rows = jnp.einsum("pik,pfkl->pfil", row_band, fields, precision=lax.Precision.HIGHEST)
    box_sums = jnp.einsum("pfil,plj->pfij", by_rows, col_band, precision=lax.Precision.HIGHEST)
    window = ((2 * look_sizes[:, 0] + 1) * (2 * look_sizes[:, 1] + 1)).astype(jnp.float32)[
        :, None, None, None
    ]
    interferogram = box_sums[:, 0:2] / window
    coherence = jnp.sqrt(box_sums[:, 0] ** 2 + box_sums[:, 1] ** 2) / jnp.sqrt(
        box_sums[:, 2] * box_sums[:, 3]
    )
    return (interferogram, coherence)


def solution(mesh):
    placed = (P("epoch", None, "row", "col"), P(), P("epoch", None))
    return jax.shard_map(
        body,
        mesh=mesh,
        in_specs=placed,
        out_specs=(P("epoch", None, "row", "col"), P("epoch", "row", "col")),
        check_vma=False,
    )
```

profile of v0, /device:TPU:1, one launch (start us, length us, event | category | flops | bytes accessed | tf_op | source)
XLA Modules:
  0.0 195.9 jit_solution(14135968795215943830)
XLA Ops:
  7.2 0.7 all-gather.2.cloned.1.call-update
  7.9 0.8 copy.27
  9.0 0.8 slice_bitcast_fusion.1
  9.8 112.8 %all-gather.2.cloned.1.call-done = bf16[64,2,64,1024]{3,2,1,0:T(8,128)(2,1)} async-done(((bf16[2,2,64,1024]{3,2,1,0:T(8,128)(2,1)}), bf16[64,2,64,1024]{3,2,1,0:T(8,128)(2,1)}) %all-gather.2.cloned.1.call-update) | async-done | bytes 16777232 | tf_op jit(solution)/shard_map/all_gather | solution.py:53
  122.7 6.4 %gather_fusion = bf16[8,2,64,1024]{3,2,1,0:T(8,128)(2,1)S(1)} fusion(bf16[64,2,64,1024]{3,2,1,0:T(8,128)(2,1)} %all-gather.2.cloned.1.call-done, s32[1024]{0:T(1024)S(1)} %pad_clamp_fusion), kind=kCustom, calls=%fused_computation | custom fusion | bytes 4194336 | tf_op jit(solution)/shard_map/gather | solution.py:58
  129.3 0.7 fusion.9
  130.2 3.1 %collective-permute-start = (f32[4,4,8,1024]{3,2,1,0:T(8,128)S(1)}, f32[4,4,8,1024]{3,2,1,0:T(8,128)S(1)}, u32[]{:S(2)}, u32[]{:S(2)}) collective-permute-start(f32[4,4,8,1024]{3,2,1,0:T(8,128)S(1)} %get-tuple-element.4), channel_id=1, source_target_pairs={{0,4},{4,8},{8,12},{1,5},{5,9},{9,13},{2,6},{6,10},{10,14},{3,7},{... | collective-permute-start | bytes 1572872 | tf_op jit(solution)/shard_map/ppermute | solution.py:16
  133.3 1.3 collective-permute-start.1
  134.6 2.7 %subtract_abs_fusion = s32[1024,1040]{0,1:T(8,128)} fusion(s32[1040]{0:T(1024)S(1)} %iota_add_fusion), kind=kLoop, calls=%fused_computation.8 | loop fusion | flops 2129920 | bytes 4264000 | tf_op jit(solution)/shard_map/abs | solution.py:41
  137.3 7.0 %collective-permute-done = f32[4,4,8,1024]{3,2,1,0:T(8,128)S(1)} collective-permute-done((f32[4,4,8,1024]{3,2,1,0:T(8,128)S(1)}, f32[4,4,8,1024]{3,2,1,0:T(8,128)S(1)}, u32[]{:S(2)}, u32[]{:S(2)}) %collective-permute-start) | collective-permute-done | bytes 524320 | tf_op jit(solution)/shard_map/ppermute | solution.py:16
  144.3 3.8 %collective-permute-done.1 = f32[4,4,8,1024]{3,2,1,0:T(8,128)S(1)} collective-permute-done((f32[4,4,8,1024]{3,2,1,0:T(8,128)S(1)}, f32[4,4,8,1024]{3,2,1,0:T(8,128)S(1)}, u32[]{:S(2)}, u32[]{:S(2)}) %collective-permute-start.1) | collective-permute-done | bytes 524320 | tf_op jit(solution)/shard_map/ppermute | solution.py:17
  148.1 0.7 pad_maximum_fusion
  148.8 2.4 %copy-done = f32[4,4,80,1024]{3,2,1,0:T(8,128)} copy-done((f32[4,4,80,1024]{3,2,1,0:T(8,128)}, f32[4,4,80,1024]{3,2,1,0:T(8,128)S(1)}, u32[]{:S(2)}) %copy-start) | copy-done | bytes 5242904
  151.2 0.2 fusion.25
  151.6 3.1 %collective-permute-start.2 = (f32[4,4,80,8]{2,3,1,0:T(8,128)S(1)}, f32[4,4,80,8]{2,3,1,0:T(8,128)S(1)}, u32[]{:S(2)}, u32[]{:S(2)}) collective-permute-start(f32[4,4,80,8]{2,3,1,0:T(8,128)S(1)} %copy.33), channel_id=1, source_target_pairs={{0,1},{1,2},{2,3},{4,5},{5,6},{6,7},{8,9},{9,10},{10,11},{12,13},{... | collective-permute-start | bytes 122888 | tf_op jit(solution)/shard_map/ppermute | solution.py:16
  154.9 1.3 collective-permute-start.3
  156.3 0.2 copy.35
  156.5 3.4 %collective-permute-done.3 = f32[4,4,80,8]{2,3,1,0:T(8,128)S(1)} collective-permute-done((f32[4,4,80,8]{2,3,1,0:T(8,128)S(1)}, f32[4,4,80,8]{2,3,1,0:T(8,128)S(1)}, u32[]{:S(2)}, u32[]{:S(2)}) %collective-permute-start.3) | collective-permute-done | bytes 40992 | tf_op jit(solution)/shard_map/ppermute | solution.py:17
  160.0 0.2 copy.36
  160.2 8.2 %concatenate.7 = f32[4,4,80,1040]{3,2,1,0:T(8,128)} concatenate(f32[4,4,80,8]{3,2,1,0:T(8,128)S(1)} %copy.35, f32[4,4,80,1024]{3,2,1,0:T(8,128)} %copy-done, f32[4,4,80,8]{3,2,1,0:T(8,128)S(1)} %copy.36), dimensions={3} | concatenate | bytes 10649600 | tf_op jit(solution)/shard_map/concatenate | solution.py:18
  168.4 5.8 %fusion.19 = f32[4,4,1040,64]{2,3,1,0:T(8,128)S(1)} fusion(f32[4,4,80,1040]{3,2,1,0:T(8,128)} %concatenate.7, s32[64,80]{1,0:T(8,128)S(1)} %subtract_abs_fusion.1, s32[4]{0:T(128)S(1)} %get-tuple-element.10), kind=kOutput, calls=%fused_computation.39 | convolution fusion | flops 1022382080 | bytes 9605136 | tf_op jit(solution)/shard_map/pik,pfkl->pfil/dot_general | solution.py:63
  174.2 11.6 %fusion = f32[4,4,64,1024]{3,2,1,0:T(8,128)S(1)} fusion(s32[1024,1040]{0,1:T(8,128)} %subtract_abs_fusion, s32[4]{0:T(128)S(1)} %get-tuple-element.11, f32[4,4,1040,64]{2,3,1,0:T(8,128)S(1)} %fusion.19), kind=kOutput, calls=%fused_computation.1 | convolution fusion | flops 13090488320 | bytes 12714000 | tf_op jit(solution)/shard_map/pfil,plj->pfij/dot_general | solution.py:64
  185.8 1.5 fusion.16
  187.3 1.7 slice_divide_fusion
  (19 shorter events, 1.1 us)
Async XLA Ops:
  7.2 115.5 %all-gather.2.cloned.1.call-start = ((), (), s32[]{:S(2)}) async-start(), calls=%async_computation | async-start | bytes 17301504 | tf_op jit(solution)/shard_map/all_gather | solution.py:53
  130.2 14.1 %collective-permute-start = (f32[4,4,8,1024]{3,2,1,0:T(8,128)S(1)}, f32[4,4,8,1024]{3,2,1,0:T(8,128)S(1)}, u32[]{:S(2)}, u32[]{:S(2)}) collective-permute-start(f32[4,4,8,1024]{3,2,1,0:T(8,128)S(1)} %get-tuple-element.4), channel_id=1, source_target_pairs={{0,4},{4,8},{8,12},{1,5},{5,9},{9,13},{2,6},{6,10},{10,14},{3,7},{... | collective-permute-start | bytes 1572872 | tf_op jit(solution)/shard_map/ppermute | solution.py:16
  133.3 14.8 %collective-permute-start.1 = (f32[4,4,8,1024]{3,2,1,0:T(8,128)S(1)}, f32[4,4,8,1024]{3,2,1,0:T(8,128)S(1)}, u32[]{:S(2)}, u32[]{:S(2)}) collective-permute-start(f32[4,4,8,1024]{3,2,1,0:T(8,128)S(1)} %get-tuple-element.5), channel_id=1, source_target_pairs={{4,0},{8,4},{12,8},{5,1},{9,5},{13,9},{6,2},{10,6},{14,10},{7,3},{... | collective-permute-start | bytes 1572872 | tf_op jit(solution)/shard_map/ppermute | solution.py:17
  137.3 19.0 %copy-start.1 = (s32[4,2]{0,1:T(2,128)S(1)}, s32[4,2]{0,1:T(2,128)}, u32[]{:S(2)}) copy-start(s32[4,2]{0,1:T(2,128)} %param.5) | copy-start | bytes 100
  148.8 2.4 %copy-start = (f32[4,4,80,1024]{3,2,1,0:T(8,128)}, f32[4,4,80,1024]{3,2,1,0:T(8,128)S(1)}, u32[]{:S(2)}) copy-start(f32[4,4,80,1024]{3,2,1,0:T(8,128)S(1)} %pad_maximum_fusion) | copy-start | bytes 15728644
  151.6 4.7 %collective-permute-start.2 = (f32[4,4,80,8]{2,3,1,0:T(8,128)S(1)}, f32[4,4,80,8]{2,3,1,0:T(8,128)S(1)}, u32[]{:S(2)}, u32[]{:S(2)}) collective-permute-start(f32[4,4,80,8]{2,3,1,0:T(8,128)S(1)} %copy.33), channel_id=1, source_target_pairs={{0,1},{1,2},{2,3},{4,5},{5,6},{6,7},{8,9},{9,10},{10,11},{12,13},{... | collective-permute-start | bytes 122888 | tf_op jit(solution)/shard_map/ppermute | solution.py:16
  154.9 5.0 %collective-permute-start.3 = (f32[4,4,80,8]{2,3,1,0:T(8,128)S(1)}, f32[4,4,80,8]{2,3,1,0:T(8,128)S(1)}, u32[]{:S(2)}, u32[]{:S(2)}) collective-permute-start(f32[4,4,80,8]{2,3,1,0:T(8,128)S(1)} %copy.34), channel_id=1, source_target_pairs={{1,0},{2,1},{3,2},{5,4},{6,5},{7,6},{9,8},{10,9},{11,10},{13,12},{... | collective-permute-start | bytes 122888 | tf_op jit(solution)/shard_map/ppermute | solution.py:17
Sparse Core Ops, SparseCore 0:
  10.1 112.4 all-gather.1
where the time goes:
time: 198 us; the launch traced here: 196 us
  waiting for transfers between devices  128 us (65%)
  local copies, waits for them, and re-layouts  19.9 us (10%)
  matrix products  17.4 us (9%)
  between operations  14.2 us (7%)
  starting transfers between devices  8.9 us (4%)
  other arithmetic  7.63 us (4%)
    all_gather x1, waiting for transfers between devices, body(): piece = lax.all_gather(slc_images, 'epoch', axis=0, tiled=True)  113 us
    dot_general x1, matrix products, body(): jnp.einsum('pfil,plj->pfij', by_rows, col_band, precision=lax.Precision.H...  11.6 us
    concatenate x1, local copies, waits for them, and re-layouts, with_halo(): x = jnp.concatenate([before, x, after], axis=dim)  8.17 us
    ppermute x2, waiting for transfers between devices, with_halo(): after = lax.ppermute(first, axis, down)  7.25 us
    ppermute x2, waiting for transfers between devices, with_halo(): before = lax.ppermute(last, axis, up)  7.03 us
    gather x1, local copies, waits for them, and re-layouts, body(): gathered = jnp.where(inside[:, None, None, None], piece[offset], empty)  6.45 us
    ppermute x2, starting transfers between devices, with_halo(): before = lax.ppermute(last, axis, up)  6.26 us
    dot_general x1, matrix products, body(): jnp.einsum('pik,pfkl->pfil', row_band, fields, precision=lax.Precision.HI...  5.8 us
  transfers between devices with their start and end apart: 5, of which 4 were waited for; matrix products, arithmetic and copies ran while one was open for 3% of the time, Pallas kernels for 0%

commit v1 on v0

v1 whole, which is shorter than its diff:
```python
import functools

import jax
import jax.numpy as jnp
from jax import lax
from jax.experimental import pallas as pl
from jax.experimental.pallas import tpu as pltpu
from jax.sharding import PartitionSpec as P

HALO = 8
LANES = 128
ROWS = 64
COLS = 1024
BLOCKS = COLS // LANES
PADDED = ROWS + 2 * HALO
F32 = jnp.float32
BF16 = jnp.bfloat16
VMEM_LIMIT = 48 * 1024 * 1024


def lane_iota(rows):
    return lax.broadcasted_iota(jnp.int32, (rows, LANES), 1)


def move_strip(values, source, target):
    return pltpu.roll(values, (target - source) % LANES, 1)


def put_strip(total, values, source, target):
    lane = lane_iota(values.shape[0])
    inside = (lane >= target) & (lane < target + HALO)
    return jnp.where(inside, move_strip(values, source, target), total)


def block(index):
    return slice(index * LANES, (index + 1) * LANES)


def far_lane(part, field, side):
    return HALO * (part * 4 + field * 2 + side)


def split_far_kernel(which, images, border, inner):
    lead = which[0]
    strips = jnp.zeros((16, LANES), F32)
    for column in range(BLOCKS):
        for field in range(2):
            values = images[lead, field, :, block(column)].astype(F32)
            rows = jnp.concatenate([values[:HALO], values[ROWS - HALO :]], axis=0)
            border[pl.ds(column * 32 + field * 16, 16), :] = rows.astype(BF16)
            inner[field, :, block(column)] = values[HALO : ROWS - HALO].astype(BF16)
            for side, at in ((0, 0), (1, BLOCKS - 1)):
                if column == at:
                    for part in range(3):
                        begin = HALO + 16 * part
                        strips = put_strip(
                            strips,
                            values[begin : begin + 16],
                            side * (LANES - HALO),
                            far_lane(part, field, side),
                        )
    border[pl.ds(BLOCKS * 32, 16), :] = strips.astype(BF16)


def top_and_bottom(images, chip_next, far_next, border, acquisition, field, column):
    if acquisition < 4:
        if acquisition < 2:
            first = images[acquisition, field, :16, block(column)].astype(F32)
            last = images[acquisition, field, ROWS - 16 :, block(column)].astype(F32)
        else:
            k = acquisition - 2
            first = chip_next[k, field, :16, block(column)].astype(F32) + far_next[
                k, field, :16, block(column)
            ].astype(F32)
            last = chip_next[k, field, ROWS - 16 :, block(column)].astype(F32) + far_next[
                k, field, ROWS - 16 :, block(column)
            ].astype(F32)
        return first[:HALO], last[HALO:]
    rows = border[pl.ds(column * 32 + field * 16, 16), :].astype(F32)
    return rows[:HALO], rows[HALO:]


def pack_rows_kernel(images, chip_next, far_next, border, up, down):
    for acquisition in range(5):
        at = pl.ds(acquisition * 16, 16)
        for column in range(BLOCKS):
            tops, bottoms = [], []
            for field in range(2):
                top, bottom = top_and_bottom(
                    images, chip_next, far_next, border, acquisition, field, column
                )
                tops.append(top)
                bottoms.append(bottom)
            up[at, block(column)] = jnp.concatenate(tops, axis=0).astype(BF16)
            down[at, block(column)] = jnp.concatenate(bottoms, axis=0).astype(BF16)


def halo_rows(above, below, acquisition, field, column):
    at = pl.ds(acquisition * 16, 16)
    rows = slice(field * HALO, (field + 1) * HALO)
    return (
        above[at, block(column)].astype(F32)[rows],
        below[at, block(column)].astype(F32)[rows],
    )


def pack_columns_kernel(images, chip_next, far_next, border, above, below, left, right):
    strips = border[pl.ds(BLOCKS * 32, 16), :].astype(F32)
    totals = [jnp.zeros((PADDED, LANES), F32), jnp.zeros((PADDED, LANES), F32)]
    for acquisition in range(5):
        for field in range(2):
            target = HALO * (2 * acquisition + field)
            for side, column in ((0, 0), (1, BLOCKS - 1)):
                source = side * (LANES - HALO)
                before, after = halo_rows(above, below, acquisition, field, column)
                if acquisition < 2:
                    main = images[acquisition, field, :, block(column)].astype(F32)
                elif acquisition < 4:
                    k = acquisition - 2
                    main = chip_next[k, field, :, block(column)].astype(F32) + far_next[
                        k, field, :, block(column)
                    ].astype(F32)
                else:
                    rows = border[pl.ds(column * 32 + field * 16, 16), :].astype(F32)
                    inner = [
                        move_strip(strips, far_lane(part, field, side), source)
                        for part in range(3)
                    ]
                    main = jnp.concatenate([rows[:HALO], *inner, rows[HALO:]], axis=0)
                values = jnp.concatenate([before, main, after], axis=0)
                totals[side] = put_strip(totals[side], values, source, target)
    left[...] = totals[0].astype(BF16)
    right[...] = totals[1].astype(BF16)


def halo_block(from_left, from_right, acquisition, field):
    source = HALO * (2 * acquisition + field)
    blank = jnp.zeros((PADDED, LANES), F32)
    after = put_strip(blank, from_right[...].astype(F32), source, 0)
    return put_strip(after, from_left[...].astype(F32), source, LANES - HALO)


def box_sums(reference, secondary, looks, products, sums, write):
    half_rows, half_cols = looks
    for column in range(BLOCKS + 1):
        at = block(column)
        a, b = reference(0, at), reference(1, at)
        c, d = secondary(0, at), secondary(1, at)
        fields = (a * c + b * d, b * c - a * d, a * a + b * b, c * c + d * d)
        for f, value in enumerate(fields):
            high = value.astype(BF16)
            products[f, :PADDED, at] = high
            products[f, PADDED:, at] = (value - high.astype(F32)).astype(BF16)
    inner = lax.broadcasted_iota(jnp.int32, (ROWS, 2 * PADDED), 0)
    outer = lax.broadcasted_iota(jnp.int32, (ROWS, 2 * PADDED), 1)
    outer = jnp.where(outer >= PADDED, outer - PADDED, outer)
    row_band = (jnp.abs(outer - HALO - inner) <= half_rows).astype(F32).astype(BF16)
    outer = lax.broadcasted_iota(jnp.int32, (4 * LANES, 2 * LANES), 0)
    inner = lax.broadcasted_iota(jnp.int32, (4 * LANES, 2 * LANES), 1)
    col_band = (jnp.abs(outer - LANES - inner) <= half_cols).astype(F32).astype(BF16)
    for f in range(4):
        by_rows = jnp.dot(row_band, products[f], preferred_element_type=F32)
        high = by_rows.astype(BF16)
        low = (by_rows - high.astype(F32)).astype(BF16)
        for part, value in ((0, high), (1, low)):
            at = slice((2 * f + part) * ROWS, (2 * f + part + 1) * ROWS)
            sums[at, LANES : LANES + COLS] = value[:, :COLS]
            sums[at, :LANES] = value[:, COLS:]
            sums[at, LANES + COLS :] = value[:, COLS:]
    window = ((2 * half_rows + 1) * (2 * half_cols + 1)).astype(F32)
    scale = 1.0 / jnp.full((ROWS, 2 * LANES), window, F32)
    for j in range(BLOCKS // 2):
        both = jnp.dot(
            sums[:, j * 256 : j * 256 + 512], col_band, preferred_element_type=F32
        )
        real, imag, power, other = (
            both[2 * f * ROWS : (2 * f + 1) * ROWS] + both[(2 * f + 1) * ROWS : (2 * f + 2) * ROWS]
            for f in range(4)
        )
        coherence = jnp.sqrt(real * real + imag * imag) / jnp.sqrt(power * other)
        write(slice(j * 256, (j + 1) * 256), real * scale, imag * scale, coherence)


def near_kernel(
    table, images, chip_next, far_next, above, below, from_left, from_right,
    interferogram, coherence, staged, products, sums,
):
    step = pl.program_id(0)

    @pl.when(step == 0)
    def _():
        for acquisition in range(4):
            for field in range(2):
                for column in range(BLOCKS):
                    before, after = halo_rows(above, below, acquisition, field, column)
                    if acquisition < 2:
                        main = images[acquisition, field, :, block(column)].astype(F32)
                    else:
                        k = acquisition - 2
                        main = chip_next[k, field, :, block(column)].astype(F32) + far_next[
                            k, field, :, block(column)
                        ].astype(F32)
                    staged[acquisition, field, :, block(column)] = jnp.concatenate(
                        [before, main, after], axis=0
                    )
                staged[acquisition, field, :, block(BLOCKS)] = halo_block(
                    from_left, from_right, acquisition, field
                )

    pair = jnp.where(step == 0, 0, step + 1)
    first, second = table[pair, 0], table[pair, 1]

    def write(at, real, imag, value):
        interferogram[0, 0, :, at] = real
        interferogram[0, 1, :, at] = imag
        coherence[0, :, at] = value

    box_sums(
        lambda field, at: staged[first, field, :, at],
        lambda field, at: staged[second, field, :, at],
        (table[pair, 2], table[pair, 3]),
        products,
        sums,
        write,
    )


def far_kernel(
    table, images, border, inner, above, below, from_left, from_right, _, __,
    interferogram, coherence, staged, products, sums,
):
    first = table[1, 0]
    for acquisition in range(2):

        @pl.when(first == acquisition)
        def _(acquisition=acquisition):
            for field in range(2):
                for column in range(BLOCKS):
                    before, after = halo_rows(above, below, acquisition, field, column)
                    main = images[acquisition, field, :, block(column)].astype(F32)
                    staged[0, field, :, block(column)] = jnp.concatenate(
                        [before, main, after], axis=0
                    )
                staged[0, field, :, block(BLOCKS)] = halo_block(
                    from_left, from_right, acquisition, field
                )

    for field in range(2):
        for column in range(BLOCKS):
            before, after = halo_rows(above, below, 4, field, column)
            rows = border[pl.ds(column * 32 + field * 16, 16), :].astype(F32)
            main = inner[field, :, block(column)].astype(F32)
            staged[1, field, :, block(column)] = jnp.concatenate(
                [before, rows[:HALO], main, rows[HALO:], after], axis=0
            )
        staged[1, field, :, block(BLOCKS)] = halo_block(from_left, from_right, 4, field)

    def write(at, real, imag, value):
        interferogram[0, 0, :, at] = real
        interferogram[0, 1, :, at] = imag
        coherence[0, :, at] = value

    box_sums(
        lambda field, at: staged[0, field, :, at],
        lambda field, at: staged[1, field, :, at],
        (table[1, 2], table[1, 3]),
        products,
        sums,
        write,
    )


VMEM = pl.BlockSpec(memory_space=pltpu.VMEM)
SMEM = pl.BlockSpec(memory_space=pltpu.SMEM)
PARAMS = pltpu.CompilerParams(vmem_limit_bytes=VMEM_LIMIT)


def shape(dims, dtype=BF16):
    return jax.ShapeDtypeStruct(dims, dtype)


def scratch(acquisitions):
    return [
        pltpu.VMEM((acquisitions, 2, PADDED, COLS + LANES), F32),
        pltpu.VMEM((4, 2 * PADDED, COLS + LANES), BF16),
        pltpu.VMEM((8 * ROWS, COLS + 2 * LANES), BF16),
    ]


def exchange(first, last, axis):
    peers = lax.axis_size(axis)
    up = [(i, i + 1) for i in range(peers - 1)]
    down = [(j, i) for i, j in up]
    return lax.ppermute(last, axis, up), lax.ppermute(first, axis, down)


def body(slc_images, pair_list, look_sizes):
    groups = lax.axis_size("epoch")
    half = groups // 2
    myself = lax.axis_index("epoch")

    inside = [(b + 1, b) for b in range(0, groups, 2)] + [(groups - 2, groups - 1)]
    across = [(b + 1, b) for b in range(1, groups - 1, 2)]
    far_next = lax.ppermute(slc_images, "epoch", across)

    asker = (myself + half) % groups
    asked = lax.dynamic_slice(pair_list, (4 * asker + 1, 1), (1, 1))[0] - 2 * myself
    border, inner = pl.pallas_call(
        split_far_kernel,
        in_specs=[SMEM, VMEM],
        out_specs=[VMEM, VMEM],
        out_shape=[
            shape((BLOCKS * 32 + 16, LANES)),
            shape((2, ROWS - 2 * HALO, COLS)),
        ],
        compiler_params=PARAMS,
        name="split_far",
    )(asked, slc_images)
    swap = [(b, (b + half) % groups) for b in range(groups)]
    border = lax.ppermute(border, "epoch", swap)
    inner = lax.ppermute(inner, "epoch", swap)

    chip_next = lax.ppermute(slc_images, "epoch", inside)

    up, down = pl.pallas_call(
        pack_rows_kernel,
        in_specs=[VMEM] * 4,
        out_specs=[VMEM, VMEM],
        out_shape=[shape((80, COLS))] * 2,
        compiler_params=PARAMS,
        name="pack_rows",
    )(slc_images, chip_next, far_next, border)
    above, below = exchange(up, down, "row")
    left, right = pl.pallas_call(
        pack_columns_kernel,
        in_specs=[VMEM] * 6,
        out_specs=[VMEM, VMEM],
        out_shape=[shape((PADDED, LANES))] * 2,
        compiler_params=PARAMS,
        name="pack_columns",
    )(slc_images, chip_next, far_next, border, above, below)
    from_left, from_right = exchange(left, right, "col")

    mine = lax.dynamic_slice_in_dim(pair_list, 4 * myself, 4, axis=0)
    near = (mine // 2) == myself
    slots = jnp.where(near, 0, 2) + mine % 2
    table = jnp.concatenate([slots, look_sizes], axis=1)

    outs = [
        shape((4, 2, ROWS, COLS), F32),
        shape((4, ROWS, COLS), F32),
    ]
    interferogram, coherence = pl.pallas_call(
        near_kernel,
        grid=(3,),
        in_specs=[SMEM] + [VMEM] * 7,
        out_specs=[
            pl.BlockSpec((1, 2, ROWS, COLS), lambda i: (jnp.where(i == 0, 0, i + 1), 0, 0, 0)),
            pl.BlockSpec((1, ROWS, COLS), lambda i: (jnp.where(i == 0, 0, i + 1), 0, 0)),
        ],
        out_shape=outs,
        scratch_shapes=scratch(4),
        compiler_params=PARAMS,
        name="near_pairs",
    )(table, slc_images, chip_next, far_next, above, below, from_left, from_right)
    return pl.pallas_call(
        far_kernel,
        grid=(1,),
        in_specs=[SMEM] + [VMEM] * 7 + [pl.BlockSpec(memory_space=pl.ANY)] * 2,
        out_specs=[
            pl.BlockSpec((1, 2, ROWS, COLS), lambda i: (1, 0, 0, 0)),
            pl.BlockSpec((1, ROWS, COLS), lambda i: (1, 0, 0)),
        ],
        out_shape=outs,
        scratch_shapes=scratch(2),
        input_output_aliases={8: 0, 9: 1},
        compiler_params=PARAMS,
        name="far_pair",
    )(table, slc_images, border, inner, above, below, from_left, from_right, interferogram, coherence)


def solution(mesh):
    placed = (P("epoch", None, "row", "col"), P(), P("epoch", None))
    return jax.shard_map(
        body,
        mesh=mesh,
        in_specs=placed,
        out_specs=(P("epoch", None, "row", "col"), P("epoch", "row", "col")),
        check_vma=False,
    )
```

time: 198 us -> 63.2 us (0.32)
  the two profiles are of different devices: /device:TPU:1 before, /device:TPU:385 now
where the time goes in v1:
time: 63.2 us; the launch traced here: 62.8 us
  starting transfers between devices  29.6 us (47%)
  waiting for transfers between devices  19.2 us (30%)
  Pallas kernels  9.6 us (15%)
  local copies, waits for them, and re-layouts  2.94 us (5%)
  between operations  1.44 us (2%)
    ppermute x1, starting transfers between devices, body(): inner = lax.ppermute(inner, 'epoch', swap)  12.1 us
    ppermute x1, waiting for transfers between devices, body(): border = lax.ppermute(border, 'epoch', swap)  11.4 us
    ppermute x4, starting transfers between devices, exchange(): return (lax.ppermute(last, axis, up), lax.ppermute(first, axis, down))  9.13 us
    ppermute x4, waiting for transfers between devices, exchange(): return (lax.ppermute(last, axis, up), lax.ppermute(first, axis, down))  7.79 us
    pallas_call x1, Pallas kernels, body(): pl.pallas_call(near_kernel, grid=(3,), in_specs=[SMEM] + [VMEM] * 7, out_...  6.27 us
    ppermute x1, starting transfers between devices, body(): chip_next = lax.ppermute(slc_images, 'epoch', inside)  4.92 us
    pallas_call x1, Pallas kernels, body(): pl.pallas_call(far_kernel, grid=(1,), in_specs=[SMEM] + [VMEM] * 7 + [pl....  2.94 us
    unnamed x12, local copies, waits for them, and re-layouts  2.28 us
  transfers between devices with their start and end apart: 8, of which 4 were waited for; matrix products, arithmetic and copies ran while one was open for 1% of the time, Pallas kernels for 11%

profile of v1, /device:TPU:385, one launch (start us, length us, event | category | flops | bytes accessed | tf_op | source)
XLA Modules:
  0.0 62.8 jit_solution(14652343960463669964)
XLA Ops:
  0.7 1.4 %collective-permute-start.3 = (bf16[2,2,64,1024]{3,2,1,0:T(8,128)(2,1)}, bf16[2,2,64,1024]{3,2,1,0:T(8,128)(2,1)S(1)}, u32[]{:S(2)}, u32[]{:S(2)}) collective-permute-start(bf16[2,2,64,1024]{3,2,1,0:T(8,128)(2,1)} %images.9), channel_id=1, source_target_pairs={{32,16},{64,48},{96,80},{128,112},{160,144},{192,176},{224,208},{2... | collective-permute-start | bytes 1572872 | tf_op jit(solution)/shard_map/ppermute | solution.py:304
  2.1 4.9 %collective-permute-start.2 = (bf16[2,2,64,1024]{3,2,1,0:T(8,128)(2,1)}, bf16[2,2,64,1024]{3,2,1,0:T(8,128)(2,1)S(1)}, u32[]{:S(2)}, u32[]{:S(2)}) collective-permute-start(bf16[2,2,64,1024]{3,2,1,0:T(8,128)(2,1)} %images.9), channel_id=1, source_target_pairs={{16,0},{48,32},{80,64},{112,96},{144,128},{176,160},{208,192},{240... | collective-permute-start | bytes 1572872 | tf_op jit(solution)/shard_map/ppermute | solution.py:323
  7.0 0.6 constant_dynamic-slice_fusion
  8.3 1.0 %copy-done.1 = bf16[2,2,64,1024]{3,2,1,0:T(8,128)(2,1)S(1)} copy-done((bf16[2,2,64,1024]{3,2,1,0:T(8,128)(2,1)S(1)}, bf16[2,2,64,1024]{3,2,1,0:T(8,128)(2,1)}, u32[]{:S(2)}) %copy-start.1) | copy-done | bytes 524312
  9.3 0.1 split_far.1
  9.4 2.1 %collective-permute-start = (bf16[272,128]{1,0:T(8,128)(2,1)S(1)}, bf16[272,128]{1,0:T(8,128)(2,1)S(1)}, u32[]{:S(2)}, u32[]{:S(2)}) collective-permute-start(bf16[272,128]{1,0:T(8,128)(2,1)S(1)} %get-tuple-element.10), channel_id=1, source_target_pairs={{0,256},{16,272},{32,288},{48,304},{64,320},{80,336},{96,352},{112... | collective-permute-start | bytes 208904 | tf_op jit(solution)/shard_map/ppermute | solution.py:320
  11.5 12.1 %collective-permute-start.1 = (bf16[2,48,1024]{2,1,0:T(8,128)(2,1)S(1)}, bf16[2,48,1024]{2,1,0:T(8,128)(2,1)S(1)}, u32[]{:S(2)}, u32[]{:S(2)}) collective-permute-start(bf16[2,48,1024]{2,1,0:T(8,128)(2,1)S(1)} %get-tuple-element.11), channel_id=1, source_target_pairs={{0,256},{16,272},{32,288},{48,304},{64,320},{80,336},{96,352},{112... | collective-permute-start | bytes 589832 | tf_op jit(solution)/shard_map/ppermute | solution.py:321
  23.6 0.1 constant_dynamic-slice_fusion.1
  23.7 0.1 copy.9
  23.8 11.4 %collective-permute-done.border = bf16[272,128]{1,0:T(8,128)(2,1)S(1)} collective-permute-done((bf16[272,128]{1,0:T(8,128)(2,1)S(1)}, bf16[272,128]{1,0:T(8,128)(2,1)S(1)}, u32[]{:S(2)}, u32[]{:S(2)}) %collective-permute-start) | collective-permute-done | bytes 69664 | tf_op jit(solution)/shard_map/ppermute | solution.py:320
  35.1 1.0 %copy-done.2 = bf16[2,2,64,1024]{3,2,1,0:T(8,128)(2,1)S(1)} copy-done((bf16[2,2,64,1024]{3,2,1,0:T(8,128)(2,1)S(1)}, bf16[2,2,64,1024]{3,2,1,0:T(8,128)(2,1)}, u32[]{:S(2)}) %copy-start.2) | copy-done | bytes 524312
  36.2 0.1 pack_rows.1
  36.2 3.3 %collective-permute-start.4 = (bf16[80,1024]{1,0:T(8,128)(2,1)S(1)}, bf16[80,1024]{1,0:T(8,128)(2,1)S(1)}, u32[]{:S(2)}, u32[]{:S(2)}) collective-permute-start(bf16[80,1024]{1,0:T(8,128)(2,1)S(1)} %get-tuple-element.12), channel_id=1, source_target_pairs={{0,4},{4,8},{8,12},{1,5},{5,9},{9,13},{2,6},{6,10},{10,14},{3,7},{... | collective-permute-start | bytes 491528 | tf_op jit(solution)/shard_map/ppermute | solution.py:294
  39.6 1.3 %collective-permute-start.5 = (bf16[80,1024]{1,0:T(8,128)(2,1)S(1)}, bf16[80,1024]{1,0:T(8,128)(2,1)S(1)}, u32[]{:S(2)}, u32[]{:S(2)}) collective-permute-start(bf16[80,1024]{1,0:T(8,128)(2,1)S(1)} %get-tuple-element.13), channel_id=1, source_target_pairs={{4,0},{8,4},{12,8},{5,1},{9,5},{13,9},{6,2},{10,6},{14,10},{7,3},{... | collective-permute-start | bytes 491528 | tf_op jit(solution)/shard_map/ppermute | solution.py:294
  40.9 0.1 copy.8
  41.0 0.8 %collective-permute-done.4.above = bf16[80,1024]{1,0:T(8,128)(2,1)S(1)} collective-permute-done((bf16[80,1024]{1,0:T(8,128)(2,1)S(1)}, bf16[80,1024]{1,0:T(8,128)(2,1)S(1)}, u32[]{:S(2)}, u32[]{:S(2)}) %collective-permute-start.4) | collective-permute-done | bytes 163872 | tf_op jit(solution)/shard_map/ppermute | solution.py:294
  41.8 3.8 %collective-permute-done.5.below = bf16[80,1024]{1,0:T(8,128)(2,1)S(1)} collective-permute-done((bf16[80,1024]{1,0:T(8,128)(2,1)S(1)}, bf16[80,1024]{1,0:T(8,128)(2,1)S(1)}, u32[]{:S(2)}, u32[]{:S(2)}) %collective-permute-start.5) | collective-permute-done | bytes 163872 | tf_op jit(solution)/shard_map/ppermute | solution.py:294
  45.7 0.2 pack_columns.1
  45.9 3.2 %collective-permute-start.6 = (bf16[80,128]{1,0:T(8,128)(2,1)S(1)}, bf16[80,128]{1,0:T(8,128)(2,1)S(1)}, u32[]{:S(2)}, u32[]{:S(2)}) collective-permute-start(bf16[80,128]{1,0:T(8,128)(2,1)S(1)} %get-tuple-element.14), channel_id=1, source_target_pairs={{0,1},{1,2},{2,3},{4,5},{5,6},{6,7},{8,9},{9,10},{10,11},{12,13},{... | collective-permute-start | bytes 61448 | tf_op jit(solution)/shard_map/ppermute | solution.py:294
  49.1 1.3 %collective-permute-start.7 = (bf16[80,128]{1,0:T(8,128)(2,1)S(1)}, bf16[80,128]{1,0:T(8,128)(2,1)S(1)}, u32[]{:S(2)}, u32[]{:S(2)}) collective-permute-start(bf16[80,128]{1,0:T(8,128)(2,1)S(1)} %get-tuple-element.15), channel_id=1, source_target_pairs={{1,0},{2,1},{3,2},{5,4},{6,5},{7,6},{9,8},{10,9},{11,10},{13,12},{... | collective-permute-start | bytes 61448 | tf_op jit(solution)/shard_map/ppermute | solution.py:294
  50.4 0.1 pad_add_fusion.table
  50.5 3.1 %collective-permute-done.7.from_right = bf16[80,128]{1,0:T(8,128)(2,1)S(1)} collective-permute-done((bf16[80,128]{1,0:T(8,128)(2,1)S(1)}, bf16[80,128]{1,0:T(8,128)(2,1)S(1)}, u32[]{:S(2)}, u32[]{:S(2)}) %collective-permute-start.7) | collective-permute-done | bytes 20512 | tf_op jit(solution)/shard_map/ppermute | solution.py:294
  53.6 6.3 %near_pairs.1 = (f32[4,2,64,1024]{3,2,1,0:T(8,128)}, f32[4,64,1024]{2,1,0:T(8,128)}) custom-call(s32[4,4]{1,0:T(4,128)S(1)} %pad_add_fusion.table, bf16[2,2,64,1024]{3,2,1,0:T(8,128)(2,1)S(1)} %copy-done.3, bf16[2,2,64,1024]{3,2,1,0:T(8,128)(2,1)S(1)} %collective-permute-done.2.chip_next, bf16[2,2,64,1024]{3,2,1,0:T(8,128)(2,1)S(1)} %collective-permute-done.3.far_next, ...), custom_call_target="tpu_custom_call" | custom-call | tf_op jit(solution)/shard_map/near_pairs/pallas_call | solution.py:353
  59.9 2.9 %far_pair.1 = (f32[4,2,64,1024]{3,2,1,0:T(8,128)}, f32[4,64,1024]{2,1,0:T(8,128)}) custom-call(s32[4,4]{1,0:T(4,128)S(1)} %pad_add_fusion.table, bf16[2,2,64,1024]{3,2,1,0:T(8,128)(2,1)S(1)} %copy-done.3, bf16[272,128]{1,0:T(8,128)(2,1)S(1)} %collective-permute-done.border, ...), custom_call_target="tpu_custom_call", output_to_operand_aliasing={{0}: (8, {}), {1}: (9, {})} | custom-call | tf_op jit(solution)/shard_map/far_pair/pallas_call | solution.py:366
  (13 shorter events, 0.0 us)
Async XLA Ops:
  0.6 6.4 %copy-start = (s32[128,2]{0,1:T(2,128)S(1)}, s32[128,2]{0,1:T(2,128)}, u32[]{:S(2)}) copy-start(s32[128,2]{0,1:T(2,128)} %param.4) | copy-start | bytes 3076
  0.6 40.3 %copy-start.4 = (s32[4,2]{0,1:T(2,128)S(1)}, s32[4,2]{0,1:T(2,128)}, u32[]{:S(2)}) copy-start(s32[4,2]{0,1:T(2,128)} %param.5) | copy-start | bytes 100
  0.7 34.5 %collective-permute-start.3 = (bf16[2,2,64,1024]{3,2,1,0:T(8,128)(2,1)}, bf16[2,2,64,1024]{3,2,1,0:T(8,128)(2,1)S(1)}, u32[]{:S(2)}, u32[]{:S(2)}) collective-permute-start(bf16[2,2,64,1024]{3,2,1,0:T(8,128)(2,1)} %images.9), channel_id=1, source_target_pairs={{32,16},{64,48},{96,80},{128,112},{160,144},{192,176},{224,208},{2... | collective-permute-start | bytes 1572872 | tf_op jit(solution)/shard_map/ppermute | solution.py:304
  2.1 33.1 %collective-permute-start.2 = (bf16[2,2,64,1024]{3,2,1,0:T(8,128)(2,1)}, bf16[2,2,64,1024]{3,2,1,0:T(8,128)(2,1)S(1)}, u32[]{:S(2)}, u32[]{:S(2)}) collective-permute-start(bf16[2,2,64,1024]{3,2,1,0:T(8,128)(2,1)} %images.9), channel_id=1, source_target_pairs={{16,0},{48,32},{80,64},{112,96},{144,128},{176,160},{208,192},{240... | collective-permute-start | bytes 1572872 | tf_op jit(solution)/shard_map/ppermute | solution.py:323
  8.3 1.0 %copy-start.1 = (bf16[2,2,64,1024]{3,2,1,0:T(8,128)(2,1)S(1)}, bf16[2,2,64,1024]{3,2,1,0:T(8,128)(2,1)}, u32[]{:S(2)}) copy-start(bf16[2,2,64,1024]{3,2,1,0:T(8,128)(2,1)} %images.9) | copy-start | bytes 1572868
  9.3 36.3 %copy-start.3 = (bf16[2,2,64,1024]{3,2,1,0:T(8,128)(2,1)S(1)}, bf16[2,2,64,1024]{3,2,1,0:T(8,128)(2,1)}, u32[]{:S(2)}) copy-start(bf16[2,2,64,1024]{3,2,1,0:T(8,128)(2,1)} %images.9) | copy-start | bytes 1572868
  9.4 25.7 %collective-permute-start = (bf16[272,128]{1,0:T(8,128)(2,1)S(1)}, bf16[272,128]{1,0:T(8,128)(2,1)S(1)}, u32[]{:S(2)}, u32[]{:S(2)}) collective-permute-start(bf16[272,128]{1,0:T(8,128)(2,1)S(1)} %get-tuple-element.10), channel_id=1, source_target_pairs={{0,256},{16,272},{32,288},{48,304},{64,320},{80,336},{96,352},{112... | collective-permute-start | bytes 208904 | tf_op jit(solution)/shard_map/ppermute | solution.py:320
  11.5 48.4 %collective-permute-start.1 = (bf16[2,48,1024]{2,1,0:T(8,128)(2,1)S(1)}, bf16[2,48,1024]{2,1,0:T(8,128)(2,1)S(1)}, u32[]{:S(2)}, u32[]{:S(2)}) collective-permute-start(bf16[2,48,1024]{2,1,0:T(8,128)(2,1)S(1)} %get-tuple-element.11), channel_id=1, source_target_pairs={{0,256},{16,272},{32,288},{48,304},{64,320},{80,336},{96,352},{112... | collective-permute-start | bytes 589832 | tf_op jit(solution)/shard_map/ppermute | solution.py:321
  35.1 1.0 %copy-start.2 = (bf16[2,2,64,1024]{3,2,1,0:T(8,128)(2,1)S(1)}, bf16[2,2,64,1024]{3,2,1,0:T(8,128)(2,1)}, u32[]{:S(2)}) copy-start(bf16[2,2,64,1024]{3,2,1,0:T(8,128)(2,1)} %images.9) | copy-start | bytes 1572868
  36.2 5.6 %collective-permute-start.4 = (bf16[80,1024]{1,0:T(8,128)(2,1)S(1)}, bf16[80,1024]{1,0:T(8,128)(2,1)S(1)}, u32[]{:S(2)}, u32[]{:S(2)}) collective-permute-start(bf16[80,1024]{1,0:T(8,128)(2,1)S(1)} %get-tuple-element.12), channel_id=1, source_target_pairs={{0,4},{4,8},{8,12},{1,5},{5,9},{9,13},{2,6},{6,10},{10,14},{3,7},{... | collective-permute-start | bytes 491528 | tf_op jit(solution)/shard_map/ppermute | solution.py:294
  39.6 6.1 %collective-permute-start.5 = (bf16[80,1024]{1,0:T(8,128)(2,1)S(1)}, bf16[80,1024]{1,0:T(8,128)(2,1)S(1)}, u32[]{:S(2)}, u32[]{:S(2)}) collective-permute-start(bf16[80,1024]{1,0:T(8,128)(2,1)S(1)} %get-tuple-element.13), channel_id=1, source_target_pairs={{4,0},{8,4},{12,8},{5,1},{9,5},{13,9},{6,2},{10,6},{14,10},{7,3},{... | collective-permute-start | bytes 491528 | tf_op jit(solution)/shard_map/ppermute | solution.py:294
  45.9 4.6 %collective-permute-start.6 = (bf16[80,128]{1,0:T(8,128)(2,1)S(1)}, bf16[80,128]{1,0:T(8,128)(2,1)S(1)}, u32[]{:S(2)}, u32[]{:S(2)}) collective-permute-start(bf16[80,128]{1,0:T(8,128)(2,1)S(1)} %get-tuple-element.14), channel_id=1, source_target_pairs={{0,1},{1,2},{2,3},{4,5},{5,6},{6,7},{8,9},{9,10},{10,11},{12,13},{... | collective-permute-start | bytes 61448 | tf_op jit(solution)/shard_map/ppermute | solution.py:294
  49.1 4.5 %collective-permute-start.7 = (bf16[80,128]{1,0:T(8,128)(2,1)S(1)}, bf16[80,128]{1,0:T(8,128)(2,1)S(1)}, u32[]{:S(2)}, u32[]{:S(2)}) collective-permute-start(bf16[80,128]{1,0:T(8,128)(2,1)S(1)} %get-tuple-element.15), channel_id=1, source_target_pairs={{1,0},{2,1},{3,2},{5,4},{6,5},{7,6},{9,8},{10,9},{11,10},{13,12},{... | collective-permute-start | bytes 61448 | tf_op jit(solution)/shard_map/ppermute | solution.py:294

commit v2 on v1

v2 whole, which is shorter than its diff:
```python
import jax
import jax.numpy as jnp
from jax import lax
from jax.experimental import pallas as pl
from jax.experimental.pallas import tpu as pltpu
from jax.sharding import PartitionSpec as P

HALO = 8
LANES = 128
ROWS = 64
COLS = 1024
BLOCKS = COLS // LANES
PADDED = ROWS + 2 * HALO
F32 = jnp.float32
BF16 = jnp.bfloat16
VMEM_LIMIT = 48 * 1024 * 1024


def lane_iota(rows):
    return lax.broadcasted_iota(jnp.int32, (rows, LANES), 1)


def move_strip(values, source, target):
    return pltpu.roll(values, (target - source) % LANES, 1)


def put_strip(total, values, source, target):
    lane = lane_iota(values.shape[0])
    inside = (lane >= target) & (lane < target + HALO)
    return jnp.where(inside, move_strip(values, source, target), total)


def block(index):
    return slice(index * LANES, (index + 1) * LANES)


def far_lane(part, field, side):
    return HALO * (part * 4 + field * 2 + side)


def my_index(pairs, pair, column):
    return pairs[4 * lax.axis_index("epoch") + pair, column]


def asked(pairs):
    groups = lax.axis_size("epoch")
    myself = lax.axis_index("epoch")
    asker = lax.rem(myself + groups // 2, groups)
    return pairs[4 * asker + 1, 1] - 2 * myself


def select_kernel(pairs, images, selected):
    selected[...] = images[asked(pairs)]


def next_rows(one, other, k, field, rows, column):
    at = block(column)
    return one[k, field, rows, at].astype(F32) + other[k, field, rows, at].astype(F32)


def pack_rows_kernel(images, one, other, up, down):
    for acquisition in range(4):
        at = pl.ds(acquisition * 16, 16)
        for column in range(BLOCKS):
            for ref, rows, part in (
                (up, slice(0, 16), slice(0, HALO)),
                (down, slice(ROWS - 16, ROWS), slice(HALO, 16)),
            ):
                fields = []
                for field in range(2):
                    if acquisition < 2:
                        values = images[acquisition, field, rows, block(column)].astype(F32)
                    else:
                        values = next_rows(one, other, acquisition - 2, field, rows, column)
                    fields.append(values[part])
                ref[at, block(column)] = jnp.concatenate(fields, axis=0).astype(BF16)


def halo_rows(above, below, acquisition, field, column):
    at = pl.ds(acquisition * 16, 16)
    rows = slice(field * HALO, (field + 1) * HALO)
    return (
        above[at, block(column)].astype(F32)[rows],
        below[at, block(column)].astype(F32)[rows],
    )


def pack_columns_kernel(images, one, other, above, below, left, right):
    everything = slice(0, ROWS)
    for side, column, ref in ((0, 0, left), (1, BLOCKS - 1, right)):
        total = jnp.zeros((PADDED, LANES), F32)
        for acquisition in range(4):
            for field in range(2):
                before, after = halo_rows(above, below, acquisition, field, column)
                if acquisition < 2:
                    main = images[acquisition, field, :, block(column)].astype(F32)
                else:
                    main = next_rows(one, other, acquisition - 2, field, everything, column)
                total = put_strip(
                    total,
                    jnp.concatenate([before, main, after], axis=0),
                    side * (LANES - HALO),
                    HALO * (2 * acquisition + field),
                )
        ref[...] = total.astype(BF16)


PARTS = ((0, 32), (32, 32), (64, 16))


def pack_far_halo_kernel(pairs, above, below, from_left, from_right, halo):
    which = asked(pairs)
    at = pl.ds(pl.multiple_of(which * 16, 16), 16)
    for column in range(BLOCKS):
        rows = above[at, block(column)].astype(F32), below[at, block(column)].astype(F32)
        for field in range(2):
            part = slice(field * HALO, (field + 1) * HALO)
            both = jnp.concatenate([rows[0][part], rows[1][part]], axis=0)
            halo[pl.ds(column * 32 + field * 16, 16), :] = both.astype(BF16)
    total = jnp.zeros((32, LANES), F32)
    for side, ref in ((0, from_left), (1, from_right)):
        values = ref[...].astype(F32)
        values = jnp.where(which == 0, values, move_strip(values, 2 * HALO, 0))
        for field in range(2):
            for part, (begin, count) in enumerate(PARTS):
                rows = values[begin : begin + count]
                if count < 32:
                    rows = jnp.concatenate([rows, jnp.zeros((32 - count, LANES), F32)], axis=0)
                total = put_strip(total, rows, HALO * field, far_lane(part, field, side))
    halo[pl.ds(BLOCKS * 32, 32), :] = total.astype(BF16)


def halo_block(from_left, from_right, acquisition, field):
    source = HALO * (2 * acquisition + field)
    blank = jnp.zeros((PADDED, LANES), F32)
    after = put_strip(blank, from_right[...].astype(F32), source, 0)
    return put_strip(after, from_left[...].astype(F32), source, LANES - HALO)


def box_sums(reference, secondary, looks, products, sums, write):
    half_rows, half_cols = looks
    for column in range(BLOCKS + 1):
        at = block(column)
        a, b = reference(0, at), reference(1, at)
        c, d = secondary(0, at), secondary(1, at)
        fields = (a * c + b * d, b * c - a * d, a * a + b * b, c * c + d * d)
        for f, value in enumerate(fields):
            high = value.astype(BF16)
            products[f, :PADDED, at] = high
            products[f, PADDED:, at] = (value - high.astype(F32)).astype(BF16)
    inner = lax.broadcasted_iota(jnp.int32, (ROWS, 2 * PADDED), 0)
    outer = lax.broadcasted_iota(jnp.int32, (ROWS, 2 * PADDED), 1)
    outer = jnp.where(outer >= PADDED, outer - PADDED, outer)
    row_band = (jnp.abs(outer - HALO - inner) <= half_rows).astype(F32).astype(BF16)
    outer = lax.broadcasted_iota(jnp.int32, (4 * LANES, 2 * LANES), 0)
    inner = lax.broadcasted_iota(jnp.int32, (4 * LANES, 2 * LANES), 1)
    col_band = (jnp.abs(outer - LANES - inner) <= half_cols).astype(F32).astype(BF16)
    for f in range(4):
        by_rows = jnp.dot(row_band, products[f], preferred_element_type=F32)
        high = by_rows.astype(BF16)
        low = (by_rows - high.astype(F32)).astype(BF16)
        for part, value in ((0, high), (1, low)):
            at = slice((2 * f + part) * ROWS, (2 * f + part + 1) * ROWS)
            sums[at, LANES : LANES + COLS] = value[:, :COLS]
            sums[at, :LANES] = value[:, COLS:]
            sums[at, LANES + COLS :] = value[:, COLS:]
    window = ((2 * half_rows + 1) * (2 * half_cols + 1)).astype(F32)
    scale = 1.0 / jnp.full((ROWS, 2 * LANES), window, F32)
    for j in range(BLOCKS // 2):
        both = jnp.dot(
            sums[:, j * 256 : j * 256 + 512], col_band, preferred_element_type=F32
        )
        real, imag, power, other = (
            both[2 * f * ROWS : (2 * f + 1) * ROWS] + both[(2 * f + 1) * ROWS : (2 * f + 2) * ROWS]
            for f in range(4)
        )
        coherence = jnp.sqrt(real * real + imag * imag) / jnp.sqrt(power * other)
        write(slice(j * 256, (j + 1) * 256), real * scale, imag * scale, coherence)


def stage(target, slot, main, halos, edges):
    for field in range(2):
        for column in range(BLOCKS):
            before, after = halos(field, column)
            target[slot, field, :, block(column)] = jnp.concatenate(
                [before, main(field, column), after], axis=0
            )
        target[slot, field, :, block(BLOCKS)] = edges(field)


def stage_mine(target, slot, acquisition, images, above, below, from_left, from_right):
    stage(
        target,
        slot,
        lambda field, column: images[acquisition, field, :, block(column)].astype(F32),
        lambda field, column: halo_rows(above, below, acquisition, field, column),
        lambda field: halo_block(from_left, from_right, acquisition, field),
    )


def writer(interferogram, coherence):
    def write(at, real, imag, value):
        interferogram[0, 0, :, at] = real
        interferogram[0, 1, :, at] = imag
        coherence[0, :, at] = value

    return write


def near_kernel(
    pairs, looks, images, one, other, above, below, from_left, from_right,
    interferogram, coherence, staged, products, sums,
):
    step = pl.program_id(0)

    @pl.when(step == 0)
    def _():
        for acquisition in range(2):
            stage_mine(
                staged, acquisition, acquisition, images, above, below, from_left, from_right
            )
        for k in range(2):
            stage(
                staged,
                2 + k,
                lambda field, column, k=k: next_rows(one, other, k, field, slice(0, ROWS), column),
                lambda field, column, k=k: halo_rows(above, below, 2 + k, field, column),
                lambda field, k=k: halo_block(from_left, from_right, 2 + k, field),
            )

    pair = jnp.where(step == 0, 0, step + 1)
    first, second = my_index(pairs, pair, 0), my_index(pairs, pair, 1)
    begin = 2 * lax.axis_index("epoch")
    inside = (second >= begin) & (second < begin + 2)
    second = (second & 1) + jnp.where(inside, 0, 2)
    box_sums(
        lambda field, at: staged[first - begin, field, :, at],
        lambda field, at: staged[second, field, :, at],
        (looks[pair, 0], looks[pair, 1]),
        products,
        sums,
        writer(interferogram, coherence),
    )


def far_kernel(
    pairs, looks, images, main, halo, above, below, from_left, from_right, _, __,
    interferogram, coherence, staged, products, sums,
):
    first = my_index(pairs, 1, 0) - 2 * lax.axis_index("epoch")
    for acquisition in range(2):

        @pl.when(first == acquisition)
        def _(acquisition=acquisition):
            stage_mine(staged, 0, acquisition, images, above, below, from_left, from_right)

    strips = halo[pl.ds(BLOCKS * 32, 32), :].astype(F32)

    def halos(field, column):
        rows = halo[pl.ds(column * 32 + field * 16, 16), :].astype(F32)
        return rows[:HALO], rows[HALO:]

    def edges(field):
        blank = jnp.zeros((32, LANES), F32)
        rows = []
        for part, (_, count) in enumerate(PARTS):
            both = put_strip(blank, strips, far_lane(part, field, 1), 0)
            both = put_strip(both, strips, far_lane(part, field, 0), LANES - HALO)
            rows.append(both[:count])
        return jnp.concatenate(rows, axis=0)

    stage(staged, 1, lambda field, column: main[field, :, block(column)].astype(F32), halos, edges)
    box_sums(
        lambda field, at: staged[0, field, :, at],
        lambda field, at: staged[1, field, :, at],
        (looks[1, 0], looks[1, 1]),
        products,
        sums,
        writer(interferogram, coherence),
    )


VMEM = pl.BlockSpec(memory_space=pltpu.VMEM)
SMEM = pl.BlockSpec(memory_space=pltpu.SMEM)
PARAMS = pltpu.CompilerParams(vmem_limit_bytes=VMEM_LIMIT)


def shape(dims, dtype=BF16):
    return jax.ShapeDtypeStruct(dims, dtype)


def scratch(acquisitions):
    return [
        pltpu.VMEM((acquisitions, 2, PADDED, COLS + LANES), F32),
        pltpu.VMEM((4, 2 * PADDED, COLS + LANES), BF16),
        pltpu.VMEM((8 * ROWS, COLS + 2 * LANES), BF16),
    ]


def exchange(first, last, axis):
    peers = lax.axis_size(axis)
    up = [(i, i + 1) for i in range(peers - 1)]
    down = [(j, i) for i, j in up]
    return lax.ppermute(last, axis, up), lax.ppermute(first, axis, down)


def local(kernel, operands, results, name, scalars=0):
    return pl.pallas_call(
        kernel,
        in_specs=[SMEM] * scalars + [VMEM] * (len(operands) - scalars),
        out_specs=[VMEM] * len(results),
        out_shape=results,
        compiler_params=PARAMS,
        name=name,
    )(*operands)


def body(slc_images, pair_list, look_sizes):
    groups = lax.axis_size("epoch")
    swap = [(b, (b + groups // 2) % groups) for b in range(groups)]

    one = lax.ppermute(slc_images, "epoch", [(b + 1, b) for b in range(groups - 1)])
    (selected,) = local(
        select_kernel, (pair_list, slc_images), [shape((2, ROWS, COLS))], "select", 1
    )
    main = lax.ppermute(selected, "epoch", swap)
    other = lax.ppermute(slc_images, "epoch", [(groups - 2, groups - 1)])

    up, down = local(
        pack_rows_kernel, (slc_images, one, other), [shape((64, COLS))] * 2, "pack_rows"
    )
    above, below = exchange(up, down, "row")
    left, right = local(
        pack_columns_kernel,
        (slc_images, one, other, above, below),
        [shape((PADDED, LANES))] * 2,
        "pack_columns",
    )
    from_left, from_right = exchange(left, right, "col")
    edges = (above, below, from_left, from_right)
    (halo,) = local(
        pack_far_halo_kernel,
        (pair_list, *edges),
        [shape((BLOCKS * 32 + 32, LANES))],
        "pack_far_halo",
        1,
    )
    halo = lax.ppermute(halo, "epoch", swap)

    outs = [shape((4, 2, ROWS, COLS), F32), shape((4, ROWS, COLS), F32)]
    interferogram, coherence = pl.pallas_call(
        near_kernel,
        grid=(3,),
        in_specs=[SMEM] * 2 + [VMEM] * 7,
        out_specs=[
            pl.BlockSpec((1, 2, ROWS, COLS), lambda i: (jnp.where(i == 0, 0, i + 1), 0, 0, 0)),
            pl.BlockSpec((1, ROWS, COLS), lambda i: (jnp.where(i == 0, 0, i + 1), 0, 0)),
        ],
        out_shape=outs,
        scratch_shapes=scratch(4),
        compiler_params=PARAMS,
        name="near_pairs",
    )(pair_list, look_sizes, slc_images, one, other, *edges)
    return pl.pallas_call(
        far_kernel,
        grid=(1,),
        in_specs=[SMEM] * 2 + [VMEM] * 7 + [pl.BlockSpec(memory_space=pl.ANY)] * 2,
        out_specs=[
            pl.BlockSpec((1, 2, ROWS, COLS), lambda i: (1, 0, 0, 0)),
            pl.BlockSpec((1, ROWS, COLS), lambda i: (1, 0, 0)),
        ],
        out_shape=outs,
        scratch_shapes=scratch(2),
        input_output_aliases={9: 0, 10: 1},
        compiler_params=PARAMS,
        name="far_pair",
    )(pair_list, look_sizes, slc_images, main, halo, *edges, interferogram, coherence)


def solution(mesh):
    placed = (P("epoch", None, "row", "col"), P(), P("epoch", None))
    return jax.shard_map(
        body,
        mesh=mesh,
        in_specs=placed,
        out_specs=(P("epoch", None, "row", "col"), P("epoch", "row", "col")),
        check_vma=False,
    )
```

time: 63.2 us -> 66.1 us (1.046)
  the two profiles are of different devices: /device:TPU:385 before, /device:TPU:40 now
where the time goes in v2:
time: 66.1 us; the launch traced here: 65.7 us
  starting transfers between devices  33.7 us (51%)
  Pallas kernels  15.1 us (23%)
  waiting for transfers between devices  13.2 us (20%)
  local copies, waits for them, and re-layouts  2.96 us (4%)
  between operations  0.77 us (1%)
    ppermute x1, starting transfers between devices, body(): main = lax.ppermute(selected, 'epoch', swap)  15.3 us
    ppermute x4, starting transfers between devices, exchange(): return (lax.ppermute(last, axis, up), lax.ppermute(first, axis, down))  10.5 us
    ppermute x4, waiting for transfers between devices, exchange(): return (lax.ppermute(last, axis, up), lax.ppermute(first, axis, down))  8.87 us
    pallas_call x1, Pallas kernels, body(): pl.pallas_call(near_kernel, grid=(3,), in_specs=[SMEM] * 2 + [VMEM] * 7,...  7.39 us
    ppermute x1, starting transfers between devices, body(): halo = lax.ppermute(halo, 'epoch', swap)  5.34 us
    ppermute x1, waiting for transfers between devices, body(): halo = lax.ppermute(halo, 'epoch', swap)  4.3 us
    pallas_call x1, Pallas kernels, body(): pl.pallas_call(far_kernel, grid=(1,), in_specs=[SMEM] * 2 + [VMEM] * 7 +...  4.02 us
    pallas_call x4, Pallas kernels, local(): pl.pallas_call(kernel, in_specs=[SMEM] * scalars + [VMEM] * (len(operands...  3.65 us
  transfers between devices with their start and end apart: 8, of which 4 were waited for; matrix products, arithmetic and copies ran while one was open for 1% of the time, Pallas kernels for 17%

profile of v2, /device:TPU:40, one launch (start us, length us, event | category | flops | bytes accessed | tf_op | source)
XLA Modules:
  0.0 65.7 jit_solution(2149152164025238203)
XLA Ops:
  0.6 0.7 %collective-permute-start.2 = (bf16[2,2,64,1024]{3,2,1,0:T(8,128)(2,1)}, bf16[2,2,64,1024]{3,2,1,0:T(8,128)(2,1)S(1)}, u32[]{:S(2)}, u32[]{:S(2)}) collective-permute-start(bf16[2,2,64,1024]{3,2,1,0:T(8,128)(2,1)} %images.9), channel_id=1, source_target_pairs={{480,496},{481,497},{482,498},{483,499},{484,500},{485,501},{486,5... | collective-permute-start | bytes 1572872 | tf_op jit(solution)/shard_map/ppermute | solution.py:327
  1.3 1.9 %collective-permute-start.1 = (bf16[2,2,64,1024]{3,2,1,0:T(8,128)(2,1)}, bf16[2,2,64,1024]{3,2,1,0:T(8,128)(2,1)S(1)}, u32[]{:S(2)}, u32[]{:S(2)}) collective-permute-start(bf16[2,2,64,1024]{3,2,1,0:T(8,128)(2,1)} %images.9), channel_id=1, source_target_pairs={{16,0},{32,16},{48,32},{64,48},{80,64},{96,80},{112,96},{128,112},... | collective-permute-start | bytes 1572872 | tf_op jit(solution)/shard_map/ppermute | solution.py:322
  3.3 0.8 %copy.11.pairs = s32[128,2]{1,0:T(8,128)S(1)} copy(s32[128,2]{0,1:T(2,128)} %param.4) | data formatting | bytes 2048 | tf_op args[1]
  4.1 1.0 %copy-done = bf16[2,2,64,1024]{3,2,1,0:T(8,128)(2,1)S(1)} copy-done((bf16[2,2,64,1024]{3,2,1,0:T(8,128)(2,1)S(1)}, bf16[2,2,64,1024]{3,2,1,0:T(8,128)(2,1)}, u32[]{:S(2)}) %copy-start) | copy-done | bytes 524312
  5.1 1.6 %select.1 = bf16[2,64,1024]{2,1,0:T(8,128)(2,1)S(1)} custom-call(s32[128,2]{1,0:T(8,128)S(1)} %copy.11.pairs, bf16[2,2,64,1024]{3,2,1,0:T(8,128)(2,1)S(1)} %copy-done), custom_call_target="tpu_custom_call" | custom-call | tf_op jit(solution)/shard_map/select/pallas_call | solution.py:308
  6.7 15.3 %collective-permute-start = (bf16[2,64,1024]{2,1,0:T(8,128)(2,1)S(1)}, bf16[2,64,1024]{2,1,0:T(8,128)(2,1)S(1)}, u32[]{:S(2)}, u32[]{:S(2)}) collective-permute-start(bf16[2,64,1024]{2,1,0:T(8,128)(2,1)S(1)} %select.1), channel_id=1, source_target_pairs={{0,256},{16,272},{32,288},{48,304},{64,320},{80,336},{96,352},{112... | collective-permute-start | bytes 786440 | tf_op jit(solution)/shard_map/ppermute | solution.py:326
  22.0 0.0 collective-permute-done.2.other
  22.0 0.0 copy-start.1
  22.0 1.0 %copy-done.1 = bf16[2,2,64,1024]{3,2,1,0:T(8,128)(2,1)S(1)} copy-done((bf16[2,2,64,1024]{3,2,1,0:T(8,128)(2,1)S(1)}, bf16[2,2,64,1024]{3,2,1,0:T(8,128)(2,1)}, u32[]{:S(2)}) %copy-start.1) | copy-done | bytes 524312
  23.1 0.1 pack_rows.1
  23.1 3.4 %collective-permute-start.3 = (bf16[64,1024]{1,0:T(8,128)(2,1)S(1)}, bf16[64,1024]{1,0:T(8,128)(2,1)S(1)}, u32[]{:S(2)}, u32[]{:S(2)}) collective-permute-start(bf16[64,1024]{1,0:T(8,128)(2,1)S(1)} %get-tuple-element.8), channel_id=1, source_target_pairs={{0,4},{4,8},{8,12},{1,5},{5,9},{9,13},{2,6},{6,10},{10,14},{3,7},{... | collective-permute-start | bytes 393224 | tf_op jit(solution)/shard_map/ppermute | solution.py:304
  26.6 1.3 %collective-permute-start.4 = (bf16[64,1024]{1,0:T(8,128)(2,1)S(1)}, bf16[64,1024]{1,0:T(8,128)(2,1)S(1)}, u32[]{:S(2)}, u32[]{:S(2)}) collective-permute-start(bf16[64,1024]{1,0:T(8,128)(2,1)S(1)} %get-tuple-element.9), channel_id=1, source_target_pairs={{4,0},{8,4},{12,8},{5,1},{9,5},{13,9},{6,2},{10,6},{14,10},{7,3},{... | collective-permute-start | bytes 393224 | tf_op jit(solution)/shard_map/ppermute | solution.py:304
  27.9 1.4 %collective-permute-done.3.above = bf16[64,1024]{1,0:T(8,128)(2,1)S(1)} collective-permute-done((bf16[64,1024]{1,0:T(8,128)(2,1)S(1)}, bf16[64,1024]{1,0:T(8,128)(2,1)S(1)}, u32[]{:S(2)}, u32[]{:S(2)}) %collective-permute-start.3) | collective-permute-done | bytes 131104 | tf_op jit(solution)/shard_map/ppermute | solution.py:304
  29.2 4.2 %collective-permute-done.4.below = bf16[64,1024]{1,0:T(8,128)(2,1)S(1)} collective-permute-done((bf16[64,1024]{1,0:T(8,128)(2,1)S(1)}, bf16[64,1024]{1,0:T(8,128)(2,1)S(1)}, u32[]{:S(2)}, u32[]{:S(2)}) %collective-permute-start.4) | collective-permute-done | bytes 131104 | tf_op jit(solution)/shard_map/ppermute | solution.py:304
  33.4 0.2 pack_columns.1
  33.6 3.5 %collective-permute-start.5 = (bf16[80,128]{1,0:T(8,128)(2,1)S(1)}, bf16[80,128]{1,0:T(8,128)(2,1)S(1)}, u32[]{:S(2)}, u32[]{:S(2)}) collective-permute-start(bf16[80,128]{1,0:T(8,128)(2,1)S(1)} %get-tuple-element.10), channel_id=1, source_target_pairs={{0,1},{1,2},{2,3},{4,5},{5,6},{6,7},{8,9},{9,10},{10,11},{12,13},{... | collective-permute-start | bytes 61448 | tf_op jit(solution)/shard_map/ppermute | solution.py:304
  37.1 2.4 %collective-permute-start.6 = (bf16[80,128]{1,0:T(8,128)(2,1)S(1)}, bf16[80,128]{1,0:T(8,128)(2,1)S(1)}, u32[]{:S(2)}, u32[]{:S(2)}) collective-permute-start(bf16[80,128]{1,0:T(8,128)(2,1)S(1)} %get-tuple-element.11), channel_id=1, source_target_pairs={{1,0},{2,1},{3,2},{5,4},{6,5},{7,6},{9,8},{10,9},{11,10},{13,12},{... | collective-permute-start | bytes 61448 | tf_op jit(solution)/shard_map/ppermute | solution.py:304
  39.5 3.3 %collective-permute-done.6.from_right = bf16[80,128]{1,0:T(8,128)(2,1)S(1)} collective-permute-done((bf16[80,128]{1,0:T(8,128)(2,1)S(1)}, bf16[80,128]{1,0:T(8,128)(2,1)S(1)}, u32[]{:S(2)}, u32[]{:S(2)}) %collective-permute-start.6) | collective-permute-done | bytes 20512 | tf_op jit(solution)/shard_map/ppermute | solution.py:304
  42.8 1.8 %pack_far_halo.1 = bf16[288,128]{1,0:T(8,128)(2,1)S(1)} custom-call(s32[128,2]{1,0:T(8,128)S(1)} %copy.11.pairs, bf16[64,1024]{1,0:T(8,128)(2,1)S(1)} %collective-permute-done.3.above, bf16[64,1024]{1,0:T(8,128)(2,1)S(1)} %collective-permute-done.4.below, bf16[80,128]{1,0:T(8,128)(2,1)S(1)} %collective-permute-done.5.from_left, ...), custom_call_target="tpu_custom_call" | custom-call | tf_op jit(solution)/shard_map/pack_far_halo/pallas_call | solution.py:308
  44.5 5.3 %collective-permute-start.7 = (bf16[288,128]{1,0:T(8,128)(2,1)S(1)}, bf16[288,128]{1,0:T(8,128)(2,1)S(1)}, u32[]{:S(2)}, u32[]{:S(2)}) collective-permute-start(bf16[288,128]{1,0:T(8,128)(2,1)S(1)} %pack_far_halo.1), channel_id=1, source_target_pairs={{0,256},{16,272},{32,288},{48,304},{64,320},{80,336},{96,352},{112... | collective-permute-start | bytes 221192 | tf_op jit(solution)/shard_map/ppermute | solution.py:348
  49.9 0.1 copy.12.looks
  50.0 7.4 %near_pairs.1 = (f32[4,2,64,1024]{3,2,1,0:T(8,128)}, f32[4,64,1024]{2,1,0:T(8,128)}) custom-call(s32[128,2]{1,0:T(8,128)S(1)} %copy.11.pairs, s32[4,2]{1,0:T(4,128)S(1)} %copy.12.looks, bf16[2,2,64,1024]{3,2,1,0:T(8,128)(2,1)S(1)} %copy-done.2, bf16[2,2,64,1024]{3,2,1,0:T(8,128)(2,1)S(1)} %collective-permute-done.1.one, ...), custom_call_target="tpu_custom_call" | custom-call | tf_op jit(solution)/shard_map/near_pairs/pallas_call | solution.py:351
  57.4 4.3 %collective-permute-done.7.halo = bf16[288,128]{1,0:T(8,128)(2,1)S(1)} collective-permute-done((bf16[288,128]{1,0:T(8,128)(2,1)S(1)}, bf16[288,128]{1,0:T(8,128)(2,1)S(1)}, u32[]{:S(2)}, u32[]{:S(2)}) %collective-permute-start.7) | collective-permute-done | bytes 73760 | tf_op jit(solution)/shard_map/ppermute | solution.py:348
  61.7 4.0 %far_pair.1 = (f32[4,2,64,1024]{3,2,1,0:T(8,128)}, f32[4,64,1024]{2,1,0:T(8,128)}) custom-call(s32[128,2]{1,0:T(8,128)S(1)} %copy.11.pairs, s32[4,2]{1,0:T(4,128)S(1)} %copy.12.looks, bf16[2,2,64,1024]{3,2,1,0:T(8,128)(2,1)S(1)} %copy-done.2, bf16[2,64,1024]{2,1,0:T(8,128)(2,1)S(1)} %collective-permute-done.main, ...), custom_call_target="tpu_custom_call", output_to_operand_aliasing={{0}: (9, {}), {1}: (10, {})} | custom-call | tf_op jit(solution)/shard_map/far_pair/pallas_call | solution.py:364
  (8 shorter events, 0.0 us)
Async XLA Ops:
  0.6 21.4 %collective-permute-start.2 = (bf16[2,2,64,1024]{3,2,1,0:T(8,128)(2,1)}, bf16[2,2,64,1024]{3,2,1,0:T(8,128)(2,1)S(1)}, u32[]{:S(2)}, u32[]{:S(2)}) collective-permute-start(bf16[2,2,64,1024]{3,2,1,0:T(8,128)(2,1)} %images.9), channel_id=1, source_target_pairs={{480,496},{481,497},{482,498},{483,499},{484,500},{485,501},{486,5... | collective-permute-start | bytes 1572872 | tf_op jit(solution)/shard_map/ppermute | solution.py:327
  1.3 20.7 %collective-permute-start.1 = (bf16[2,2,64,1024]{3,2,1,0:T(8,128)(2,1)}, bf16[2,2,64,1024]{3,2,1,0:T(8,128)(2,1)S(1)}, u32[]{:S(2)}, u32[]{:S(2)}) collective-permute-start(bf16[2,2,64,1024]{3,2,1,0:T(8,128)(2,1)} %images.9), channel_id=1, source_target_pairs={{16,0},{32,16},{48,32},{64,48},{80,64},{96,80},{112,96},{128,112},... | collective-permute-start | bytes 1572872 | tf_op jit(solution)/shard_map/ppermute | solution.py:322
  4.0 1.0 %copy-start = (bf16[2,2,64,1024]{3,2,1,0:T(8,128)(2,1)S(1)}, bf16[2,2,64,1024]{3,2,1,0:T(8,128)(2,1)}, u32[]{:S(2)}) copy-start(bf16[2,2,64,1024]{3,2,1,0:T(8,128)(2,1)} %images.9) | copy-start | bytes 1572868
  5.1 44.8 %copy-start.3 = (s32[4,2]{0,1:T(2,128)S(1)}, s32[4,2]{0,1:T(2,128)}, u32[]{:S(2)}) copy-start(s32[4,2]{0,1:T(2,128)} %param.5) | copy-start | bytes 100
  5.1 44.9 %copy-start.2 = (bf16[2,2,64,1024]{3,2,1,0:T(8,128)(2,1)S(1)}, bf16[2,2,64,1024]{3,2,1,0:T(8,128)(2,1)}, u32[]{:S(2)}) copy-start(bf16[2,2,64,1024]{3,2,1,0:T(8,128)(2,1)} %images.9) | copy-start | bytes 1572868
  6.7 50.6 %collective-permute-start = (bf16[2,64,1024]{2,1,0:T(8,128)(2,1)S(1)}, bf16[2,64,1024]{2,1,0:T(8,128)(2,1)S(1)}, u32[]{:S(2)}, u32[]{:S(2)}) collective-permute-start(bf16[2,64,1024]{2,1,0:T(8,128)(2,1)S(1)} %select.1), channel_id=1, source_target_pairs={{0,256},{16,272},{32,288},{48,304},{64,320},{80,336},{96,352},{112... | collective-permute-start | bytes 786440 | tf_op jit(solution)/shard_map/ppermute | solution.py:326
  22.0 1.0 %copy-start.1 = (bf16[2,2,64,1024]{3,2,1,0:T(8,128)(2,1)S(1)}, bf16[2,2,64,1024]{3,2,1,0:T(8,128)(2,1)}, u32[]{:S(2)}) copy-start(bf16[2,2,64,1024]{3,2,1,0:T(8,128)(2,1)} %images.9) | copy-start | bytes 1572868
  23.1 6.1 %collective-permute-start.3 = (bf16[64,1024]{1,0:T(8,128)(2,1)S(1)}, bf16[64,1024]{1,0:T(8,128)(2,1)S(1)}, u32[]{:S(2)}, u32[]{:S(2)}) collective-permute-start(bf16[64,1024]{1,0:T(8,128)(2,1)S(1)} %get-tuple-element.8), channel_id=1, source_target_pairs={{0,4},{4,8},{8,12},{1,5},{5,9},{9,13},{2,6},{6,10},{10,14},{3,7},{... | collective-permute-start | bytes 393224 | tf_op jit(solution)/shard_map/ppermute | solution.py:304
  26.6 6.9 %collective-permute-start.4 = (bf16[64,1024]{1,0:T(8,128)(2,1)S(1)}, bf16[64,1024]{1,0:T(8,128)(2,1)S(1)}, u32[]{:S(2)}, u32[]{:S(2)}) collective-permute-start(bf16[64,1024]{1,0:T(8,128)(2,1)S(1)} %get-tuple-element.9), channel_id=1, source_target_pairs={{4,0},{8,4},{12,8},{5,1},{9,5},{13,9},{6,2},{10,6},{14,10},{7,3},{... | collective-permute-start | bytes 393224 | tf_op jit(solution)/shard_map/ppermute | solution.py:304
  33.6 5.9 %collective-permute-start.5 = (bf16[80,128]{1,0:T(8,128)(2,1)S(1)}, bf16[80,128]{1,0:T(8,128)(2,1)S(1)}, u32[]{:S(2)}, u32[]{:S(2)}) collective-permute-start(bf16[80,128]{1,0:T(8,128)(2,1)S(1)} %get-tuple-element.10), channel_id=1, source_target_pairs={{0,1},{1,2},{2,3},{4,5},{5,6},{6,7},{8,9},{9,10},{10,11},{12,13},{... | collective-permute-start | bytes 61448 | tf_op jit(solution)/shard_map/ppermute | solution.py:304
  37.1 5.7 %collective-permute-start.6 = (bf16[80,128]{1,0:T(8,128)(2,1)S(1)}, bf16[80,128]{1,0:T(8,128)(2,1)S(1)}, u32[]{:S(2)}, u32[]{:S(2)}) collective-permute-start(bf16[80,128]{1,0:T(8,128)(2,1)S(1)} %get-tuple-element.11), channel_id=1, source_target_pairs={{1,0},{2,1},{3,2},{5,4},{6,5},{7,6},{9,8},{10,9},{11,10},{13,12},{... | collective-permute-start | bytes 61448 | tf_op jit(solution)/shard_map/ppermute | solution.py:304
  44.5 17.1 %collective-permute-start.7 = (bf16[288,128]{1,0:T(8,128)(2,1)S(1)}, bf16[288,128]{1,0:T(8,128)(2,1)S(1)}, u32[]{:S(2)}, u32[]{:S(2)}) collective-permute-start(bf16[288,128]{1,0:T(8,128)(2,1)S(1)} %pack_far_halo.1), channel_id=1, source_target_pairs={{0,256},{16,272},{32,288},{48,304},{64,320},{80,336},{96,352},{112... | collective-permute-start | bytes 221192 | tf_op jit(solution)/shard_map/ppermute | solution.py:348

commit v3 on v0

v3 whole, which is shorter than its diff:
```python
import jax
import jax.numpy as jnp
from jax import lax
from jax.experimental import pallas as pl
from jax.experimental.pallas import tpu as pltpu
from jax.sharding import PartitionSpec as P

HALO = 8
LANES = 128
ROWS = 64
COLS = 1024
BLOCKS = COLS // LANES
PADDED = ROWS + 2 * HALO
F32 = jnp.float32
BF16 = jnp.bfloat16
WORK = 20_000_000_000
VMEM_LIMIT = 48 * 1024 * 1024


def lane_iota(rows):
    return lax.broadcasted_iota(jnp.int32, (rows, LANES), 1)


def move_strip(values, source, target):
    return pltpu.roll(values, (target - source) % LANES, 1)


def put_strip(total, values, source, target):
    lane = lane_iota(values.shape[0])
    inside = (lane >= target) & (lane < target + HALO)
    return jnp.where(inside, move_strip(values, source, target), total)


def block(index):
    return slice(index * LANES, (index + 1) * LANES)


def far_lane(part, field, side):
    return HALO * (part * 4 + field * 2 + side)


def my_index(pairs, pair, which):
    return pairs[which, 4 * lax.axis_index("epoch") + pair]


def asked(pairs):
    groups = lax.axis_size("epoch")
    myself = lax.axis_index("epoch")
    asker = lax.rem(myself + groups // 2, groups)
    return pairs[1, 4 * asker + 1] - 2 * myself


def split_kernel(pairs, images, border, own_up, own_down, own_columns, held, done):
    copies = [
        pltpu.make_async_copy(images.at[a, f], held.at[a, f], done.at[a, f])
        for a in range(2)
        for f in range(2)
    ]
    for copy in copies:
        copy.start()
    lead = asked(pairs)
    for copy in copies:
        copy.wait()
    strips = jnp.zeros((16, LANES), F32)
    for column in range(BLOCKS):
        for field in range(2):
            values = held[lead, field, :, block(column)].astype(F32)
            rows = jnp.concatenate([values[:HALO], values[ROWS - HALO :]], axis=0)
            border[pl.ds(column * 32 + field * 16, 16), :] = rows.astype(BF16)
            for side, at in ((0, 0), (1, BLOCKS - 1)):
                if column == at:
                    for part in range(3):
                        begin = HALO + 16 * part
                        strips = put_strip(
                            strips,
                            values[begin : begin + 16],
                            side * (LANES - HALO),
                            far_lane(part, field, side),
                        )
    border[pl.ds(BLOCKS * 32, 16), :] = strips.astype(BF16)
    for a in range(2):
        at = pl.ds(a * 16, 16)
        for column in range(BLOCKS):
            tops, bottoms = [], []
            for field in range(2):
                tops.append(held[a, field, :16, block(column)].astype(F32)[:HALO])
                bottoms.append(held[a, field, ROWS - 16 :, block(column)].astype(F32)[HALO:])
            own_up[at, block(column)] = jnp.concatenate(tops, axis=0).astype(BF16)
            own_down[at, block(column)] = jnp.concatenate(bottoms, axis=0).astype(BF16)
        for field in range(2):
            own_columns[2 * a + field, :, block(0)] = held[a, field, :, block(0)]
            own_columns[2 * a + field, :, block(1)] = held[a, field, :, block(BLOCKS - 1)]


def next_rows(one, other, k, field, rows, column):
    at = block(column)
    return one[k, field, rows, at].astype(F32) + other[k, field, rows, at].astype(F32)


def fields_of(a, b, c, d):
    return a * c + b * d, b * c - a * d, a * a + b * b, c * c + d * d


def put_split(target, f, at, value):
    count = value.shape[0]
    high = value.astype(BF16)
    target[f, :count, at] = high
    target[f, count : 2 * count, at] = (value - high.astype(F32)).astype(BF16)


def row_band(half_rows, count, row_of):
    inner = lax.broadcasted_iota(jnp.int32, (ROWS, 2 * count), 0)
    outer = lax.broadcasted_iota(jnp.int32, (ROWS, 2 * count), 1)
    outer = row_of(jnp.where(outer >= count, outer - count, outer))
    return (jnp.abs(outer - inner) <= half_rows).astype(F32).astype(BF16)


def border_row(k):
    return jnp.where(k < HALO, k - HALO, k + ROWS - HALO)


def wide_border_row(k):
    return jnp.where(k < 16, k - HALO, k + ROWS - 3 * HALO)


def row_sums(band, products):
    return jnp.dot(band, products, preferred_element_type=F32)


def pair_of(step):
    return jnp.where(step == 0, 0, step + 1)


def near_slots(pairs, pair):
    begin = 2 * lax.axis_index("epoch")
    second = my_index(pairs, pair, 1)
    inside = (second >= begin) & (second < begin + 2)
    return my_index(pairs, pair, 0) - begin, (second & 1) + jnp.where(inside, 0, 2)


def main_rows_kernel(pairs, looks, images, one, other, inner, partial, held, products):
    lead = asked(pairs)
    held[:2] = images[...]
    for column in range(BLOCKS):
        at = block(column)
        for field in range(2):
            values = images[lead, field, :, at].astype(F32)
            inner[field, :, at] = values[HALO : ROWS - HALO].astype(BF16)
            for k in range(2):
                values = next_rows(one, other, k, field, slice(0, ROWS), column)
                held[2 + k, field, :, at] = values.astype(BF16)

    def one_pair(step, carry):
        pair = pair_of(step)
        first, second = near_slots(pairs, pair)
        for column in range(BLOCKS):
            at = block(column)
            a, b = (held[first, field, :, at].astype(F32) for field in range(2))
            c, d = (held[second, field, :, at].astype(F32) for field in range(2))
            for f, value in enumerate(fields_of(a, b, c, d)):
                put_split(products, f, at, value)
        band = row_band(looks[0, pair], ROWS, lambda k: k)
        for f in range(4):
            partial[4 * step + f] = row_sums(band, products[f])
        return carry

    lax.fori_loop(0, 3, one_pair, 0)
    first = my_index(pairs, 1, 0) - 2 * lax.axis_index("epoch")
    for column in range(BLOCKS):
        at = block(column)
        a, b = (held[first, field, :, at].astype(F32) for field in range(2))
        put_split(products, 0, at, a * a + b * b)
    partial[12] = row_sums(row_band(looks[0, 1], ROWS, lambda k: k), products[0])


def pack_rows_kernel(own_up, own_down, one, other, border, up, down):
    up[:32, :] = own_up[...]
    down[:32, :] = own_down[...]
    for column in range(BLOCKS):
        at = block(column)
        for k in range(2):
            tops, bottoms = [], []
            for field in range(2):
                tops.append(next_rows(one, other, k, field, slice(0, 16), column)[:HALO])
                bottoms.append(
                    next_rows(one, other, k, field, slice(ROWS - 16, ROWS), column)[HALO:]
                )
            rows = pl.ds(32 + 16 * k, 16)
            up[rows, at] = jnp.concatenate(tops, axis=0).astype(BF16)
            down[rows, at] = jnp.concatenate(bottoms, axis=0).astype(BF16)
        real = border[pl.ds(column * 32, 16), :].astype(F32)
        imag = border[pl.ds(column * 32 + 16, 16), :].astype(F32)
        up[64:, at] = jnp.concatenate([real[:HALO], imag[:HALO]], axis=0).astype(BF16)
        down[64:, at] = jnp.concatenate([real[HALO:], imag[HALO:]], axis=0).astype(BF16)


def halo_rows(above, below, acquisition, field, column):
    at = pl.ds(acquisition * 16, 16)
    rows = slice(field * HALO, (field + 1) * HALO)
    return (
        above[at, block(column)].astype(F32)[rows],
        below[at, block(column)].astype(F32)[rows],
    )


def pack_columns_kernel(own_columns, one, other, border, above, below, left, right):
    strips = border[pl.ds(BLOCKS * 32, 16), :].astype(F32)
    for side, column, ref in ((0, 0, left), (1, BLOCKS - 1, right)):
        total = jnp.zeros((PADDED, LANES), F32)
        source = side * (LANES - HALO)
        for acquisition in range(5):
            for field in range(2):
                before, after = halo_rows(above, below, acquisition, field, column)
                if acquisition < 2:
                    main = own_columns[2 * acquisition + field, :, block(side)].astype(F32)
                elif acquisition < 4:
                    main = next_rows(one, other, acquisition - 2, field, slice(0, ROWS), column)
                else:
                    rows = border[pl.ds(column * 32 + field * 16, 16), :].astype(F32)
                    inner = [
                        move_strip(strips, far_lane(part, field, side), source)
                        for part in range(3)
                    ]
                    main = jnp.concatenate([rows[:HALO], *inner, rows[HALO:]], axis=0)
                values = jnp.concatenate([before, main, after], axis=0)
                total = put_strip(total, values, source, HALO * (2 * acquisition + field))
        ref[...] = total.astype(BF16)


def halo_block(from_left, from_right, acquisition, field):
    source = HALO * (2 * acquisition + field)
    blank = jnp.zeros((PADDED, LANES), F32)
    after = put_strip(blank, from_right[...].astype(F32), source, 0)
    return put_strip(after, from_left[...].astype(F32), source, LANES - HALO)


def column_sums(by_rows, half_cols, sums, count, write):
    for f in range(count):
        value, edge = by_rows(f)
        for part in range(2):
            rows = slice((2 * f + part) * ROWS, (2 * f + part + 1) * ROWS)
            high, high_edge = value.astype(BF16), edge.astype(BF16)
            sums[rows, LANES : LANES + COLS] = high
            sums[rows, :LANES] = high_edge
            sums[rows, LANES + COLS :] = high_edge
            value, edge = value - high.astype(F32), edge - high_edge.astype(F32)
    outer = lax.broadcasted_iota(jnp.int32, (4 * LANES, 2 * LANES), 0)
    inner = lax.broadcasted_iota(jnp.int32, (4 * LANES, 2 * LANES), 1)
    band = (jnp.abs(outer - LANES - inner) <= half_cols).astype(F32).astype(BF16)
    for j in range(BLOCKS // 2):
        both = jnp.dot(
            sums[: 2 * count * ROWS, j * 256 : j * 256 + 512], band, preferred_element_type=F32
        )
        write(
            j,
            [
                both[2 * f * ROWS : (2 * f + 1) * ROWS]
                + both[(2 * f + 1) * ROWS : (2 * f + 2) * ROWS]
                for f in range(count)
            ],
        )


def result_copies(pair, slot, j, held, interferogram, coherence, done):
    at = pl.ds(j * 256, 256)
    return (
        pltpu.make_async_copy(
            held.at[slot, pl.ds(0, 2), :, at],
            interferogram.at[pair, :, :, at],
            done.at[slot, j, 0],
        ),
        pltpu.make_async_copy(
            held.at[slot, 2, :, at], coherence.at[pair, :, at], done.at[slot, j, 1]
        ),
    )


def finish(real, imag, power, other, looks, pair, slot, j, results):
    held = results[0]
    window = ((2 * looks[0] + 1) * (2 * looks[1] + 1)).astype(F32)
    scale = 1.0 / jnp.full((8, 2 * LANES), window, F32)
    scale = jnp.concatenate([scale] * (ROWS // 8), axis=0)
    at = slice(j * 256, (j + 1) * 256)
    held[slot, 0, :, at] = real * scale
    held[slot, 1, :, at] = imag * scale
    held[slot, 2, :, at] = jnp.sqrt(real * real + imag * imag) / jnp.sqrt(power * other)
    for copy in result_copies(pair, slot, j, *results):
        copy.start()


def wait_for_results(pair, slot, results):
    for j in range(BLOCKS // 2):
        for copy in result_copies(pair, slot, j, *results):
            copy.wait()


def two_rows(upper, lower, acquisition, at):
    rows = pl.ds(pl.multiple_of(acquisition * 16, 16), 16)
    first, last = upper[rows, at].astype(F32), lower[rows, at].astype(F32)
    return (
        jnp.concatenate([first[:HALO], last[:HALO]], axis=0),
        jnp.concatenate([first[HALO:], last[HALO:]], axis=0),
    )


def near_kernel(
    pairs, looks, partial, own_up, own_down, border, above, below, from_left, from_right,
    interferogram, coherence, far_power, far_partial,
    halos, halo_products, edge_products, sums, held, done,
):
    for acquisition in range(5):
        for field in range(2):
            halos[acquisition, field] = halo_block(from_left, from_right, acquisition, field)
    results = held, interferogram, coherence, done
    everything = slice(0, LANES)

    def edge(slots, half_rows, fields):
        values = [halos[slot, field] for slot in slots for field in range(2)]
        band = row_band(half_rows, PADDED, lambda k: k - HALO)
        out = []
        for f, value in enumerate(fields(*values)):
            put_split(edge_products, f, everything, value)
            out.append(row_sums(band, edge_products[f]))
        return out

    def one_pair(step, carry):
        pair = pair_of(step)
        slots = near_slots(pairs, pair)
        half_rows, half_cols = looks[0, pair], looks[1, pair]
        for column in range(BLOCKS):
            at = block(column)
            values = [v for slot in slots for v in two_rows(above, below, slot, at)]
            for f, value in enumerate(fields_of(*values)):
                put_split(halo_products, f, at, value)
        band = row_band(half_rows, 16, border_row)
        edges = edge(slots, half_rows, fields_of)
        column_sums(
            lambda f: (
                partial[4 * step + f] + row_sums(band, halo_products[f, :32, :]),
                edges[f],
            ),
            half_cols,
            sums,
            4,
            lambda j, blocks: finish(
                *blocks, (half_rows, half_cols), pair, step, j, results
            ),
        )
        return carry

    lax.fori_loop(0, 3, one_pair, 0)

    first = my_index(pairs, 1, 0) - 2 * lax.axis_index("epoch")
    half_rows = looks[0, 1]

    def power(a, b):
        return (a * a + b * b,)

    for column in range(BLOCKS):
        at = block(column)
        put_split(halo_products, 0, at, power(*two_rows(above, below, first, at))[0])
    band = row_band(half_rows, 16, border_row)
    (edges,) = edge((first,), half_rows, power)

    def keep(j, blocks):
        far_power[:, j * 256 : (j + 1) * 256] = blocks[0]

    column_sums(
        lambda f: (partial[12] + row_sums(band, halo_products[0, :32, :]), edges),
        looks[1, 1],
        sums,
        1,
        keep,
    )

    def three(a, b, c, d):
        return a * c + b * d, b * c - a * d, c * c + d * d

    for column in range(BLOCKS):
        at = block(column)
        outside = two_rows(above, below, first, at)
        inside = two_rows(own_up, own_down, first, at)
        values = [
            jnp.concatenate([o[:HALO], i, o[HALO:]], axis=0)
            for o, i in zip(outside, inside, strict=True)
        ]
        outside = two_rows(above, below, 4, at)
        for field in range(2):
            inside = border[pl.ds(column * 32 + field * 16, 16), :].astype(F32)
            values.append(
                jnp.concatenate([outside[field][:HALO], inside, outside[field][HALO:]], axis=0)
            )
        for f, value in enumerate(three(*values)):
            put_split(halo_products, f, at, value)
    band = row_band(half_rows, 32, wide_border_row)
    edges = edge((first, 4), half_rows, three)
    for f in range(3):
        far_partial[f, :, :COLS] = row_sums(band, halo_products[f])
        far_partial[f, :, COLS:] = edges[f]
    for step, pair in enumerate((0, 2, 3)):
        wait_for_results(pair, step, results)


def far_kernel(
    pairs, looks, images, inner, far_power, far_partial, _, __,
    interferogram, coherence, products, sums, held, done,
):
    first = my_index(pairs, 1, 0) - 2 * lax.axis_index("epoch")
    sizes = looks[0, 1], looks[1, 1]
    results = held, interferogram, coherence, done
    for column in range(BLOCKS):
        at = block(column)
        a, b = (
            images[first, field, :, at].astype(F32)[HALO : ROWS - HALO] for field in range(2)
        )
        c, d = (inner[field, :, at].astype(F32) for field in range(2))
        for f, value in enumerate((a * c + b * d, b * c - a * d, c * c + d * d)):
            put_split(products, f, at, value)
    band = row_band(sizes[0], ROWS - 2 * HALO, lambda k: k + HALO)

    def write(j, blocks):
        real, imag, other = blocks
        power = far_power[:, j * 256 : (j + 1) * 256]
        finish(real, imag, power, other, sizes, 1, 0, j, results)

    column_sums(
        lambda f: (
            far_partial[f, :, :COLS] + row_sums(band, products[f]),
            far_partial[f, :, COLS:],
        ),
        sizes[1],
        sums,
        3,
        write,
    )
    wait_for_results(1, 0, results)


VMEM = pl.BlockSpec(memory_space=pltpu.VMEM)
SMEM = pl.BlockSpec(memory_space=pltpu.SMEM)
ANY = pl.BlockSpec(memory_space=pl.ANY)
PARAMS = pltpu.CompilerParams(vmem_limit_bytes=VMEM_LIMIT)


def shape(dims, dtype=BF16):
    return jax.ShapeDtypeStruct(dims, dtype)


def exchange(first, last, axis):
    peers = lax.axis_size(axis)
    up = [(i, i + 1) for i in range(peers - 1)]
    down = [(j, i) for i, j in up]
    return lax.ppermute(last, axis, up), lax.ppermute(first, axis, down)


def local(kernel, operands, places, results, name, kept=None, held=(), aliases=None, flops=0):
    return pl.pallas_call(
        kernel,
        in_specs=places,
        out_specs=kept or [VMEM] * len(results),
        out_shape=results,
        scratch_shapes=list(held),
        input_output_aliases=aliases or {},
        compiler_params=PARAMS,
        cost_estimate=pl.CostEstimate(flops=flops, bytes_accessed=0, transcendentals=0),
        name=name,
    )(*operands)


def body(slc_images, pair_list, look_sizes):
    groups = lax.axis_size("epoch")
    swap = [(b, (b + groups // 2) % groups) for b in range(groups)]
    pairs, looks = pair_list.T, look_sizes.T

    one = lax.ppermute(slc_images, "epoch", [(b + 1, b) for b in range(groups - 1)])
    border, own_up, own_down, own_columns, images = local(
        split_kernel,
        (pairs, slc_images),
        [SMEM, ANY],
        [
            shape((BLOCKS * 32 + 16, LANES)),
            shape((32, COLS)),
            shape((32, COLS)),
            shape((4, ROWS, 2 * LANES)),
            shape((2, 2, ROWS, COLS)),
        ],
        "split",
        held=[pltpu.SemaphoreType.DMA((2, 2))],
    )
    border = lax.ppermute(border, "epoch", swap)
    other = lax.ppermute(images, "epoch", [(groups - 2, groups - 1)])
    inner, partial = local(
        main_rows_kernel,
        (pairs, looks, images, one, other),
        [SMEM] * 2 + [VMEM] * 3,
        [shape((2, ROWS - 2 * HALO, COLS)), shape((13, ROWS, COLS), F32)],
        "main_rows",
        held=[
            pltpu.VMEM((4, 2, ROWS, COLS), BF16),
            pltpu.VMEM((4, 2 * ROWS, COLS), BF16),
        ],
        flops=WORK,
    )
    inner = lax.ppermute(inner, "epoch", swap)

    up, down = local(
        pack_rows_kernel,
        (own_up, own_down, one, other, border),
        [VMEM] * 5,
        [shape((80, COLS))] * 2,
        "pack_rows",
    )
    above, below = exchange(up, down, "row")
    left, right = local(
        pack_columns_kernel,
        (own_columns, one, other, border, above, below),
        [VMEM] * 6,
        [shape((PADDED, LANES))] * 2,
        "pack_columns",
    )
    edges = (above, below, *exchange(left, right, "col"))

    outs = [shape((4, 2, ROWS, COLS), F32), shape((4, ROWS, COLS), F32)]
    interferogram, coherence, power, rest = local(
        near_kernel,
        (pairs, looks, partial, own_up, own_down, border, *edges),
        [SMEM] * 2 + [VMEM] * 8,
        [*outs, shape((ROWS, COLS), F32), shape((3, ROWS, COLS + LANES), F32)],
        "near_pairs",
        kept=[ANY, ANY, VMEM, VMEM],
        held=[
            pltpu.VMEM((5, 2, PADDED, LANES), F32),
            pltpu.VMEM((4, 64, COLS), BF16),
            pltpu.VMEM((4, 2 * PADDED, LANES), BF16),
            pltpu.VMEM((8 * ROWS, COLS + 2 * LANES), BF16),
            pltpu.VMEM((3, 3, ROWS, COLS), F32),
            pltpu.SemaphoreType.DMA((3, BLOCKS // 2, 2)),
        ],
    )
    return local(
        far_kernel,
        (pairs, looks, images, inner, power, rest, interferogram, coherence),
        [SMEM] * 2 + [VMEM] * 4 + [ANY] * 2,
        outs,
        "far_pair",
        kept=[ANY, ANY],
        held=[
            pltpu.VMEM((3, 2 * (ROWS - 2 * HALO), COLS), BF16),
            pltpu.VMEM((6 * ROWS, COLS + 2 * LANES), BF16),
            pltpu.VMEM((1, 3, ROWS, COLS), F32),
            pltpu.SemaphoreType.DMA((1, BLOCKS // 2, 2)),
        ],
        aliases={6: 0, 7: 1},
    )


def solution(mesh):
    placed = (P("epoch", None, "row", "col"), P(), P("epoch", None))
    return jax.shard_map(
        body,
        mesh=mesh,
        in_specs=placed,
        out_specs=(P("epoch", None, "row", "col"), P("epoch", "row", "col")),
        check_vma=False,
    )
```

time: 198 us -> 58.9 us (0.30)
  waiting for transfers between devices: 128 us -> 9.43 us
  starting transfers between devices: 8.9 us -> 33.6 us
  local copies, waits for them, and re-layouts: 19.9 us -> 2.39 us
  matrix products: 17.4 us -> 0 us
  between operations: 14.2 us -> 0.79 us
  Pallas kernels: 0 us -> 12.3 us
  other arithmetic: 7.63 us -> 0 us
    all_gather x1 -> x0, waiting for transfers between devices: 113 us -> none  [body(): piece = lax.all_gather(slc_images, 'epoch', axis=0, tiled=True)]
    ppermute x4 -> x8, starting transfers between devices: 8.86 us -> 33.6 us  [the longest x1 10.1 us: body(): border = lax.ppermute(border, 'epoch', swap)]
    dot_general x2 -> x0, matrix products: 17.4 us -> none  [the longest x1 11.6 us: body(): jnp.einsum('pfil,plj->pfij', by_rows, col_band, precision=lax.Precision.H...]
    pallas_call x0 -> x6, Pallas kernels: none -> 12.3 us  [local(): pl.pallas_call(kernel, in_specs=places, out_specs=kept or [VMEM] * len(re...]
    concatenate x1 -> x0, local copies, waits for them, and re-layouts: 8.17 us -> none  [with_halo(): x = jnp.concatenate([before, x, after], axis=dim)]
    gather x1 -> x0, local copies, waits for them, and re-layouts: 6.45 us -> none  [body(): gathered = jnp.where(inside[:, None, None, None], piece[offset], empty)]
    ppermute x4 -> x8, waiting for transfers between devices: 14.3 us -> 9.43 us  [the longest x4 9.42 us: exchange(): return (lax.ppermute(last, axis, up), lax.ppermute(first, axis, down))]
    div x2 -> x0, other arithmetic: 3.19 us -> none  [the longest x1 1.73 us: body(): interferogram = box_sums[:, 0:2] / window]
  transfers between devices with their start and end apart: 5 -> 8, of which waited for: 4 -> 3; matrix products, arithmetic and copies ran while one was open for 3% -> 0% of each run, Pallas kernels for 0% -> 17%
where the time goes in v3:
time: 58.9 us; the launch traced here: 58.5 us
  starting transfers between devices  33.6 us (57%)
  Pallas kernels  12.3 us (21%)
  waiting for transfers between devices  9.43 us (16%)
  local copies, waits for them, and re-layouts  2.39 us (4%)
  between operations  0.79 us (1%)
    pallas_call x6, Pallas kernels, local(): pl.pallas_call(kernel, in_specs=places, out_specs=kept or [VMEM] * len(re...  12.3 us
    ppermute x1, starting transfers between devices, body(): border = lax.ppermute(border, 'epoch', swap)  10.1 us
    ppermute x4, waiting for transfers between devices, exchange(): return (lax.ppermute(last, axis, up), lax.ppermute(first, axis, down))  9.42 us
    ppermute x4, starting transfers between devices, exchange(): return (lax.ppermute(last, axis, up), lax.ppermute(first, axis, down))  8.91 us
    ppermute x1, starting transfers between devices, body(): lax.ppermute(slc_images, 'epoch', [(b + 1, b) for b in range(groups - 1)])  8.79 us
    ppermute x1, starting transfers between devices, body(): inner = lax.ppermute(inner, 'epoch', swap)  5.18 us
    unnamed x8, local copies, waits for them, and re-layouts  2.39 us
  transfers between devices with their start and end apart: 8, of which 3 were waited for; matrix products, arithmetic and copies ran while one was open for 0% of the time, Pallas kernels for 17%

profile of v3, /device:TPU:1, one launch (start us, length us, event | category | flops | bytes accessed | tf_op | source)
XLA Modules:
  0.0 58.5 jit_solution(630521985158974921)
XLA Ops:
  0.6 8.8 %collective-permute-start = (bf16[2,2,64,1024]{3,2,1,0:T(8,128)(2,1)}, bf16[2,2,64,1024]{3,2,1,0:T(8,128)(2,1)S(1)}, u32[]{:S(2)}, u32[]{:S(2)}) collective-permute-start(bf16[2,2,64,1024]{3,2,1,0:T(8,128)(2,1)} %images.1), channel_id=1, source_target_pairs={{16,0},{32,16},{48,32},{64,48},{80,64},{96,80},{112,96},{128,112},... | collective-permute-start | bytes 1572872 | tf_op jit(solution)/shard_map/ppermute | solution.py:475
  9.4 1.0 %copy-done = bf16[2,2,64,1024]{3,2,1,0:T(8,128)(2,1)S(1)} copy-done((bf16[2,2,64,1024]{3,2,1,0:T(8,128)(2,1)S(1)}, bf16[2,2,64,1024]{3,2,1,0:T(8,128)(2,1)}, u32[]{:S(2)}) %copy-start) | copy-done | bytes 524312
  10.5 0.7 %copy-done.1 = s32[128,2]{0,1:T(2,128)S(1)} copy-done((s32[128,2]{0,1:T(2,128)S(1)}, s32[128,2]{0,1:T(2,128)}, u32[]{:S(2)}) %copy-start.1) | copy-done | bytes 1048
  11.1 1.4 %split.1 = (bf16[272,128]{1,0:T(8,128)(2,1)S(1)}, bf16[32,1024]{1,0:T(8,128)(2,1)S(1)}, bf16[32,1024]{1,0:T(8,128)(2,1)S(1)}, bf16[4,64,256]{2,1,0:T(8,128)(2,1)S(1)}, bf16[2,2,64,1024]{3,2,1,0:T(8,128)(2,1)S(1)}) custom-call(s32[2,128]{1,0:T(2,128)S(1)} %bitcast.2, bf16[2,2,64,1024]{3,2,1,0:T(8,128)(2,1)S(1)} %copy-done), custom_call_target="tpu_custom_call" | custom-call | tf_op jit(solution)/shard_map/split/pallas_call | solution.py:457
  12.6 0.7 %collective-permute-start.1 = (bf16[2,2,64,1024]{3,2,1,0:T(8,128)(2,1)S(1)}, bf16[2,2,64,1024]{3,2,1,0:T(8,128)(2,1)S(1)}, u32[]{:S(2)}, u32[]{:S(2)}) collective-permute-start(bf16[2,2,64,1024]{3,2,1,0:T(8,128)(2,1)S(1)} %get-tuple-element.17.images), channel_id=1, source_target_pairs={{480,496},{481,497},{482,498},{483,499},{484,500},{485,501},{486,5... | collective-permute-start | bytes 1572872 | tf_op jit(solution)/shard_map/ppermute | solution.py:491
  13.3 10.1 %collective-permute-start.3 = (bf16[272,128]{1,0:T(8,128)(2,1)S(1)}, bf16[272,128]{1,0:T(8,128)(2,1)S(1)}, u32[]{:S(2)}, u32[]{:S(2)}) collective-permute-start(bf16[272,128]{1,0:T(8,128)(2,1)S(1)} %get-tuple-element.22), channel_id=1, source_target_pairs={{0,256},{16,272},{32,288},{48,304},{64,320},{80,336},{96,352},{112... | collective-permute-start | bytes 208904 | tf_op jit(solution)/shard_map/ppermute | solution.py:490
  23.3 0.0 collective-permute-done.one
  23.4 0.0 copy-start.2
  23.4 0.7 %copy-done.2 = s32[4,2]{0,1:T(2,128)S(1)} copy-done((s32[4,2]{0,1:T(2,128)S(1)}, s32[4,2]{0,1:T(2,128)}, u32[]{:S(2)}) %copy-start.2) | copy-done | bytes 56
  24.1 3.1 %main_rows.1 = (bf16[2,48,1024]{2,1,0:T(8,128)(2,1)S(1)}, f32[13,64,1024]{2,1,0:T(8,128)S(1)}) custom-call(s32[2,128]{1,0:T(2,128)S(1)} %bitcast.3, s32[2,4]{1,0:T(2,128)S(1)} %bitcast.6, bf16[2,2,64,1024]{3,2,1,0:T(8,128)(2,1)S(1)} %get-tuple-element.17.images, bf16[2,2,64,1024]{3,2,1,0:T(8,128)(2,1)S(1)} %collective-permute-done.one, ...), custom_call_target="tpu_custom_call" | custom-call | flops 20000000000 | tf_op jit(solution)/shard_map/main_rows/pallas_call | solution.py:457
  27.2 0.0 copy-start.3
  27.2 5.2 %collective-permute-start.2 = (bf16[2,48,1024]{2,1,0:T(8,128)(2,1)S(1)}, bf16[2,48,1024]{2,1,0:T(8,128)(2,1)S(1)}, u32[]{:S(2)}, u32[]{:S(2)}) collective-permute-start(bf16[2,48,1024]{2,1,0:T(8,128)(2,1)S(1)} %get-tuple-element.18), channel_id=1, source_target_pairs={{0,256},{16,272},{32,288},{48,304},{64,320},{80,336},{96,352},{112... | collective-permute-start | bytes 589832 | tf_op jit(solution)/shard_map/ppermute | solution.py:504
  32.4 0.0 collective-permute-done.3.border
  32.4 0.1 pack_rows.1
  32.4 3.1 %collective-permute-start.4 = (bf16[80,1024]{1,0:T(8,128)(2,1)S(1)}, bf16[80,1024]{1,0:T(8,128)(2,1)S(1)}, u32[]{:S(2)}, u32[]{:S(2)}) collective-permute-start(bf16[80,1024]{1,0:T(8,128)(2,1)S(1)} %get-tuple-element.23), channel_id=1, source_target_pairs={{0,4},{4,8},{8,12},{1,5},{5,9},{9,13},{2,6},{6,10},{10,14},{3,7},{... | collective-permute-start | bytes 491528 | tf_op jit(solution)/shard_map/ppermute | solution.py:453
  35.6 1.3 %collective-permute-start.5 = (bf16[80,1024]{1,0:T(8,128)(2,1)S(1)}, bf16[80,1024]{1,0:T(8,128)(2,1)S(1)}, u32[]{:S(2)}, u32[]{:S(2)}) collective-permute-start(bf16[80,1024]{1,0:T(8,128)(2,1)S(1)} %get-tuple-element.24), channel_id=1, source_target_pairs={{4,0},{8,4},{12,8},{5,1},{9,5},{13,9},{6,2},{10,6},{14,10},{7,3},{... | collective-permute-start | bytes 491528 | tf_op jit(solution)/shard_map/ppermute | solution.py:453
  36.9 1.4 %collective-permute-done.4.above = bf16[80,1024]{1,0:T(8,128)(2,1)S(1)} collective-permute-done((bf16[80,1024]{1,0:T(8,128)(2,1)S(1)}, bf16[80,1024]{1,0:T(8,128)(2,1)S(1)}, u32[]{:S(2)}, u32[]{:S(2)}) %collective-permute-start.4) | collective-permute-done | bytes 163872 | tf_op jit(solution)/shard_map/ppermute | solution.py:453
  38.3 4.4 %collective-permute-done.5.below = bf16[80,1024]{1,0:T(8,128)(2,1)S(1)} collective-permute-done((bf16[80,1024]{1,0:T(8,128)(2,1)S(1)}, bf16[80,1024]{1,0:T(8,128)(2,1)S(1)}, u32[]{:S(2)}, u32[]{:S(2)}) %collective-permute-start.5) | collective-permute-done | bytes 163872 | tf_op jit(solution)/shard_map/ppermute | solution.py:453
  42.7 0.2 pack_columns.1
  42.9 3.2 %collective-permute-start.6 = (bf16[80,128]{1,0:T(8,128)(2,1)S(1)}, bf16[80,128]{1,0:T(8,128)(2,1)S(1)}, u32[]{:S(2)}, u32[]{:S(2)}) collective-permute-start(bf16[80,128]{1,0:T(8,128)(2,1)S(1)} %get-tuple-element.26), channel_id=1, source_target_pairs={{0,1},{1,2},{2,3},{4,5},{5,6},{6,7},{8,9},{9,10},{10,11},{12,13},{... | collective-permute-start | bytes 61448 | tf_op jit(solution)/shard_map/ppermute | solution.py:453
  46.1 1.3 %collective-permute-start.7 = (bf16[80,128]{1,0:T(8,128)(2,1)S(1)}, bf16[80,128]{1,0:T(8,128)(2,1)S(1)}, u32[]{:S(2)}, u32[]{:S(2)}) collective-permute-start(bf16[80,128]{1,0:T(8,128)(2,1)S(1)} %get-tuple-element.27), channel_id=1, source_target_pairs={{1,0},{2,1},{3,2},{5,4},{6,5},{7,6},{9,8},{10,9},{11,10},{13,12},{... | collective-permute-start | bytes 61448 | tf_op jit(solution)/shard_map/ppermute | solution.py:453
  47.4 3.6 %collective-permute-done.7.from_right = bf16[80,128]{1,0:T(8,128)(2,1)S(1)} collective-permute-done((bf16[80,128]{1,0:T(8,128)(2,1)S(1)}, bf16[80,128]{1,0:T(8,128)(2,1)S(1)}, u32[]{:S(2)}, u32[]{:S(2)}) %collective-permute-start.7) | collective-permute-done | bytes 20512 | tf_op jit(solution)/shard_map/ppermute | solution.py:453
  51.0 5.0 %near_pairs.1 = (f32[4,2,64,1024]{3,2,1,0:T(8,128)}, f32[4,64,1024]{2,1,0:T(8,128)}, f32[64,1024]{1,0:T(8,128)S(1)}, f32[3,64,1152]{2,1,0:T(8,128)S(1)}) custom-call(s32[2,128]{1,0:T(2,128)S(1)} %bitcast.4, s32[2,4]{1,0:T(2,128)S(1)} %bitcast.7, f32[13,64,1024]{2,1,0:T(8,128)S(1)} %get-tuple-element.19.partial, ...), custom_call_target="tpu_custom_call" | custom-call | tf_op jit(solution)/shard_map/near_pairs/pallas_call | solution.py:457
  56.0 2.5 %far_pair.1 = (f32[4,2,64,1024]{3,2,1,0:T(8,128)}, f32[4,64,1024]{2,1,0:T(8,128)}) custom-call(s32[2,128]{1,0:T(2,128)S(1)} %bitcast.5, s32[2,4]{1,0:T(2,128)S(1)} %bitcast.8, bf16[2,2,64,1024]{3,2,1,0:T(8,128)(2,1)S(1)} %get-tuple-element.17.images, ...), custom_call_target="tpu_custom_call", output_to_operand_aliasing={{0}: (6, {}), {1}: (7, {})} | custom-call | tf_op jit(solution)/shard_map/far_pair/pallas_call | solution.py:457
  (6 shorter events, 0.0 us)
Async XLA Ops:
  0.6 22.7 %collective-permute-start = (bf16[2,2,64,1024]{3,2,1,0:T(8,128)(2,1)}, bf16[2,2,64,1024]{3,2,1,0:T(8,128)(2,1)S(1)}, u32[]{:S(2)}, u32[]{:S(2)}) collective-permute-start(bf16[2,2,64,1024]{3,2,1,0:T(8,128)(2,1)} %images.1), channel_id=1, source_target_pairs={{16,0},{32,16},{48,32},{64,48},{80,64},{96,80},{112,96},{128,112},... | collective-permute-start | bytes 1572872 | tf_op jit(solution)/shard_map/ppermute | solution.py:475
  9.4 1.0 %copy-start = (bf16[2,2,64,1024]{3,2,1,0:T(8,128)(2,1)S(1)}, bf16[2,2,64,1024]{3,2,1,0:T(8,128)(2,1)}, u32[]{:S(2)}) copy-start(bf16[2,2,64,1024]{3,2,1,0:T(8,128)(2,1)} %images.1) | copy-start | bytes 1572868
  10.5 0.7 %copy-start.1 = (s32[128,2]{0,1:T(2,128)S(1)}, s32[128,2]{0,1:T(2,128)}, u32[]{:S(2)}) copy-start(s32[128,2]{0,1:T(2,128)} %param.4) | copy-start | bytes 3076
  12.6 10.8 %collective-permute-start.1 = (bf16[2,2,64,1024]{3,2,1,0:T(8,128)(2,1)S(1)}, bf16[2,2,64,1024]{3,2,1,0:T(8,128)(2,1)S(1)}, u32[]{:S(2)}, u32[]{:S(2)}) collective-permute-start(bf16[2,2,64,1024]{3,2,1,0:T(8,128)(2,1)S(1)} %get-tuple-element.17.images), channel_id=1, source_target_pairs={{480,496},{481,497},{482,498},{483,499},{484,500},{485,501},{486,5... | collective-permute-start | bytes 1572872 | tf_op jit(solution)/shard_map/ppermute | solution.py:491
  13.3 19.1 %collective-permute-start.3 = (bf16[272,128]{1,0:T(8,128)(2,1)S(1)}, bf16[272,128]{1,0:T(8,128)(2,1)S(1)}, u32[]{:S(2)}, u32[]{:S(2)}) collective-permute-start(bf16[272,128]{1,0:T(8,128)(2,1)S(1)} %get-tuple-element.22), channel_id=1, source_target_pairs={{0,256},{16,272},{32,288},{48,304},{64,320},{80,336},{96,352},{112... | collective-permute-start | bytes 208904 | tf_op jit(solution)/shard_map/ppermute | solution.py:490
  23.4 0.7 %copy-start.2 = (s32[4,2]{0,1:T(2,128)S(1)}, s32[4,2]{0,1:T(2,128)}, u32[]{:S(2)}) copy-start(s32[4,2]{0,1:T(2,128)} %param.5) | copy-start | bytes 100
  27.2 23.9 %copy-start.3 = (s32[4,2]{0,1:T(2,128)S(1)}, s32[4,2]{0,1:T(2,128)}, u32[]{:S(2)}) copy-start(s32[4,2]{0,1:T(2,128)} %param.5) | copy-start | bytes 100
  27.2 28.8 %collective-permute-start.2 = (bf16[2,48,1024]{2,1,0:T(8,128)(2,1)S(1)}, bf16[2,48,1024]{2,1,0:T(8,128)(2,1)S(1)}, u32[]{:S(2)}, u32[]{:S(2)}) collective-permute-start(bf16[2,48,1024]{2,1,0:T(8,128)(2,1)S(1)} %get-tuple-element.18), channel_id=1, source_target_pairs={{0,256},{16,272},{32,288},{48,304},{64,320},{80,336},{96,352},{112... | collective-permute-start | bytes 589832 | tf_op jit(solution)/shard_map/ppermute | solution.py:504
  32.4 5.8 %collective-permute-start.4 = (bf16[80,1024]{1,0:T(8,128)(2,1)S(1)}, bf16[80,1024]{1,0:T(8,128)(2,1)S(1)}, u32[]{:S(2)}, u32[]{:S(2)}) collective-permute-start(bf16[80,1024]{1,0:T(8,128)(2,1)S(1)} %get-tuple-element.23), channel_id=1, source_target_pairs={{0,4},{4,8},{8,12},{1,5},{5,9},{9,13},{2,6},{6,10},{10,14},{3,7},{... | collective-permute-start | bytes 491528 | tf_op jit(solution)/shard_map/ppermute | solution.py:453
  35.6 7.1 %collective-permute-start.5 = (bf16[80,1024]{1,0:T(8,128)(2,1)S(1)}, bf16[80,1024]{1,0:T(8,128)(2,1)S(1)}, u32[]{:S(2)}, u32[]{:S(2)}) collective-permute-start(bf16[80,1024]{1,0:T(8,128)(2,1)S(1)} %get-tuple-element.24), channel_id=1, source_target_pairs={{4,0},{8,4},{12,8},{5,1},{9,5},{13,9},{6,2},{10,6},{14,10},{7,3},{... | collective-permute-start | bytes 491528 | tf_op jit(solution)/shard_map/ppermute | solution.py:453
  42.9 4.5 %collective-permute-start.6 = (bf16[80,128]{1,0:T(8,128)(2,1)S(1)}, bf16[80,128]{1,0:T(8,128)(2,1)S(1)}, u32[]{:S(2)}, u32[]{:S(2)}) collective-permute-start(bf16[80,128]{1,0:T(8,128)(2,1)S(1)} %get-tuple-element.26), channel_id=1, source_target_pairs={{0,1},{1,2},{2,3},{4,5},{5,6},{6,7},{8,9},{9,10},{10,11},{12,13},{... | collective-permute-start | bytes 61448 | tf_op jit(solution)/shard_map/ppermute | solution.py:453
  46.1 4.9 %collective-permute-start.7 = (bf16[80,128]{1,0:T(8,128)(2,1)S(1)}, bf16[80,128]{1,0:T(8,128)(2,1)S(1)}, u32[]{:S(2)}, u32[]{:S(2)}) collective-permute-start(bf16[80,128]{1,0:T(8,128)(2,1)S(1)} %get-tuple-element.27), channel_id=1, source_target_pairs={{1,0},{2,1},{3,2},{5,4},{6,5},{7,6},{9,8},{10,9},{11,10},{13,12},{... | collective-permute-start | bytes 61448 | tf_op jit(solution)/shard_map/ppermute | solution.py:453

commit v4 on v3

v4 whole, which is shorter than its diff:
```python
import jax
import jax.numpy as jnp
from jax import lax
from jax.experimental import pallas as pl
from jax.experimental.pallas import tpu as pltpu
from jax.sharding import PartitionSpec as P

HALO = 8
LANES = 128
ROWS = 64
COLS = 1024
BLOCKS = COLS // LANES
PADDED = ROWS + 2 * HALO
F32 = jnp.float32
BF16 = jnp.bfloat16
WORK = 20_000_000_000
LITTLE = 100_000_000
VMEM_LIMIT = 24 * 1024 * 1024


def lane_iota(rows):
    return lax.broadcasted_iota(jnp.int32, (rows, LANES), 1)


def move_strip(values, source, target):
    return pltpu.roll(values, (target - source) % LANES, 1)


def put_strip(total, values, source, target):
    lane = lane_iota(values.shape[0])
    inside = (lane >= target) & (lane < target + HALO)
    return jnp.where(inside, move_strip(values, source, target), total)


def block(index):
    return slice(index * LANES, (index + 1) * LANES)


def far_lane(part, field, side):
    return HALO * (part * 4 + field * 2 + side)


def my_index(pairs, pair, which):
    return pairs[which, 4 * lax.axis_index("epoch") + pair]


def look(pairs, pair, which):
    return pairs[which, 4 * lax.axis_size("epoch") + pair]


def is_last():
    return lax.axis_index("epoch") == lax.axis_size("epoch") - 1


def asked(pairs):
    groups = lax.axis_size("epoch")
    myself = lax.axis_index("epoch")
    asker = lax.rem(myself + groups // 2, groups)
    return pairs[1, 4 * asker + 1] - 2 * myself


def split_kernel(pairs, images, border, kept):
    lead = asked(pairs)
    kept[...] = images[...]
    strips = jnp.zeros((16, LANES), F32)
    for column in range(BLOCKS):
        for field in range(2):
            first = images[lead, field, :16, block(column)].astype(F32)
            last = images[lead, field, ROWS - 16 :, block(column)].astype(F32)
            rows = jnp.concatenate([first[:HALO], last[HALO:]], axis=0)
            border[pl.ds(column * 32 + field * 16, 16), :] = rows.astype(BF16)
            for side, at in ((0, 0), (1, BLOCKS - 1)):
                if column == at:
                    values = images[lead, field, :, block(column)].astype(F32)
                    for part in range(3):
                        begin = HALO + 16 * part
                        strips = put_strip(
                            strips,
                            values[begin : begin + 16],
                            side * (LANES - HALO),
                            far_lane(part, field, side),
                        )
    border[pl.ds(BLOCKS * 32, 16), :] = strips.astype(BF16)


def next_rows(one, other, k, field, rows, column):
    at = block(column)
    return one[k, field, rows, at].astype(F32) + other[k, field, rows, at].astype(F32)


def fields_of(a, b, c, d):
    return a * c + b * d, b * c - a * d, a * a + b * b, c * c + d * d


def put_split(target, f, at, value):
    count = value.shape[0]
    high = value.astype(BF16)
    target[f, :count, at] = high
    target[f, count : 2 * count, at] = (value - high.astype(F32)).astype(BF16)


def row_band(half_rows, count, row_of):
    inner = lax.broadcasted_iota(jnp.int32, (ROWS, 2 * count), 0)
    outer = lax.broadcasted_iota(jnp.int32, (ROWS, 2 * count), 1)
    outer = row_of(jnp.where(outer >= count, outer - count, outer))
    return (jnp.abs(outer - inner) <= half_rows).astype(F32).astype(BF16)


def border_row(k):
    return jnp.where(k < HALO, k - HALO, k + ROWS - HALO)


def wide_border_row(k):
    return jnp.where(k < 16, k - HALO, k + ROWS - 3 * HALO)


def row_sums(band, products):
    return jnp.dot(band, products, preferred_element_type=F32)


def near_slots(pairs, pair):
    begin = 2 * lax.axis_index("epoch")
    second = my_index(pairs, pair, 1)
    inside = (second >= begin) & (second < begin + 2)
    return my_index(pairs, pair, 0) - begin, (second & 1) + jnp.where(inside, 0, 2)


def column_band(half_cols):
    outer = lax.broadcasted_iota(jnp.int32, (4 * LANES, 2 * LANES), 0)
    inner = lax.broadcasted_iota(jnp.int32, (4 * LANES, 2 * LANES), 1)
    return (jnp.abs(outer - LANES - inner) <= half_cols).astype(F32).astype(BF16)


def own_kernel(
    pairs, images, inner, powers, own_up, own_down, own_columns, bands, products
):
    lead = asked(pairs)
    for column in range(BLOCKS):
        at = block(column)
        for field in range(2):
            values = images[lead, field, :, at].astype(F32)
            inner[field, :, at] = values[HALO : ROWS - HALO].astype(BF16)
    for a in range(2):
        rows = pl.ds(a * 16, 16)
        for column in range(BLOCKS):
            at = block(column)
            tops, bottoms = [], []
            for field in range(2):
                tops.append(images[a, field, :16, at].astype(F32)[:HALO])
                bottoms.append(images[a, field, ROWS - 16 :, at].astype(F32)[HALO:])
            own_up[rows, at] = jnp.concatenate(tops, axis=0).astype(BF16)
            own_down[rows, at] = jnp.concatenate(bottoms, axis=0).astype(BF16)
        for field in range(2):
            own_columns[2 * a + field, :, block(0)] = images[a, field, :, block(0)]
            own_columns[2 * a + field, :, block(1)] = images[a, field, :, block(BLOCKS - 1)]
    for pair in range(4):
        first = my_index(pairs, pair, 0) - 2 * lax.axis_index("epoch")
        for column in range(BLOCKS):
            at = block(column)
            a, b = (images[first, field, :, at].astype(F32) for field in range(2))
            put_split(products, pair, at, a * a + b * b)
        band = row_band(look(pairs, pair, 0), ROWS, lambda k: k)
        powers[pair] = row_sums(band, products[pair])
        band = column_band(look(pairs, pair, 1))
        bands[pair, : 4 * LANES, :] = band
        bands[pair, 4 * LANES :, :] = band


def far_fields(a, b, c, d):
    return a * c + b * d, b * c - a * d, c * c + d * d


def near_rows_kernel(pairs, images, one, other, partial, held, products):
    held[:2] = images[...]
    for column in range(BLOCKS):
        at = block(column)
        for k in range(2):
            for field in range(2):
                values = next_rows(one, other, k, field, slice(0, ROWS), column)
                held[2 + k, field, :, at] = values.astype(BF16)

    def one_pair(step, carry):
        pair = jnp.where(step == 0, 0, step + 1)
        first, second = near_slots(pairs, pair)
        for column in range(BLOCKS):
            at = block(column)
            a, b = (held[first, field, :, at].astype(F32) for field in range(2))
            c, d = (held[second, field, :, at].astype(F32) for field in range(2))
            for f, value in enumerate(far_fields(a, b, c, d)):
                put_split(products, f, at, value)
        band = row_band(look(pairs, pair, 0), ROWS, lambda k: k)
        for f in range(3):
            partial[3 * step + f] = row_sums(band, products[f])
        return carry

    lax.fori_loop(0, 3, one_pair, 0)


def pack_rows_kernel(own_up, own_down, one, other, border, _, up, down):
    up[:32, :] = own_up[...]
    down[:32, :] = own_down[...]
    for column in range(BLOCKS):
        at = block(column)
        for k in range(2):
            tops, bottoms = [], []
            for field in range(2):
                tops.append(next_rows(one, other, k, field, slice(0, 16), column)[:HALO])
                bottoms.append(
                    next_rows(one, other, k, field, slice(ROWS - 16, ROWS), column)[HALO:]
                )
            rows = pl.ds(32 + 16 * k, 16)
            up[rows, at] = jnp.concatenate(tops, axis=0).astype(BF16)
            down[rows, at] = jnp.concatenate(bottoms, axis=0).astype(BF16)
        real = border[pl.ds(column * 32, 16), :].astype(F32)
        imag = border[pl.ds(column * 32 + 16, 16), :].astype(F32)
        up[64:, at] = jnp.concatenate([real[:HALO], imag[:HALO]], axis=0).astype(BF16)
        down[64:, at] = jnp.concatenate([real[HALO:], imag[HALO:]], axis=0).astype(BF16)


def halo_rows(above, below, acquisition, field, column):
    at = pl.ds(acquisition * 16, 16)
    rows = slice(field * HALO, (field + 1) * HALO)
    return (
        above[at, block(column)].astype(F32)[rows],
        below[at, block(column)].astype(F32)[rows],
    )


def pack_columns_kernel(own_columns, one, other, border, above, below, _, left, right):
    strips = border[pl.ds(BLOCKS * 32, 16), :].astype(F32)
    for side, column, ref in ((0, 0, left), (1, BLOCKS - 1, right)):
        total = jnp.zeros((PADDED, LANES), F32)
        source = side * (LANES - HALO)
        for acquisition in range(5):
            for field in range(2):
                before, after = halo_rows(above, below, acquisition, field, column)
                if acquisition < 2:
                    main = own_columns[2 * acquisition + field, :, block(side)].astype(F32)
                elif acquisition < 4:
                    main = next_rows(one, other, acquisition - 2, field, slice(0, ROWS), column)
                else:
                    rows = border[pl.ds(column * 32 + field * 16, 16), :].astype(F32)
                    inner = [
                        move_strip(strips, far_lane(part, field, side), source)
                        for part in range(3)
                    ]
                    main = jnp.concatenate([rows[:HALO], *inner, rows[HALO:]], axis=0)
                values = jnp.concatenate([before, main, after], axis=0)
                total = put_strip(total, values, source, HALO * (2 * acquisition + field))
        ref[...] = total.astype(BF16)


def halo_block(from_left, from_right, acquisition, field):
    source = HALO * (2 * acquisition + field)
    blank = jnp.zeros((PADDED, LANES), F32)
    after = put_strip(blank, from_right[...].astype(F32), source, 0)
    return put_strip(after, from_left[...].astype(F32), source, LANES - HALO)


def column_sums(j, band, rows, edges):
    begin, end = max(j * 256 - LANES, 0), min(j * 256 + 3 * LANES, COLS)
    parts = []
    for term in range(2):
        if j == 0:
            parts.append(edges(term))
        parts.append(rows(term, slice(begin, end)))
        if j == BLOCKS // 2 - 1:
            parts.append(edges(term))
    both = row_sums(jnp.concatenate(parts, axis=1), band)
    return [both[f : f + ROWS] for f in range(0, both.shape[0], ROWS)]


def put_terms(target, f, value, columns=slice(None)):
    high = value.astype(BF16)
    at = pl.ds(f * ROWS, ROWS)
    target[0, at, columns] = high
    target[1, at, columns] = (value - high.astype(F32)).astype(BF16)


def result_copies(pair, slot, j, held, interferogram, coherence, done):
    at = pl.ds(j * 256, 256)
    return (
        pltpu.make_async_copy(
            held.at[slot, pl.ds(0, 2), :, at],
            interferogram.at[pair, :, :, at],
            done.at[slot, j, 0],
        ),
        pltpu.make_async_copy(
            held.at[slot, 2, :, at], coherence.at[pair, :, at], done.at[slot, j, 1]
        ),
    )


def finish(real, imag, power, other, pairs, pair, slot, j, results):
    held = results[0]
    window = ((2 * look(pairs, pair, 0) + 1) * (2 * look(pairs, pair, 1) + 1)).astype(F32)
    scale = 1.0 / jnp.full((8, 2 * LANES), window, F32)
    scale = jnp.concatenate([scale] * (ROWS // 8), axis=0)
    at = slice(j * 256, (j + 1) * 256)
    held[slot, 0, :, at] = real * scale
    held[slot, 1, :, at] = imag * scale
    held[slot, 2, :, at] = jnp.sqrt(real * real + imag * imag) / jnp.sqrt(power * other)
    for copy in result_copies(pair, slot, j, *results):
        copy.start()


def wait_for_results(pair, slot, results):
    for j in range(BLOCKS // 2):
        for copy in result_copies(pair, slot, j, *results):
            copy.wait()


def two_rows(upper, lower, acquisition, at):
    rows = pl.ds(pl.multiple_of(acquisition * 16, 16), 16)
    first, last = upper[rows, at].astype(F32), lower[rows, at].astype(F32)
    return (
        jnp.concatenate([first[:HALO], last[:HALO]], axis=0),
        jnp.concatenate([first[HALO:], last[HALO:]], axis=0),
    )


def power_of(a, b):
    return (a * a + b * b,)


def halo_rows_kernel(
    pairs, powers, partial, own_up, own_down, border, above, below, terms, far_partial, products
):
    def add(slots, half_rows, fields, place, main):
        for column in range(BLOCKS):
            at = block(column)
            values = [v for slot in slots for v in two_rows(above, below, slot, at)]
            for f, value in enumerate(fields(*values)):
                put_split(products, f, at, value)
        band = row_band(half_rows, 16, border_row)
        for f, value in enumerate(main):
            put_terms(terms, place + f, value() + row_sums(band, products[f, :32, :]))

    def one_pair(step, carry):
        pair = jnp.where(step == 0, 0, step + 1)
        main = (
            lambda: partial[3 * step],
            lambda: partial[3 * step + 1],
            lambda: powers[pair],
            lambda: partial[3 * step + 2],
        )
        add(near_slots(pairs, pair), look(pairs, pair, 0), fields_of, 4 * step, main)
        return carry

    lax.fori_loop(0, 3, one_pair, 0)
    first = my_index(pairs, 1, 0) - 2 * lax.axis_index("epoch")
    half_rows = look(pairs, 1, 0)
    add((first,), half_rows, power_of, 12, (lambda: powers[1],))
    for column in range(BLOCKS):
        at = block(column)
        outside = two_rows(above, below, first, at)
        inside = two_rows(own_up, own_down, first, at)
        values = [
            jnp.concatenate([o[:HALO], i, o[HALO:]], axis=0)
            for o, i in zip(outside, inside, strict=True)
        ]
        outside = two_rows(above, below, 4, at)
        for field in range(2):
            inside = border[pl.ds(column * 32 + field * 16, 16), :].astype(F32)
            values.append(
                jnp.concatenate([outside[field][:HALO], inside, outside[field][HALO:]], axis=0)
            )
        for f, value in enumerate(far_fields(*values)):
            put_split(products, f, at, value)
    band = row_band(half_rows, 32, wide_border_row)
    for f in range(3):
        far_partial[f] = row_sums(band, products[f])


def near_kernel(
    pairs, bands, terms, from_left, from_right,
    interferogram, coherence, far_power, far_edges,
    halos, products, edges, held, done,
):
    for acquisition in range(5):
        for field in range(2):
            halos[acquisition, field] = halo_block(from_left, from_right, acquisition, field)
    results = held, interferogram, coherence, done
    everything = slice(0, LANES)

    def edge(target, slots, half_rows, fields):
        values = [halos[slot, field] for slot in slots for field in range(2)]
        band = row_band(half_rows, PADDED, lambda k: k - HALO)
        for f, value in enumerate(fields(*values)):
            put_split(products, f, everything, value)
            put_terms(target, f, row_sums(band, products[f]))

    def one_pair(step, carry):
        pair = jnp.where(step == 0, 0, step + 1)
        edge(edges, near_slots(pairs, pair), look(pairs, pair, 0), fields_of)
        at = pl.ds(pl.multiple_of(step * 4 * ROWS, 4 * ROWS), 4 * ROWS)
        for j in range(BLOCKS // 2):
            blocks = column_sums(
                j, bands[pair], lambda term, columns: terms[term, at, columns], lambda term: edges[term]
            )
            finish(*blocks, pairs, pair, step, j, results)
        return carry

    lax.fori_loop(0, 3, one_pair, 0)

    first = my_index(pairs, 1, 0) - 2 * lax.axis_index("epoch")
    edge(edges, (first,), look(pairs, 1, 0), power_of)
    for j in range(BLOCKS // 2):
        (far_power[:, j * 256 : (j + 1) * 256],) = column_sums(
            j,
            bands[1],
            lambda term, columns: terms[term, 12 * ROWS :, columns],
            lambda term: edges[term, :ROWS, :],
        )
    edge(far_edges, (first, 4), look(pairs, 1, 0), far_fields)
    for step, pair in enumerate((0, 2, 3)):
        wait_for_results(pair, step, results)


def far_kernel(
    pairs, bands, images, inner, far_power, far_partial, far_edges, _, __,
    interferogram, coherence, products, terms, held, done,
):
    first = my_index(pairs, 1, 0) - 2 * lax.axis_index("epoch")
    results = held, interferogram, coherence, done
    band = row_band(look(pairs, 1, 0), ROWS - 2 * HALO, lambda k: k + HALO)

    def rows(j):
        for column in (2 * j, 2 * j + 1):
            at = block(column)
            a, b = (
                images[first, field, :, at].astype(F32)[HALO : ROWS - HALO] for field in range(2)
            )
            c, d = (inner[field, :, at].astype(F32) for field in range(2))
            for f, value in enumerate(far_fields(a, b, c, d)):
                put_split(products, f, at, value)
        at = slice(j * 256, (j + 1) * 256)
        for f in range(3):
            put_terms(terms, f, far_partial[f, :, at] + row_sums(band, products[f, :, at]), at)

    def columns(j):
        real, imag, other = column_sums(
            j, bands[1], lambda term, at: terms[term, :, at], lambda term: far_edges[term]
        )
        power = far_power[:, j * 256 : (j + 1) * 256]
        finish(real, imag, power, other, pairs, 1, 0, j, results)

    rows(0)
    for j in range(1, BLOCKS // 2):
        rows(j)
        columns(j - 1)
    columns(BLOCKS // 2 - 1)
    wait_for_results(1, 0, results)


VMEM = pl.BlockSpec(memory_space=pltpu.VMEM)
SMEM = pl.BlockSpec(memory_space=pltpu.SMEM)
ANY = pl.BlockSpec(memory_space=pl.ANY)
PARAMS = pltpu.CompilerParams(vmem_limit_bytes=VMEM_LIMIT)


def shape(dims, dtype=BF16):
    return jax.ShapeDtypeStruct(dims, dtype)


def exchange(first, last, axis):
    peers = lax.axis_size(axis)
    up = [(i, i + 1) for i in range(peers - 1)]
    down = [(j, i) for i, j in up]
    return lax.ppermute(last, axis, up), lax.ppermute(first, axis, down)


def local(kernel, operands, places, results, name, kept=None, held=(), aliases=None, flops=0):
    return pl.pallas_call(
        kernel,
        in_specs=places,
        out_specs=kept or [VMEM] * len(results),
        out_shape=results,
        scratch_shapes=list(held),
        input_output_aliases=aliases or {},
        compiler_params=PARAMS,
        cost_estimate=pl.CostEstimate(flops=flops, bytes_accessed=0, transcendentals=0),
        name=name,
    )(*operands)


def body(slc_images, pair_list, look_sizes):
    groups = lax.axis_size("epoch")
    swap = [(b, (b + groups // 2) % groups) for b in range(groups)]
    table = jnp.concatenate([pair_list.T, look_sizes.T], axis=1)

    one = lax.ppermute(slc_images, "epoch", [(b + 1, b) for b in range(groups - 1)])
    border, images = local(
        split_kernel,
        (table, slc_images),
        [SMEM, VMEM],
        [shape((BLOCKS * 32 + 16, LANES)), shape((2, 2, ROWS, COLS))],
        "split",
    )
    border = lax.ppermute(border, "epoch", swap)
    inner, powers, own_up, own_down, own_columns, bands = local(
        own_kernel,
        (table, images),
        [SMEM, VMEM],
        [
            shape((2, ROWS - 2 * HALO, COLS)),
            shape((4, ROWS, COLS), F32),
            shape((32, COLS)),
            shape((32, COLS)),
            shape((4, ROWS, 2 * LANES)),
            shape((4, 8 * LANES, 2 * LANES)),
        ],
        "own",
        held=[pltpu.VMEM((4, 2 * ROWS, COLS), BF16)],
        flops=WORK,
    )
    inner = lax.ppermute(inner, "epoch", swap)
    other = lax.ppermute(images, "epoch", [(groups - 2, groups - 1)])

    up, down = local(
        pack_rows_kernel,
        (own_up, own_down, one, other, border, powers),
        [VMEM] * 6,
        [shape((80, COLS))] * 2,
        "pack_rows",
    )
    above, below = exchange(up, down, "row")
    (partial,) = local(
        near_rows_kernel,
        (table, images, one, other),
        [SMEM] + [VMEM] * 3,
        [shape((9, ROWS, COLS), F32)],
        "near_rows",
        held=[
            pltpu.VMEM((4, 2, ROWS, COLS), BF16),
            pltpu.VMEM((3, 2 * ROWS, COLS), BF16),
        ],
        flops=LITTLE,
    )
    left, right = local(
        pack_columns_kernel,
        (own_columns, one, other, border, above, below, partial),
        [VMEM] * 7,
        [shape((PADDED, LANES))] * 2,
        "pack_columns",
    )
    from_left, from_right = exchange(left, right, "col")
    terms, rest = local(
        halo_rows_kernel,
        (table, powers, partial, own_up, own_down, border, above, below),
        [SMEM] + [VMEM] * 7,
        [shape((2, 13 * ROWS, COLS)), shape((3, ROWS, COLS), F32)],
        "halo_rows",
        held=[pltpu.VMEM((4, 64, COLS), BF16)],
        flops=LITTLE,
    )

    outs = [shape((4, 2, ROWS, COLS), F32), shape((4, ROWS, COLS), F32)]
    interferogram, coherence, power, edges = local(
        near_kernel,
        (table, bands, terms, from_left, from_right),
        [SMEM] + [VMEM] * 4,
        [*outs, shape((ROWS, COLS), F32), shape((2, 3 * ROWS, LANES))],
        "near_pairs",
        kept=[ANY, ANY, VMEM, VMEM],
        held=[
            pltpu.VMEM((5, 2, PADDED, LANES), F32),
            pltpu.VMEM((4, 2 * PADDED, LANES), BF16),
            pltpu.VMEM((2, 4 * ROWS, LANES), BF16),
            pltpu.VMEM((3, 3, ROWS, COLS), F32),
            pltpu.SemaphoreType.DMA((3, BLOCKS // 2, 2)),
        ],
    )
    return local(
        far_kernel,
        (table, bands, images, inner, power, rest, edges, interferogram, coherence),
        [SMEM] + [VMEM] * 6 + [ANY] * 2,
        outs,
        "far_pair",
        kept=[ANY, ANY],
        held=[
            pltpu.VMEM((3, 2 * (ROWS - 2 * HALO), COLS), BF16),
            pltpu.VMEM((2, 3 * ROWS, COLS), BF16),
            pltpu.VMEM((1, 3, ROWS, COLS), F32),
            pltpu.SemaphoreType.DMA((1, BLOCKS // 2, 2)),
        ],
        aliases={7: 0, 8: 1},
    )


def solution(mesh):
    placed = (P("epoch", None, "row", "col"), P(), P("epoch", None))
    return jax.shard_map(
        body,
        mesh=mesh,
        in_specs=placed,
        out_specs=(P("epoch", None, "row", "col"), P("epoch", "row", "col")),
        check_vma=False,
    )
```

time: 58.9 us -> 55.7 us (0.946)
  the two profiles are of different devices: /device:TPU:1 before, /device:TPU:328 now
where the time goes in v4:
time: 55.7 us; the launch traced here: 55.4 us
  starting transfers between devices  28.1 us (50%)
  Pallas kernels  13.9 us (25%)
  waiting for transfers between devices  10.8 us (19%)
  local copies, waits for them, and re-layouts  1.04 us (2%)
  between operations  0.74 us (1%)
  other arithmetic  0.7 us (1%)
    pallas_call x8, Pallas kernels, local(): pl.pallas_call(kernel, in_specs=places, out_specs=kept or [VMEM] * len(re...  13.9 us
    ppermute x1, starting transfers between devices, body(): inner = lax.ppermute(inner, 'epoch', swap)  12.6 us
    ppermute x4, starting transfers between devices, exchange(): return (lax.ppermute(last, axis, up), lax.ppermute(first, axis, down))  10.5 us
    ppermute x1, waiting for transfers between devices, body(): border = lax.ppermute(border, 'epoch', swap)  6.11 us
    ppermute x4, waiting for transfers between devices, exchange(): return (lax.ppermute(last, axis, up), lax.ppermute(first, axis, down))  4.7 us
    ppermute x1, starting transfers between devices, body(): lax.ppermute(slc_images, 'epoch', [(b + 1, b) for b in range(groups - 1)])  2.36 us
    ppermute x1, starting transfers between devices, body(): border = lax.ppermute(border, 'epoch', swap)  1.92 us
  transfers between devices with their start and end apart: 8, of which 3 were waited for; matrix products, arithmetic and copies ran while one was open for 1% of the time, Pallas kernels for 21%

profile of v4, /device:TPU:328, one launch (start us, length us, event | category | flops | bytes accessed | tf_op | source)
XLA Modules:
  0.0 55.4 jit_solution(14189177090948196269)
XLA Ops:
  0.6 2.4 %collective-permute-start.1 = (bf16[2,2,64,1024]{3,2,1,0:T(8,128)(2,1)}, bf16[2,2,64,1024]{3,2,1,0:T(8,128)(2,1)S(1)}, u32[]{:S(2)}, u32[]{:S(2)}) collective-permute-start(bf16[2,2,64,1024]{3,2,1,0:T(8,128)(2,1)} %images.1), channel_id=1, source_target_pairs={{16,0},{32,16},{48,32},{64,48},{80,64},{96,80},{112,96},{128,112},... | collective-permute-start | bytes 1572872 | tf_op jit(solution)/shard_map/ppermute | solution.py:492
  3.0 0.7 %pad_add_fusion.pairs = s32[2,132]{1,0:T(2,128)S(1)} fusion(s32[2,4]{1,0:T(2,128)} %bitcast.2, s32[2,128]{1,0:T(2,128)} %bitcast.3), kind=kLoop, calls=%fused_computation | loop fusion | flops 264 | bytes 2112 | tf_op jit(solution)/shard_map/concatenate | solution.py:490
  3.7 1.0 %copy-done = bf16[2,2,64,1024]{3,2,1,0:T(8,128)(2,1)S(1)} copy-done((bf16[2,2,64,1024]{3,2,1,0:T(8,128)(2,1)S(1)}, bf16[2,2,64,1024]{3,2,1,0:T(8,128)(2,1)}, u32[]{:S(2)}) %copy-start) | copy-done | bytes 524312
  4.7 0.7 %split.1 = (bf16[272,128]{1,0:T(8,128)(2,1)S(1)}, bf16[2,2,64,1024]{3,2,1,0:T(8,128)(2,1)S(1)}) custom-call(s32[2,132]{1,0:T(2,128)S(1)} %pad_add_fusion.pairs, bf16[2,2,64,1024]{3,2,1,0:T(8,128)(2,1)S(1)} %copy-done), custom_call_target="tpu_custom_call" | custom-call | tf_op jit(solution)/shard_map/split/pallas_call | solution.py:474
  5.4 1.9 %collective-permute-start.3 = (bf16[272,128]{1,0:T(8,128)(2,1)S(1)}, bf16[272,128]{1,0:T(8,128)(2,1)S(1)}, u32[]{:S(2)}, u32[]{:S(2)}) collective-permute-start(bf16[272,128]{1,0:T(8,128)(2,1)S(1)} %get-tuple-element.26), channel_id=1, source_target_pairs={{0,256},{16,272},{32,288},{48,304},{64,320},{80,336},{96,352},{112... | collective-permute-start | bytes 208904 | tf_op jit(solution)/shard_map/ppermute | solution.py:500
  7.3 0.7 %collective-permute-start.2 = (bf16[2,2,64,1024]{3,2,1,0:T(8,128)(2,1)S(1)}, bf16[2,2,64,1024]{3,2,1,0:T(8,128)(2,1)S(1)}, u32[]{:S(2)}, u32[]{:S(2)}) collective-permute-start(bf16[2,2,64,1024]{3,2,1,0:T(8,128)(2,1)S(1)} %get-tuple-element.20.images), channel_id=1, source_target_pairs={{480,496},{481,497},{482,498},{483,499},{484,500},{485,501},{486,5... | collective-permute-start | bytes 1572872 | tf_op jit(solution)/shard_map/ppermute | solution.py:518
  8.0 1.6 %own.1 = (bf16[2,48,1024]{2,1,0:T(8,128)(2,1)S(1)}, f32[4,64,1024]{2,1,0:T(8,128)S(1)}, bf16[32,1024]{1,0:T(8,128)(2,1)S(1)}, bf16[32,1024]{1,0:T(8,128)(2,1)S(1...) custom-call(s32[2,132]{1,0:T(2,128)S(1)} %pad_add_fusion.pairs, ...), custom_call_target="tpu_custom_call" | custom-call | flops 20000000000 | tf_op jit(solution)/shard_map/own/pallas_call | solution.py:474
  9.7 12.6 %collective-permute-start = (bf16[2,48,1024]{2,1,0:T(8,128)(2,1)S(1)}, bf16[2,48,1024]{2,1,0:T(8,128)(2,1)S(1)}, u32[]{:S(2)}, u32[]{:S(2)}) collective-permute-start(bf16[2,48,1024]{2,1,0:T(8,128)(2,1)S(1)} %get-tuple-element.22), channel_id=1, source_target_pairs={{0,256},{16,272},{32,288},{48,304},{64,320},{80,336},{96,352},{112... | collective-permute-start | bytes 589832 | tf_op jit(solution)/shard_map/ppermute | solution.py:517
  22.3 6.1 %collective-permute-done.3.border = bf16[272,128]{1,0:T(8,128)(2,1)S(1)} collective-permute-done((bf16[272,128]{1,0:T(8,128)(2,1)S(1)}, bf16[272,128]{1,0:T(8,128)(2,1)S(1)}, u32[]{:S(2)}, u32[]{:S(2)}) %collective-permute-start.3) | collective-permute-done | bytes 69664 | tf_op jit(solution)/shard_map/ppermute | solution.py:500
  28.4 0.0 collective-permute-done.1.one
  28.4 0.0 collective-permute-done.2.other
  28.4 0.1 pack_rows.1
  28.5 3.4 %collective-permute-start.4 = (bf16[80,1024]{1,0:T(8,128)(2,1)S(1)}, bf16[80,1024]{1,0:T(8,128)(2,1)S(1)}, u32[]{:S(2)}, u32[]{:S(2)}) collective-permute-start(bf16[80,1024]{1,0:T(8,128)(2,1)S(1)} %get-tuple-element.27), channel_id=1, source_target_pairs={{0,4},{4,8},{8,12},{1,5},{5,9},{9,13},{2,6},{6,10},{10,14},{3,7},{... | collective-permute-start | bytes 491528 | tf_op jit(solution)/shard_map/ppermute | solution.py:470
  31.9 1.3 %collective-permute-start.5 = (bf16[80,1024]{1,0:T(8,128)(2,1)S(1)}, bf16[80,1024]{1,0:T(8,128)(2,1)S(1)}, u32[]{:S(2)}, u32[]{:S(2)}) collective-permute-start(bf16[80,1024]{1,0:T(8,128)(2,1)S(1)} %get-tuple-element.28), channel_id=1, source_target_pairs={{4,0},{8,4},{12,8},{5,1},{9,5},{13,9},{6,2},{10,6},{14,10},{7,3},{... | collective-permute-start | bytes 491528 | tf_op jit(solution)/shard_map/ppermute | solution.py:470
  33.2 2.5 %near_rows.1.partial._ = f32[9,64,1024]{2,1,0:T(8,128)S(1)} custom-call(s32[2,132]{1,0:T(2,128)S(1)} %pad_add_fusion.pairs, bf16[2,2,64,1024]{3,2,1,0:T(8,128)(2,1)S(1)} %get-tuple-element.20.images, bf16[2,2,64,1024]{3,2,1,0:T(8,128)(2,1)S(1)} %collective-permute-done.1.one, bf16[2,2,64,1024]{3,2,1,0:T(8,128)(2,1)S(1)} %collective-permute-done.2.other), custom_call_target="tpu_custom_call" | custom-call | flops 100000000 | tf_op jit(solution)/shard_map/near_rows/pallas_call | solution.py:474
  35.7 3.4 %collective-permute-done.5.below = bf16[80,1024]{1,0:T(8,128)(2,1)S(1)} collective-permute-done((bf16[80,1024]{1,0:T(8,128)(2,1)S(1)}, bf16[80,1024]{1,0:T(8,128)(2,1)S(1)}, u32[]{:S(2)}, u32[]{:S(2)}) %collective-permute-start.5) | collective-permute-done | bytes 163872 | tf_op jit(solution)/shard_map/ppermute | solution.py:470
  39.1 0.2 pack_columns.1
  39.4 3.5 %collective-permute-start.6 = (bf16[80,128]{1,0:T(8,128)(2,1)S(1)}, bf16[80,128]{1,0:T(8,128)(2,1)S(1)}, u32[]{:S(2)}, u32[]{:S(2)}) collective-permute-start(bf16[80,128]{1,0:T(8,128)(2,1)S(1)} %get-tuple-element.31), channel_id=1, source_target_pairs={{0,1},{1,2},{2,3},{4,5},{5,6},{6,7},{8,9},{9,10},{10,11},{12,13},{... | collective-permute-start | bytes 61448 | tf_op jit(solution)/shard_map/ppermute | solution.py:470
  42.9 2.4 %collective-permute-start.7 = (bf16[80,128]{1,0:T(8,128)(2,1)S(1)}, bf16[80,128]{1,0:T(8,128)(2,1)S(1)}, u32[]{:S(2)}, u32[]{:S(2)}) collective-permute-start(bf16[80,128]{1,0:T(8,128)(2,1)S(1)} %get-tuple-element.32), channel_id=1, source_target_pairs={{1,0},{2,1},{3,2},{5,4},{6,5},{7,6},{9,8},{10,9},{11,10},{13,12},{... | collective-permute-start | bytes 61448 | tf_op jit(solution)/shard_map/ppermute | solution.py:470
  45.2 2.0 %halo_rows.1 = (bf16[2,832,1024]{2,1,0:T(8,128)(2,1)S(1)}, f32[3,64,1024]{2,1,0:T(8,128)S(1)}) custom-call(s32[2,132]{1,0:T(2,128)S(1)} %pad_add_fusion.pairs, f32[4,64,1024]{2,1,0:T(8,128)S(1)} %get-tuple-element.23._.powers, f32[9,64,1024]{2,1,0:T(8,128)S(1)} %near_rows.1.partial._, bf16[32,1024]{1,0:T(8,128)(2,1)S(1)} %get-tuple-element.24.own_up, ...), custom_call_target="tpu_custom_call" | custom-call | flops 100000000 | tf_op jit(solution)/shard_map/halo_rows/pallas_call | solution.py:474
  47.2 0.0 collective-permute-done.6.from_left
  47.2 1.3 %collective-permute-done.7.from_right = bf16[80,128]{1,0:T(8,128)(2,1)S(1)} collective-permute-done((bf16[80,128]{1,0:T(8,128)(2,1)S(1)}, bf16[80,128]{1,0:T(8,128)(2,1)S(1)}, u32[]{:S(2)}, u32[]{:S(2)}) %collective-permute-start.7) | collective-permute-done | bytes 20512 | tf_op jit(solution)/shard_map/ppermute | solution.py:470
  48.5 4.4 %near_pairs.1 = (f32[4,2,64,1024]{3,2,1,0:T(8,128)}, f32[4,64,1024]{2,1,0:T(8,128)}, f32[64,1024]{1,0:T(8,128)S(1)}, bf16[2,192,128]{2,1,0:T(8,128)(2,1)S(1)}) custom-call(s32[2,132]{1,0:T(2,128)S(1)} %pad_add_fusion.pairs, bf16[4,1024,256]{2,1,0:T(8,128)(2,1)S(1)} %get-tuple-element.21.bands, bf16[2,832,1024]{2,1,0:T(8,128)(2,1)S(1)} %get-tuple-element.29.terms, ...), custom_call_target="tpu_custom_call" | custom-call | tf_op jit(solution)/shard_map/near_pairs/pallas_call | solution.py:474
  53.0 2.4 %far_pair.1 = (f32[4,2,64,1024]{3,2,1,0:T(8,128)}, f32[4,64,1024]{2,1,0:T(8,128)}) custom-call(s32[2,132]{1,0:T(2,128)S(1)} %pad_add_fusion.pairs, bf16[4,1024,256]{2,1,0:T(8,128)(2,1)S(1)} %get-tuple-element.21.bands, bf16[2,2,64,1024]{3,2,1,0:T(8,128)(2,1)S(1)} %get-tuple-element.20.images, ...), custom_call_target="tpu_custom_call", output_to_operand_aliasing={{0}: (7, {}), {1}: (8, {})} | custom-call | tf_op jit(solution)/shard_map/far_pair/pallas_call | solution.py:474
  (3 shorter events, 0.0 us)
Async XLA Ops:
  0.6 27.8 %collective-permute-start.1 = (bf16[2,2,64,1024]{3,2,1,0:T(8,128)(2,1)}, bf16[2,2,64,1024]{3,2,1,0:T(8,128)(2,1)S(1)}, u32[]{:S(2)}, u32[]{:S(2)}) collective-permute-start(bf16[2,2,64,1024]{3,2,1,0:T(8,128)(2,1)} %images.1), channel_id=1, source_target_pairs={{16,0},{32,16},{48,32},{64,48},{80,64},{96,80},{112,96},{128,112},... | collective-permute-start | bytes 1572872 | tf_op jit(solution)/shard_map/ppermute | solution.py:492
  3.7 1.0 %copy-start = (bf16[2,2,64,1024]{3,2,1,0:T(8,128)(2,1)S(1)}, bf16[2,2,64,1024]{3,2,1,0:T(8,128)(2,1)}, u32[]{:S(2)}) copy-start(bf16[2,2,64,1024]{3,2,1,0:T(8,128)(2,1)} %images.1) | copy-start | bytes 1572868
  5.4 23.0 %collective-permute-start.3 = (bf16[272,128]{1,0:T(8,128)(2,1)S(1)}, bf16[272,128]{1,0:T(8,128)(2,1)S(1)}, u32[]{:S(2)}, u32[]{:S(2)}) collective-permute-start(bf16[272,128]{1,0:T(8,128)(2,1)S(1)} %get-tuple-element.26), channel_id=1, source_target_pairs={{0,256},{16,272},{32,288},{48,304},{64,320},{80,336},{96,352},{112... | collective-permute-start | bytes 208904 | tf_op jit(solution)/shard_map/ppermute | solution.py:500
  7.3 21.1 %collective-permute-start.2 = (bf16[2,2,64,1024]{3,2,1,0:T(8,128)(2,1)S(1)}, bf16[2,2,64,1024]{3,2,1,0:T(8,128)(2,1)S(1)}, u32[]{:S(2)}, u32[]{:S(2)}) collective-permute-start(bf16[2,2,64,1024]{3,2,1,0:T(8,128)(2,1)S(1)} %get-tuple-element.20.images), channel_id=1, source_target_pairs={{480,496},{481,497},{482,498},{483,499},{484,500},{485,501},{486,5... | collective-permute-start | bytes 1572872 | tf_op jit(solution)/shard_map/ppermute | solution.py:518
  9.7 43.3 %collective-permute-start = (bf16[2,48,1024]{2,1,0:T(8,128)(2,1)S(1)}, bf16[2,48,1024]{2,1,0:T(8,128)(2,1)S(1)}, u32[]{:S(2)}, u32[]{:S(2)}) collective-permute-start(bf16[2,48,1024]{2,1,0:T(8,128)(2,1)S(1)} %get-tuple-element.22), channel_id=1, source_target_pairs={{0,256},{16,272},{32,288},{48,304},{64,320},{80,336},{96,352},{112... | collective-permute-start | bytes 589832 | tf_op jit(solution)/shard_map/ppermute | solution.py:517
  28.5 7.2 %collective-permute-start.4 = (bf16[80,1024]{1,0:T(8,128)(2,1)S(1)}, bf16[80,1024]{1,0:T(8,128)(2,1)S(1)}, u32[]{:S(2)}, u32[]{:S(2)}) collective-permute-start(bf16[80,1024]{1,0:T(8,128)(2,1)S(1)} %get-tuple-element.27), channel_id=1, source_target_pairs={{0,4},{4,8},{8,12},{1,5},{5,9},{9,13},{2,6},{6,10},{10,14},{3,7},{... | collective-permute-start | bytes 491528 | tf_op jit(solution)/shard_map/ppermute | solution.py:470
  31.9 7.2 %collective-permute-start.5 = (bf16[80,1024]{1,0:T(8,128)(2,1)S(1)}, bf16[80,1024]{1,0:T(8,128)(2,1)S(1)}, u32[]{:S(2)}, u32[]{:S(2)}) collective-permute-start(bf16[80,1024]{1,0:T(8,128)(2,1)S(1)} %get-tuple-element.28), channel_id=1, source_target_pairs={{4,0},{8,4},{12,8},{5,1},{9,5},{13,9},{6,2},{10,6},{14,10},{7,3},{... | collective-permute-start | bytes 491528 | tf_op jit(solution)/shard_map/ppermute | solution.py:470
  39.4 7.9 %collective-permute-start.6 = (bf16[80,128]{1,0:T(8,128)(2,1)S(1)}, bf16[80,128]{1,0:T(8,128)(2,1)S(1)}, u32[]{:S(2)}, u32[]{:S(2)}) collective-permute-start(bf16[80,128]{1,0:T(8,128)(2,1)S(1)} %get-tuple-element.31), channel_id=1, source_target_pairs={{0,1},{1,2},{2,3},{4,5},{5,6},{6,7},{8,9},{9,10},{10,11},{12,13},{... | collective-permute-start | bytes 61448 | tf_op jit(solution)/shard_map/ppermute | solution.py:470
  42.9 5.7 %collective-permute-start.7 = (bf16[80,128]{1,0:T(8,128)(2,1)S(1)}, bf16[80,128]{1,0:T(8,128)(2,1)S(1)}, u32[]{:S(2)}, u32[]{:S(2)}) collective-permute-start(bf16[80,128]{1,0:T(8,128)(2,1)S(1)} %get-tuple-element.32), channel_id=1, source_target_pairs={{1,0},{2,1},{3,2},{5,4},{6,5},{7,6},{9,8},{10,9},{11,10},{13,12},{... | collective-permute-start | bytes 61448 | tf_op jit(solution)/shard_map/ppermute | solution.py:470

commit v5 on v4

--- a/solution.py
+++ b/solution.py
@@ -60,18 +60,22 @@
 
 
 def split_kernel(pairs, images, border, kept):
+    kept[...] = images[...]
     lead = asked(pairs)
-    kept[...] = images[...]
+
+    def chosen(field, rows, column):
+        return images[lead, field, rows, block(column)].astype(F32)
+
     strips = jnp.zeros((16, LANES), F32)
     for column in range(BLOCKS):
         for field in range(2):
-            first = images[lead, field, :16, block(column)].astype(F32)
-            last = images[lead, field, ROWS - 16 :, block(column)].astype(F32)
+            first = chosen(field, slice(0, 16), column)
+            last = chosen(field, slice(ROWS - 16, ROWS), column)
             rows = jnp.concatenate([first[:HALO], last[HALO:]], axis=0)
             border[pl.ds(column * 32 + field * 16, 16), :] = rows.astype(BF16)
             for side, at in ((0, 0), (1, BLOCKS - 1)):
                 if column == at:
-                    values = images[lead, field, :, block(column)].astype(F32)
+                    values = chosen(field, slice(0, ROWS), column)
                     for part in range(3):
                         begin = HALO + 16 * part
                         strips = put_strip(
@@ -118,6 +122,12 @@
     return jnp.dot(band, products, preferred_element_type=F32)
 
 
+def column_band(half_cols):
+    outer = lax.broadcasted_iota(jnp.int32, (4 * LANES, 2 * LANES), 0)
+    inner = lax.broadcasted_iota(jnp.int32, (4 * LANES, 2 * LANES), 1)
+    return (jnp.abs(outer - LANES - inner) <= half_cols).astype(F32).astype(BF16)
+
+
 def near_slots(pairs, pair):
     begin = 2 * lax.axis_index("epoch")
     second = my_index(pairs, pair, 1)
@@ -125,15 +135,35 @@
     return my_index(pairs, pair, 0) - begin, (second & 1) + jnp.where(inside, 0, 2)
 
 
-def column_band(half_cols):
-    outer = lax.broadcasted_iota(jnp.int32, (4 * LANES, 2 * LANES), 0)
-    inner = lax.broadcasted_iota(jnp.int32, (4 * LANES, 2 * LANES), 1)
-    return (jnp.abs(outer - LANES - inner) <= half_cols).astype(F32).astype(BF16)
-
-
-def own_kernel(
-    pairs, images, inner, powers, own_up, own_down, own_columns, bands, products
+def references_kernel(
+    pairs, images, powers, mine, bands, edge_bands, far_band, slots, scale, products
 ):
+    for pair in range(4):
+        band = column_band(look(pairs, pair, 1))
+        bands[pair, : 4 * LANES, :] = band
+        bands[pair, 4 * LANES :, :] = band
+        edge_bands[pair] = row_band(look(pairs, pair, 0), PADDED, lambda k: k - HALO)
+        window = (2 * look(pairs, pair, 0) + 1) * (2 * look(pairs, pair, 1) + 1)
+        scale[pair] = 1.0 / jnp.full((HALO, 2 * LANES), window.astype(F32), F32)
+        for k, slot in enumerate(near_slots(pairs, pair)):
+            slots[pair, k] = jnp.full((HALO, LANES), slot.astype(F32), F32)
+    far_band[...] = row_band(look(pairs, 1, 0), ROWS - 2 * HALO, lambda k: k + HALO)
+    for pair in range(4):
+        first = my_index(pairs, pair, 0) - 2 * lax.axis_index("epoch")
+        for column in range(BLOCKS):
+            at = block(column)
+            a, b = (images[first, field, :, at].astype(F32) for field in range(2))
+            put_split(products, pair, at, a * a + b * b)
+        band = row_band(look(pairs, pair, 0), ROWS, lambda k: k)
+        powers[pair] = row_sums(band, products[pair])
+    first = my_index(pairs, 1, 0) - 2 * lax.axis_index("epoch")
+    for column in range(BLOCKS):
+        at = block(column)
+        for field in range(2):
+            mine[field, :, at] = images[first, field, :, at].astype(F32)[HALO : ROWS - HALO]
+
+
+def interior_kernel(pairs, images, _, inner, own_up, own_down, own_columns):
     lead = asked(pairs)
     for column in range(BLOCKS):
         at = block(column)
@@ -153,17 +183,6 @@
         for field in range(2):
             own_columns[2 * a + field, :, block(0)] = images[a, field, :, block(0)]
             own_columns[2 * a + field, :, block(1)] = images[a, field, :, block(BLOCKS - 1)]
-    for pair in range(4):
-        first = my_index(pairs, pair, 0) - 2 * lax.axis_index("epoch")
-        for column in range(BLOCKS):
-            at = block(column)
-            a, b = (images[first, field, :, at].astype(F32) for field in range(2))
-            put_split(products, pair, at, a * a + b * b)
-        band = row_band(look(pairs, pair, 0), ROWS, lambda k: k)
-        powers[pair] = row_sums(band, products[pair])
-        band = column_band(look(pairs, pair, 1))
-        bands[pair, : 4 * LANES, :] = band
-        bands[pair, 4 * LANES :, :] = band
 
 
 def far_fields(a, b, c, d):
@@ -291,11 +310,9 @@
     )
 
 
-def finish(real, imag, power, other, pairs, pair, slot, j, results):
+def finish(real, imag, power, other, scale, pair, slot, j, results):
     held = results[0]
-    window = ((2 * look(pairs, pair, 0) + 1) * (2 * look(pairs, pair, 1) + 1)).astype(F32)
-    scale = 1.0 / jnp.full((8, 2 * LANES), window, F32)
-    scale = jnp.concatenate([scale] * (ROWS // 8), axis=0)
+    scale = jnp.concatenate([scale] * (ROWS // HALO), axis=0)
     at = slice(j * 256, (j + 1) * 256)
     held[slot, 0, :, at] = real * scale
     held[slot, 1, :, at] = imag * scale
@@ -373,7 +390,7 @@
 
 
 def near_kernel(
-    pairs, bands, terms, from_left, from_right,
+    bands, edge_bands, slots, scale, terms, from_left, from_right,
     interferogram, coherence, far_power, far_edges,
     halos, products, edges, held, done,
 ):
@@ -383,28 +400,34 @@
     results = held, interferogram, coherence, done
     everything = slice(0, LANES)
 
-    def edge(target, slots, half_rows, fields):
-        values = [halos[slot, field] for slot in slots for field in range(2)]
-        band = row_band(half_rows, PADDED, lambda k: k - HALO)
+    def halo_of(pair, k, field):
+        slot = jnp.concatenate([slots[pair, k]] * (PADDED // HALO), axis=0)
+        value = halos[0, field]
+        for other in range(1, 4 if k else 2):
+            value = jnp.where(slot == other, halos[other, field], value)
+        return value
+
+    def edge(target, values, pair, fields):
         for f, value in enumerate(fields(*values)):
             put_split(products, f, everything, value)
-            put_terms(target, f, row_sums(band, products[f]))
+            put_terms(target, f, row_sums(edge_bands[pair], products[f]))
 
     def one_pair(step, carry):
         pair = jnp.where(step == 0, 0, step + 1)
-        edge(edges, near_slots(pairs, pair), look(pairs, pair, 0), fields_of)
+        values = [halo_of(pair, k, field) for k in range(2) for field in range(2)]
+        edge(edges, values, pair, fields_of)
         at = pl.ds(pl.multiple_of(step * 4 * ROWS, 4 * ROWS), 4 * ROWS)
         for j in range(BLOCKS // 2):
             blocks = column_sums(
                 j, bands[pair], lambda term, columns: terms[term, at, columns], lambda term: edges[term]
             )
-            finish(*blocks, pairs, pair, step, j, results)
+            finish(*blocks, scale[pair], pair, step, j, results)
         return carry
 
     lax.fori_loop(0, 3, one_pair, 0)
 
-    first = my_index(pairs, 1, 0) - 2 * lax.axis_index("epoch")
-    edge(edges, (first,), look(pairs, 1, 0), power_of)
+    reference = [halo_of(1, 0, field) for field in range(2)]
+    edge(edges, reference, 1, power_of)
     for j in range(BLOCKS // 2):
         (far_power[:, j * 256 : (j + 1) * 256],) = column_sums(
             j,
@@ -412,38 +435,34 @@
             lambda term, columns: terms[term, 12 * ROWS :, columns],
             lambda term: edges[term, :ROWS, :],
         )
-    edge(far_edges, (first, 4), look(pairs, 1, 0), far_fields)
+    edge(far_edges, [*reference, halos[4, 0], halos[4, 1]], 1, far_fields)
     for step, pair in enumerate((0, 2, 3)):
         wait_for_results(pair, step, results)
 
 
 def far_kernel(
-    pairs, bands, images, inner, far_power, far_partial, far_edges, _, __,
+    bands, band, scale, mine, inner, far_power, far_partial, far_edges, _, __,
     interferogram, coherence, products, terms, held, done,
 ):
-    first = my_index(pairs, 1, 0) - 2 * lax.axis_index("epoch")
     results = held, interferogram, coherence, done
-    band = row_band(look(pairs, 1, 0), ROWS - 2 * HALO, lambda k: k + HALO)
 
     def rows(j):
         for column in (2 * j, 2 * j + 1):
             at = block(column)
-            a, b = (
-                images[first, field, :, at].astype(F32)[HALO : ROWS - HALO] for field in range(2)
-            )
+            a, b = mine[0, :, at], mine[1, :, at]
             c, d = (inner[field, :, at].astype(F32) for field in range(2))
             for f, value in enumerate(far_fields(a, b, c, d)):
                 put_split(products, f, at, value)
         at = slice(j * 256, (j + 1) * 256)
         for f in range(3):
-            put_terms(terms, f, far_partial[f, :, at] + row_sums(band, products[f, :, at]), at)
+            put_terms(terms, f, far_partial[f, :, at] + row_sums(band[...], products[f, :, at]), at)
 
     def columns(j):
         real, imag, other = column_sums(
             j, bands[1], lambda term, at: terms[term, :, at], lambda term: far_edges[term]
         )
         power = far_power[:, j * 256 : (j + 1) * 256]
-        finish(real, imag, power, other, pairs, 1, 0, j, results)
+        finish(real, imag, power, other, scale[1], 1, 0, j, results)
 
     rows(0)
     for j in range(1, BLOCKS // 2):
@@ -498,20 +517,34 @@
         "split",
     )
     border = lax.ppermute(border, "epoch", swap)
-    inner, powers, own_up, own_down, own_columns, bands = local(
-        own_kernel,
+    powers, mine, bands, edge_bands, far_band, slots, scale = local(
+        references_kernel,
         (table, images),
         [SMEM, VMEM],
         [
+            shape((4, ROWS, COLS), F32),
+            shape((2, ROWS - 2 * HALO, COLS), F32),
+            shape((4, 8 * LANES, 2 * LANES)),
+            shape((4, ROWS, 2 * PADDED)),
+            shape((ROWS, 2 * (ROWS - 2 * HALO))),
+            shape((4, 2, HALO, LANES), F32),
+            shape((4, HALO, 2 * LANES), F32),
+        ],
+        "references",
+        held=[pltpu.VMEM((4, 2 * ROWS, COLS), BF16)],
+        flops=WORK,
+    )
+    inner, own_up, own_down, own_columns = local(
+        interior_kernel,
+        (table, images, powers),
+        [SMEM, VMEM, VMEM],
+        [
             shape((2, ROWS - 2 * HALO, COLS)),
-            shape((4, ROWS, COLS), F32),
             shape((32, COLS)),
             shape((32, COLS)),
             shape((4, ROWS, 2 * LANES)),
-            shape((4, 8 * LANES, 2 * LANES)),
         ],
-        "own",
-        held=[pltpu.VMEM((4, 2 * ROWS, COLS), BF16)],
+        "interior",
         flops=WORK,
     )
     inner = lax.ppermute(inner, "epoch", swap)
@@ -558,8 +591,8 @@
     outs = [shape((4, 2, ROWS, COLS), F32), shape((4, ROWS, COLS), F32)]
     interferogram, coherence, power, edges = local(
         near_kernel,
-        (table, bands, terms, from_left, from_right),
-        [SMEM] + [VMEM] * 4,
+        (bands, edge_bands, slots, scale, terms, from_left, from_right),
+        [VMEM] * 7,
         [*outs, shape((ROWS, COLS), F32), shape((2, 3 * ROWS, LANES))],
         "near_pairs",
         kept=[ANY, ANY, VMEM, VMEM],
@@ -573,8 +606,8 @@
     )
     return local(
         far_kernel,
-        (table, bands, images, inner, power, rest, edges, interferogram, coherence),
-        [SMEM] + [VMEM] * 6 + [ANY] * 2,
+        (bands, far_band, scale, mine, inner, power, rest, edges, interferogram, coherence),
+        [VMEM] * 8 + [ANY] * 2,
         outs,
         "far_pair",
         kept=[ANY, ANY],
@@ -584,7 +617,7 @@
             pltpu.VMEM((1, 3, ROWS, COLS), F32),
             pltpu.SemaphoreType.DMA((1, BLOCKS // 2, 2)),
         ],
-        aliases={7: 0, 8: 1},
+        aliases={8: 0, 9: 1},
     )
 
 

time: 55.7 us -> 54.1 us (0.971)
  the two profiles are of different devices: /device:TPU:328 before, /device:TPU:32 now
where the time goes in v5:
time: 54.1 us; the launch traced here: 53.8 us
  starting transfers between devices  29.3 us (54%)
  Pallas kernels  13.5 us (25%)
  waiting for transfers between devices  8.52 us (16%)
  local copies, waits for them, and re-layouts  1.04 us (2%)
  between operations  0.75 us (1%)
  other arithmetic  0.7 us (1%)
    ppermute x1, starting transfers between devices, body(): border = lax.ppermute(border, 'epoch', swap)  15.3 us
    pallas_call x9, Pallas kernels, local(): pl.pallas_call(kernel, in_specs=places, out_specs=kept or [VMEM] * len(re...  13.5 us
    ppermute x4, starting transfers between devices, exchange(): return (lax.ppermute(last, axis, up), lax.ppermute(first, axis, down))  9.47 us
    ppermute x4, waiting for transfers between devices, exchange(): return (lax.ppermute(last, axis, up), lax.ppermute(first, axis, down))  5.77 us
    ppermute x1, waiting for transfers between devices, body(): border = lax.ppermute(border, 'epoch', swap)  2.75 us
    ppermute x1, starting transfers between devices, body(): inner = lax.ppermute(inner, 'epoch', swap)  1.92 us
    ppermute x1, starting transfers between devices, body(): lax.ppermute(slc_images, 'epoch', [(b + 1, b) for b in range(groups - 1)])  1.92 us
  transfers between devices with their start and end apart: 8, of which 3 were waited for; matrix products, arithmetic and copies ran while one was open for 1% of the time, Pallas kernels for 22%

profile of v5, /device:TPU:32, one launch (start us, length us, event | category | flops | bytes accessed | tf_op | source)
XLA Modules:
  0.0 53.8 jit_solution(18265402923310264374)
XLA Ops:
  0.6 1.9 %collective-permute-start.1 = (bf16[2,2,64,1024]{3,2,1,0:T(8,128)(2,1)}, bf16[2,2,64,1024]{3,2,1,0:T(8,128)(2,1)S(1)}, u32[]{:S(2)}, u32[]{:S(2)}) collective-permute-start(bf16[2,2,64,1024]{3,2,1,0:T(8,128)(2,1)} %images.1), channel_id=1, source_target_pairs={{16,0},{32,16},{48,32},{64,48},{80,64},{96,80},{112,96},{128,112},... | collective-permute-start | bytes 1572872 | tf_op jit(solution)/shard_map/ppermute | solution.py:511
  2.6 0.7 %pad_add_fusion.pairs = s32[2,132]{1,0:T(2,128)S(1)} fusion(s32[2,4]{1,0:T(2,128)} %bitcast.2, s32[2,128]{1,0:T(2,128)} %bitcast.3), kind=kLoop, calls=%fused_computation | loop fusion | flops 264 | bytes 2112 | tf_op jit(solution)/shard_map/concatenate | solution.py:509
  3.3 1.0 %copy-done = bf16[2,2,64,1024]{3,2,1,0:T(8,128)(2,1)S(1)} copy-done((bf16[2,2,64,1024]{3,2,1,0:T(8,128)(2,1)S(1)}, bf16[2,2,64,1024]{3,2,1,0:T(8,128)(2,1)}, u32[]{:S(2)}) %copy-start) | copy-done | bytes 524312
  4.3 0.7 %split.1 = (bf16[272,128]{1,0:T(8,128)(2,1)S(1)}, bf16[2,2,64,1024]{3,2,1,0:T(8,128)(2,1)S(1)}) custom-call(s32[2,132]{1,0:T(2,128)S(1)} %pad_add_fusion.pairs, bf16[2,2,64,1024]{3,2,1,0:T(8,128)(2,1)S(1)} %copy-done), custom_call_target="tpu_custom_call" | custom-call | tf_op jit(solution)/shard_map/split/pallas_call | solution.py:493
  5.0 15.3 %collective-permute-start.3 = (bf16[272,128]{1,0:T(8,128)(2,1)S(1)}, bf16[272,128]{1,0:T(8,128)(2,1)S(1)}, u32[]{:S(2)}, u32[]{:S(2)}) collective-permute-start(bf16[272,128]{1,0:T(8,128)(2,1)S(1)} %get-tuple-element.36), channel_id=1, source_target_pairs={{0,256},{16,272},{32,288},{48,304},{64,320},{80,336},{96,352},{112... | collective-permute-start | bytes 208904 | tf_op jit(solution)/shard_map/ppermute | solution.py:519
  20.2 0.7 %collective-permute-start.2 = (bf16[2,2,64,1024]{3,2,1,0:T(8,128)(2,1)S(1)}, bf16[2,2,64,1024]{3,2,1,0:T(8,128)(2,1)S(1)}, u32[]{:S(2)}, u32[]{:S(2)}) collective-permute-start(bf16[2,2,64,1024]{3,2,1,0:T(8,128)(2,1)S(1)} %get-tuple-element.25.images), channel_id=1, source_target_pairs={{480,496},{481,497},{482,498},{483,499},{484,500},{485,501},{486,5... | collective-permute-start | bytes 1572872 | tf_op jit(solution)/shard_map/ppermute | solution.py:551
  20.9 1.7 %references.1 = (f32[4,64,1024]{2,1,0:T(8,128)S(1)}, f32[2,48,1024]{2,1,0:T(8,128)S(1)}, bf16[4,1024,256]{2,1,0:T(8,128)(2,1)S(1)}, bf16[4,64,160]{2,1,0:T(8,128...) custom-call(s32[2,132]{1,0:T(2,128)S(1)} %pad_add_fusion.pairs, ...), custom_call_target="tpu_custom_call" | custom-call | flops 20000000000 | tf_op jit(solution)/shard_map/references/pallas_call | solution.py:493
  22.6 0.6 %interior.1 = (bf16[2,48,1024]{2,1,0:T(8,128)(2,1)S(1)}, bf16[32,1024]{1,0:T(8,128)(2,1)S(1)}, bf16[32,1024]{1,0:T(8,128)(2,1)S(1)}, bf16[4,64,256]{2,1,0:T(8,128)(2,1)S(1)}) custom-call(s32[2,132]{1,0:T(2,128)S(1)} %pad_add_fusion.pairs, bf16[2,2,64,1024]{3,2,1,0:T(8,128)(2,1)S(1)} %get-tuple-element.25.images, f32[4,64,1024]{2,1,0:T(8,128)S(1)} %get-tuple-element.30._.powers), custom_call_target="tpu_custom_call" | custom-call | flops 20000000000 | tf_op jit(solution)/shard_map/interior/pallas_call | solution.py:493
  23.3 1.9 %collective-permute-start = (bf16[2,48,1024]{2,1,0:T(8,128)(2,1)S(1)}, bf16[2,48,1024]{2,1,0:T(8,128)(2,1)S(1)}, u32[]{:S(2)}, u32[]{:S(2)}) collective-permute-start(bf16[2,48,1024]{2,1,0:T(8,128)(2,1)S(1)} %get-tuple-element.31), channel_id=1, source_target_pairs={{0,256},{16,272},{32,288},{48,304},{64,320},{80,336},{96,352},{112... | collective-permute-start | bytes 589832 | tf_op jit(solution)/shard_map/ppermute | solution.py:550
  25.2 2.7 %collective-permute-done.3.border = bf16[272,128]{1,0:T(8,128)(2,1)S(1)} collective-permute-done((bf16[272,128]{1,0:T(8,128)(2,1)S(1)}, bf16[272,128]{1,0:T(8,128)(2,1)S(1)}, u32[]{:S(2)}, u32[]{:S(2)}) %collective-permute-start.3) | collective-permute-done | bytes 69664 | tf_op jit(solution)/shard_map/ppermute | solution.py:519
  27.9 0.0 collective-permute-done.1.one
  27.9 0.0 collective-permute-done.2.other
  28.0 3.4 %collective-permute-start.4 = (bf16[80,1024]{1,0:T(8,128)(2,1)S(1)}, bf16[80,1024]{1,0:T(8,128)(2,1)S(1)}, u32[]{:S(2)}, u32[]{:S(2)}) collective-permute-start(bf16[80,1024]{1,0:T(8,128)(2,1)S(1)} %get-tuple-element.37), channel_id=1, source_target_pairs={{0,4},{4,8},{8,12},{1,5},{5,9},{9,13},{2,6},{6,10},{10,14},{3,7},{... | collective-permute-start | bytes 491528 | tf_op jit(solution)/shard_map/ppermute | solution.py:489
  31.4 1.3 %collective-permute-start.5 = (bf16[80,1024]{1,0:T(8,128)(2,1)S(1)}, bf16[80,1024]{1,0:T(8,128)(2,1)S(1)}, u32[]{:S(2)}, u32[]{:S(2)}) collective-permute-start(bf16[80,1024]{1,0:T(8,128)(2,1)S(1)} %get-tuple-element.38), channel_id=1, source_target_pairs={{4,0},{8,4},{12,8},{5,1},{9,5},{13,9},{6,2},{10,6},{14,10},{7,3},{... | collective-permute-start | bytes 491528 | tf_op jit(solution)/shard_map/ppermute | solution.py:489
  32.7 2.5 %near_rows.1.partial._ = f32[9,64,1024]{2,1,0:T(8,128)S(1)} custom-call(s32[2,132]{1,0:T(2,128)S(1)} %pad_add_fusion.pairs, bf16[2,2,64,1024]{3,2,1,0:T(8,128)(2,1)S(1)} %get-tuple-element.25.images, bf16[2,2,64,1024]{3,2,1,0:T(8,128)(2,1)S(1)} %collective-permute-done.1.one, bf16[2,2,64,1024]{3,2,1,0:T(8,128)(2,1)S(1)} %collective-permute-done.2.other), custom_call_target="tpu_custom_call" | custom-call | flops 100000000 | tf_op jit(solution)/shard_map/near_rows/pallas_call | solution.py:493
  35.2 3.4 %collective-permute-done.5.below = bf16[80,1024]{1,0:T(8,128)(2,1)S(1)} collective-permute-done((bf16[80,1024]{1,0:T(8,128)(2,1)S(1)}, bf16[80,1024]{1,0:T(8,128)(2,1)S(1)}, u32[]{:S(2)}, u32[]{:S(2)}) %collective-permute-start.5) | collective-permute-done | bytes 163872 | tf_op jit(solution)/shard_map/ppermute | solution.py:489
  38.6 0.2 pack_columns.1
  38.8 3.5 %collective-permute-start.6 = (bf16[80,128]{1,0:T(8,128)(2,1)S(1)}, bf16[80,128]{1,0:T(8,128)(2,1)S(1)}, u32[]{:S(2)}, u32[]{:S(2)}) collective-permute-start(bf16[80,128]{1,0:T(8,128)(2,1)S(1)} %get-tuple-element.41), channel_id=1, source_target_pairs={{0,1},{1,2},{2,3},{4,5},{5,6},{6,7},{8,9},{9,10},{10,11},{12,13},{... | collective-permute-start | bytes 61448 | tf_op jit(solution)/shard_map/ppermute | solution.py:489
  42.3 1.3 %collective-permute-start.7 = (bf16[80,128]{1,0:T(8,128)(2,1)S(1)}, bf16[80,128]{1,0:T(8,128)(2,1)S(1)}, u32[]{:S(2)}, u32[]{:S(2)}) collective-permute-start(bf16[80,128]{1,0:T(8,128)(2,1)S(1)} %get-tuple-element.42), channel_id=1, source_target_pairs={{1,0},{2,1},{3,2},{5,4},{6,5},{7,6},{9,8},{10,9},{11,10},{13,12},{... | collective-permute-start | bytes 61448 | tf_op jit(solution)/shard_map/ppermute | solution.py:489
  43.6 2.0 %halo_rows.1 = (bf16[2,832,1024]{2,1,0:T(8,128)(2,1)S(1)}, f32[3,64,1024]{2,1,0:T(8,128)S(1)}) custom-call(s32[2,132]{1,0:T(2,128)S(1)} %pad_add_fusion.pairs, f32[4,64,1024]{2,1,0:T(8,128)S(1)} %get-tuple-element.30._.powers, f32[9,64,1024]{2,1,0:T(8,128)S(1)} %near_rows.1.partial._, bf16[32,1024]{1,0:T(8,128)(2,1)S(1)} %get-tuple-element.34.own_up, ...), custom_call_target="tpu_custom_call" | custom-call | flops 100000000 | tf_op jit(solution)/shard_map/halo_rows/pallas_call | solution.py:493
  45.7 2.4 %collective-permute-done.7.from_right = bf16[80,128]{1,0:T(8,128)(2,1)S(1)} collective-permute-done((bf16[80,128]{1,0:T(8,128)(2,1)S(1)}, bf16[80,128]{1,0:T(8,128)(2,1)S(1)}, u32[]{:S(2)}, u32[]{:S(2)}) %collective-permute-start.7) | collective-permute-done | bytes 20512 | tf_op jit(solution)/shard_map/ppermute | solution.py:489
  48.0 3.9 %near_pairs.1 = (f32[4,2,64,1024]{3,2,1,0:T(8,128)}, f32[4,64,1024]{2,1,0:T(8,128)}, f32[64,1024]{1,0:T(8,128)S(1)}, bf16[2,192,128]{2,1,0:T(8,128)(2,1)S(1)}) custom-call(bf16[4,1024,256]{2,1,0:T(8,128)(2,1)S(1)} %get-tuple-element.26.bands, bf16[4,64,160]{2,1,0:T(8,128)(2,1)S(1)} %get-tuple-element.32.edge_bands, ...), custom_call_target="tpu_custom_call" | custom-call | tf_op jit(solution)/shard_map/near_pairs/pallas_call | solution.py:493
  51.9 0.0 collective-permute-done.inner
  51.9 1.9 %far_pair.1 = (f32[4,2,64,1024]{3,2,1,0:T(8,128)}, f32[4,64,1024]{2,1,0:T(8,128)}) custom-call(bf16[4,1024,256]{2,1,0:T(8,128)(2,1)S(1)} %get-tuple-element.26.bands, bf16[64,96]{1,0:T(8,128)(2,1)S(1)} %get-tuple-element.27.band, f32[4,8,256]{2,1,0:T(8,128)S(1)} %get-tuple-element.28.scale, ...), custom_call_target="tpu_custom_call", output_to_operand_aliasing={{0}: (8, {}), {1}: (9, {})} | custom-call | tf_op jit(solution)/shard_map/far_pair/pallas_call | solution.py:493
  (4 shorter events, 0.1 us)
Async XLA Ops:
  0.6 27.3 %collective-permute-start.1 = (bf16[2,2,64,1024]{3,2,1,0:T(8,128)(2,1)}, bf16[2,2,64,1024]{3,2,1,0:T(8,128)(2,1)S(1)}, u32[]{:S(2)}, u32[]{:S(2)}) collective-permute-start(bf16[2,2,64,1024]{3,2,1,0:T(8,128)(2,1)} %images.1), channel_id=1, source_target_pairs={{16,0},{32,16},{48,32},{64,48},{80,64},{96,80},{112,96},{128,112},... | collective-permute-start | bytes 1572872 | tf_op jit(solution)/shard_map/ppermute | solution.py:511
  3.3 1.0 %copy-start = (bf16[2,2,64,1024]{3,2,1,0:T(8,128)(2,1)S(1)}, bf16[2,2,64,1024]{3,2,1,0:T(8,128)(2,1)}, u32[]{:S(2)}) copy-start(bf16[2,2,64,1024]{3,2,1,0:T(8,128)(2,1)} %images.1) | copy-start | bytes 1572868
  5.0 23.0 %collective-permute-start.3 = (bf16[272,128]{1,0:T(8,128)(2,1)S(1)}, bf16[272,128]{1,0:T(8,128)(2,1)S(1)}, u32[]{:S(2)}, u32[]{:S(2)}) collective-permute-start(bf16[272,128]{1,0:T(8,128)(2,1)S(1)} %get-tuple-element.36), channel_id=1, source_target_pairs={{0,256},{16,272},{32,288},{48,304},{64,320},{80,336},{96,352},{112... | collective-permute-start | bytes 208904 | tf_op jit(solution)/shard_map/ppermute | solution.py:519
  20.2 7.7 %collective-permute-start.2 = (bf16[2,2,64,1024]{3,2,1,0:T(8,128)(2,1)S(1)}, bf16[2,2,64,1024]{3,2,1,0:T(8,128)(2,1)S(1)}, u32[]{:S(2)}, u32[]{:S(2)}) collective-permute-start(bf16[2,2,64,1024]{3,2,1,0:T(8,128)(2,1)S(1)} %get-tuple-element.25.images), channel_id=1, source_target_pairs={{480,496},{481,497},{482,498},{483,499},{484,500},{485,501},{486,5... | collective-permute-start | bytes 1572872 | tf_op jit(solution)/shard_map/ppermute | solution.py:551
  23.3 28.6 %collective-permute-start = (bf16[2,48,1024]{2,1,0:T(8,128)(2,1)S(1)}, bf16[2,48,1024]{2,1,0:T(8,128)(2,1)S(1)}, u32[]{:S(2)}, u32[]{:S(2)}) collective-permute-start(bf16[2,48,1024]{2,1,0:T(8,128)(2,1)S(1)} %get-tuple-element.31), channel_id=1, source_target_pairs={{0,256},{16,272},{32,288},{48,304},{64,320},{80,336},{96,352},{112... | collective-permute-start | bytes 589832 | tf_op jit(solution)/shard_map/ppermute | solution.py:550
  28.0 7.2 %collective-permute-start.4 = (bf16[80,1024]{1,0:T(8,128)(2,1)S(1)}, bf16[80,1024]{1,0:T(8,128)(2,1)S(1)}, u32[]{:S(2)}, u32[]{:S(2)}) collective-permute-start(bf16[80,1024]{1,0:T(8,128)(2,1)S(1)} %get-tuple-element.37), channel_id=1, source_target_pairs={{0,4},{4,8},{8,12},{1,5},{5,9},{9,13},{2,6},{6,10},{10,14},{3,7},{... | collective-permute-start | bytes 491528 | tf_op jit(solution)/shard_map/ppermute | solution.py:489
  31.4 7.2 %collective-permute-start.5 = (bf16[80,1024]{1,0:T(8,128)(2,1)S(1)}, bf16[80,1024]{1,0:T(8,128)(2,1)S(1)}, u32[]{:S(2)}, u32[]{:S(2)}) collective-permute-start(bf16[80,1024]{1,0:T(8,128)(2,1)S(1)} %get-tuple-element.38), channel_id=1, source_target_pairs={{4,0},{8,4},{12,8},{5,1},{9,5},{13,9},{6,2},{10,6},{14,10},{7,3},{... | collective-permute-start | bytes 491528 | tf_op jit(solution)/shard_map/ppermute | solution.py:489
  38.8 6.8 %collective-permute-start.6 = (bf16[80,128]{1,0:T(8,128)(2,1)S(1)}, bf16[80,128]{1,0:T(8,128)(2,1)S(1)}, u32[]{:S(2)}, u32[]{:S(2)}) collective-permute-start(bf16[80,128]{1,0:T(8,128)(2,1)S(1)} %get-tuple-element.41), channel_id=1, source_target_pairs={{0,1},{1,2},{2,3},{4,5},{5,6},{6,7},{8,9},{9,10},{10,11},{12,13},{... | collective-permute-start | bytes 61448 | tf_op jit(solution)/shard_map/ppermute | solution.py:489
  42.3 5.7 %collective-permute-start.7 = (bf16[80,128]{1,0:T(8,128)(2,1)S(1)}, bf16[80,128]{1,0:T(8,128)(2,1)S(1)}, u32[]{:S(2)}, u32[]{:S(2)}) collective-permute-start(bf16[80,128]{1,0:T(8,128)(2,1)S(1)} %get-tuple-element.42), channel_id=1, source_target_pairs={{1,0},{2,1},{3,2},{5,4},{6,5},{7,6},{9,8},{10,9},{11,10},{13,12},{... | collective-permute-start | bytes 61448 | tf_op jit(solution)/shard_map/ppermute | solution.py:489

commit v6 on v5

--- a/solution.py
+++ b/solution.py
@@ -409,31 +409,30 @@
 
     def edge(target, values, pair, fields):
         for f, value in enumerate(fields(*values)):
-            put_split(products, f, everything, value)
-            put_terms(target, f, row_sums(edge_bands[pair], products[f]))
-
-    def one_pair(step, carry):
-        pair = jnp.where(step == 0, 0, step + 1)
+            put_split(products.at[pair], f, everything, value)
+            put_terms(target, f, row_sums(edge_bands[pair], products[pair, f]))
+
+    for step, pair in enumerate((0, 2, 3)):
         values = [halo_of(pair, k, field) for k in range(2) for field in range(2)]
-        edge(edges, values, pair, fields_of)
-        at = pl.ds(pl.multiple_of(step * 4 * ROWS, 4 * ROWS), 4 * ROWS)
+        edge(edges.at[pair], values, pair, fields_of)
+        at = slice(step * 4 * ROWS, (step + 1) * 4 * ROWS)
         for j in range(BLOCKS // 2):
             blocks = column_sums(
-                j, bands[pair], lambda term, columns: terms[term, at, columns], lambda term: edges[term]
+                j,
+                bands[pair],
+                lambda term, columns, at=at: terms[term, at, columns],
+                lambda term, pair=pair: edges[pair, term],
             )
             finish(*blocks, scale[pair], pair, step, j, results)
-        return carry
-
-    lax.fori_loop(0, 3, one_pair, 0)
 
     reference = [halo_of(1, 0, field) for field in range(2)]
-    edge(edges, reference, 1, power_of)
+    edge(edges.at[1], reference, 1, power_of)
     for j in range(BLOCKS // 2):
         (far_power[:, j * 256 : (j + 1) * 256],) = column_sums(
             j,
             bands[1],
             lambda term, columns: terms[term, 12 * ROWS :, columns],
-            lambda term: edges[term, :ROWS, :],
+            lambda term: edges[1, term, :ROWS, :],
         )
     edge(far_edges, [*reference, halos[4, 0], halos[4, 1]], 1, far_fields)
     for step, pair in enumerate((0, 2, 3)):
@@ -598,8 +597,8 @@
         kept=[ANY, ANY, VMEM, VMEM],
         held=[
             pltpu.VMEM((5, 2, PADDED, LANES), F32),
-            pltpu.VMEM((4, 2 * PADDED, LANES), BF16),
-            pltpu.VMEM((2, 4 * ROWS, LANES), BF16),
+            pltpu.VMEM((4, 4, 2 * PADDED, LANES), BF16),
+            pltpu.VMEM((4, 2, 4 * ROWS, LANES), BF16),
             pltpu.VMEM((3, 3, ROWS, COLS), F32),
             pltpu.SemaphoreType.DMA((3, BLOCKS // 2, 2)),
         ],

time: 54.1 us -> 53.8 us (level)
  the two profiles are of different devices: /device:TPU:32 before, /device:TPU:42 now
where the time goes in v6:
time: 53.8 us; the launch traced here: 53.4 us
  starting transfers between devices  31.5 us (59%)
  Pallas kernels  13.2 us (25%)
  waiting for transfers between devices  6.3 us (12%)
  local copies, waits for them, and re-layouts  1.04 us (2%)
  between operations  0.75 us (1%)
  other arithmetic  0.7 us (1%)
    ppermute x1, starting transfers between devices, body(): border = lax.ppermute(border, 'epoch', swap)  15.3 us
    pallas_call x9, Pallas kernels, local(): pl.pallas_call(kernel, in_specs=places, out_specs=kept or [VMEM] * len(re...  13.2 us
    ppermute x4, starting transfers between devices, exchange(): return (lax.ppermute(last, axis, up), lax.ppermute(first, axis, down))  11.7 us
    ppermute x4, waiting for transfers between devices, exchange(): return (lax.ppermute(last, axis, up), lax.ppermute(first, axis, down))  3.55 us
    ppermute x1, waiting for transfers between devices, body(): border = lax.ppermute(border, 'epoch', swap)  2.75 us
    ppermute x1, starting transfers between devices, body(): lax.ppermute(slc_images, 'epoch', [(b + 1, b) for b in range(groups - 1)])  1.92 us
    ppermute x1, starting transfers between devices, body(): inner = lax.ppermute(inner, 'epoch', swap)  1.92 us
  transfers between devices with their start and end apart: 8, of which 3 were waited for; matrix products, arithmetic and copies ran while one was open for 1% of the time, Pallas kernels for 21%

profile of v6, /device:TPU:42, one launch (start us, length us, event | category | flops | bytes accessed | tf_op | source)
XLA Modules:
  0.0 53.4 jit_solution(10579712408125497825)
XLA Ops:
  0.6 1.9 %collective-permute-start.1 = (bf16[2,2,64,1024]{3,2,1,0:T(8,128)(2,1)}, bf16[2,2,64,1024]{3,2,1,0:T(8,128)(2,1)S(1)}, u32[]{:S(2)}, u32[]{:S(2)}) collective-permute-start(bf16[2,2,64,1024]{3,2,1,0:T(8,128)(2,1)} %images.1), channel_id=1, source_target_pairs={{16,0},{32,16},{48,32},{64,48},{80,64},{96,80},{112,96},{128,112},... | collective-permute-start | bytes 1572872 | tf_op jit(solution)/shard_map/ppermute | solution.py:510
  2.6 0.7 %pad_add_fusion.pairs = s32[2,132]{1,0:T(2,128)S(1)} fusion(s32[2,4]{1,0:T(2,128)} %bitcast.2, s32[2,128]{1,0:T(2,128)} %bitcast.3), kind=kLoop, calls=%fused_computation | loop fusion | flops 264 | bytes 2112 | tf_op jit(solution)/shard_map/concatenate | solution.py:508
  3.3 1.0 %copy-done = bf16[2,2,64,1024]{3,2,1,0:T(8,128)(2,1)S(1)} copy-done((bf16[2,2,64,1024]{3,2,1,0:T(8,128)(2,1)S(1)}, bf16[2,2,64,1024]{3,2,1,0:T(8,128)(2,1)}, u32[]{:S(2)}) %copy-start) | copy-done | bytes 524312
  4.3 0.7 %split.1 = (bf16[272,128]{1,0:T(8,128)(2,1)S(1)}, bf16[2,2,64,1024]{3,2,1,0:T(8,128)(2,1)S(1)}) custom-call(s32[2,132]{1,0:T(2,128)S(1)} %pad_add_fusion.pairs, bf16[2,2,64,1024]{3,2,1,0:T(8,128)(2,1)S(1)} %copy-done), custom_call_target="tpu_custom_call" | custom-call | tf_op jit(solution)/shard_map/split/pallas_call | solution.py:492
  5.0 15.3 %collective-permute-start.3 = (bf16[272,128]{1,0:T(8,128)(2,1)S(1)}, bf16[272,128]{1,0:T(8,128)(2,1)S(1)}, u32[]{:S(2)}, u32[]{:S(2)}) collective-permute-start(bf16[272,128]{1,0:T(8,128)(2,1)S(1)} %get-tuple-element.36), channel_id=1, source_target_pairs={{0,256},{16,272},{32,288},{48,304},{64,320},{80,336},{96,352},{112... | collective-permute-start | bytes 208904 | tf_op jit(solution)/shard_map/ppermute | solution.py:518
  20.2 0.7 %collective-permute-start.2 = (bf16[2,2,64,1024]{3,2,1,0:T(8,128)(2,1)S(1)}, bf16[2,2,64,1024]{3,2,1,0:T(8,128)(2,1)S(1)}, u32[]{:S(2)}, u32[]{:S(2)}) collective-permute-start(bf16[2,2,64,1024]{3,2,1,0:T(8,128)(2,1)S(1)} %get-tuple-element.25.images), channel_id=1, source_target_pairs={{480,496},{481,497},{482,498},{483,499},{484,500},{485,501},{486,5... | collective-permute-start | bytes 1572872 | tf_op jit(solution)/shard_map/ppermute | solution.py:550
  20.9 1.7 %references.1 = (f32[4,64,1024]{2,1,0:T(8,128)S(1)}, f32[2,48,1024]{2,1,0:T(8,128)S(1)}, bf16[4,1024,256]{2,1,0:T(8,128)(2,1)S(1)}, bf16[4,64,160]{2,1,0:T(8,128...) custom-call(s32[2,132]{1,0:T(2,128)S(1)} %pad_add_fusion.pairs, ...), custom_call_target="tpu_custom_call" | custom-call | flops 20000000000 | tf_op jit(solution)/shard_map/references/pallas_call | solution.py:492
  22.6 0.6 %interior.1 = (bf16[2,48,1024]{2,1,0:T(8,128)(2,1)S(1)}, bf16[32,1024]{1,0:T(8,128)(2,1)S(1)}, bf16[32,1024]{1,0:T(8,128)(2,1)S(1)}, bf16[4,64,256]{2,1,0:T(8,128)(2,1)S(1)}) custom-call(s32[2,132]{1,0:T(2,128)S(1)} %pad_add_fusion.pairs, bf16[2,2,64,1024]{3,2,1,0:T(8,128)(2,1)S(1)} %get-tuple-element.25.images, f32[4,64,1024]{2,1,0:T(8,128)S(1)} %get-tuple-element.30._.powers), custom_call_target="tpu_custom_call" | custom-call | flops 20000000000 | tf_op jit(solution)/shard_map/interior/pallas_call | solution.py:492
  23.3 1.9 %collective-permute-start = (bf16[2,48,1024]{2,1,0:T(8,128)(2,1)S(1)}, bf16[2,48,1024]{2,1,0:T(8,128)(2,1)S(1)}, u32[]{:S(2)}, u32[]{:S(2)}) collective-permute-start(bf16[2,48,1024]{2,1,0:T(8,128)(2,1)S(1)} %get-tuple-element.31), channel_id=1, source_target_pairs={{0,256},{16,272},{32,288},{48,304},{64,320},{80,336},{96,352},{112... | collective-permute-start | bytes 589832 | tf_op jit(solution)/shard_map/ppermute | solution.py:549
  25.2 2.7 %collective-permute-done.3.border = bf16[272,128]{1,0:T(8,128)(2,1)S(1)} collective-permute-done((bf16[272,128]{1,0:T(8,128)(2,1)S(1)}, bf16[272,128]{1,0:T(8,128)(2,1)S(1)}, u32[]{:S(2)}, u32[]{:S(2)}) %collective-permute-start.3) | collective-permute-done | bytes 69664 | tf_op jit(solution)/shard_map/ppermute | solution.py:518
  27.9 0.0 collective-permute-done.1.one
  27.9 0.0 collective-permute-done.2.other
  28.0 3.4 %collective-permute-start.4 = (bf16[80,1024]{1,0:T(8,128)(2,1)S(1)}, bf16[80,1024]{1,0:T(8,128)(2,1)S(1)}, u32[]{:S(2)}, u32[]{:S(2)}) collective-permute-start(bf16[80,1024]{1,0:T(8,128)(2,1)S(1)} %get-tuple-element.37), channel_id=1, source_target_pairs={{0,4},{4,8},{8,12},{1,5},{5,9},{9,13},{2,6},{6,10},{10,14},{3,7},{... | collective-permute-start | bytes 491528 | tf_op jit(solution)/shard_map/ppermute | solution.py:488
  31.4 2.4 %collective-permute-start.5 = (bf16[80,1024]{1,0:T(8,128)(2,1)S(1)}, bf16[80,1024]{1,0:T(8,128)(2,1)S(1)}, u32[]{:S(2)}, u32[]{:S(2)}) collective-permute-start(bf16[80,1024]{1,0:T(8,128)(2,1)S(1)} %get-tuple-element.38), channel_id=1, source_target_pairs={{4,0},{8,4},{12,8},{5,1},{9,5},{13,9},{6,2},{10,6},{14,10},{7,3},{... | collective-permute-start | bytes 491528 | tf_op jit(solution)/shard_map/ppermute | solution.py:488
  33.9 2.5 %near_rows.1.partial._ = f32[9,64,1024]{2,1,0:T(8,128)S(1)} custom-call(s32[2,132]{1,0:T(2,128)S(1)} %pad_add_fusion.pairs, bf16[2,2,64,1024]{3,2,1,0:T(8,128)(2,1)S(1)} %get-tuple-element.25.images, bf16[2,2,64,1024]{3,2,1,0:T(8,128)(2,1)S(1)} %collective-permute-done.1.one, bf16[2,2,64,1024]{3,2,1,0:T(8,128)(2,1)S(1)} %collective-permute-done.2.other), custom_call_target="tpu_custom_call" | custom-call | flops 100000000 | tf_op jit(solution)/shard_map/near_rows/pallas_call | solution.py:492
  36.4 0.0 collective-permute-done.4.above
  36.4 2.3 %collective-permute-done.5.below = bf16[80,1024]{1,0:T(8,128)(2,1)S(1)} collective-permute-done((bf16[80,1024]{1,0:T(8,128)(2,1)S(1)}, bf16[80,1024]{1,0:T(8,128)(2,1)S(1)}, u32[]{:S(2)}, u32[]{:S(2)}) %collective-permute-start.5) | collective-permute-done | bytes 163872 | tf_op jit(solution)/shard_map/ppermute | solution.py:488
  38.6 0.2 pack_columns.1
  38.8 3.5 %collective-permute-start.6 = (bf16[80,128]{1,0:T(8,128)(2,1)S(1)}, bf16[80,128]{1,0:T(8,128)(2,1)S(1)}, u32[]{:S(2)}, u32[]{:S(2)}) collective-permute-start(bf16[80,128]{1,0:T(8,128)(2,1)S(1)} %get-tuple-element.41), channel_id=1, source_target_pairs={{0,1},{1,2},{2,3},{4,5},{5,6},{6,7},{8,9},{9,10},{10,11},{12,13},{... | collective-permute-start | bytes 61448 | tf_op jit(solution)/shard_map/ppermute | solution.py:488
  42.3 2.4 %collective-permute-start.7 = (bf16[80,128]{1,0:T(8,128)(2,1)S(1)}, bf16[80,128]{1,0:T(8,128)(2,1)S(1)}, u32[]{:S(2)}, u32[]{:S(2)}) collective-permute-start(bf16[80,128]{1,0:T(8,128)(2,1)S(1)} %get-tuple-element.42), channel_id=1, source_target_pairs={{1,0},{2,1},{3,2},{5,4},{6,5},{7,6},{9,8},{10,9},{11,10},{13,12},{... | collective-permute-start | bytes 61448 | tf_op jit(solution)/shard_map/ppermute | solution.py:488
  44.7 2.0 %halo_rows.1 = (bf16[2,832,1024]{2,1,0:T(8,128)(2,1)S(1)}, f32[3,64,1024]{2,1,0:T(8,128)S(1)}) custom-call(s32[2,132]{1,0:T(2,128)S(1)} %pad_add_fusion.pairs, f32[4,64,1024]{2,1,0:T(8,128)S(1)} %get-tuple-element.30._.powers, f32[9,64,1024]{2,1,0:T(8,128)S(1)} %near_rows.1.partial._, bf16[32,1024]{1,0:T(8,128)(2,1)S(1)} %get-tuple-element.34.own_up, ...), custom_call_target="tpu_custom_call" | custom-call | flops 100000000 | tf_op jit(solution)/shard_map/halo_rows/pallas_call | solution.py:492
  46.7 1.3 %collective-permute-done.7.from_right = bf16[80,128]{1,0:T(8,128)(2,1)S(1)} collective-permute-done((bf16[80,128]{1,0:T(8,128)(2,1)S(1)}, bf16[80,128]{1,0:T(8,128)(2,1)S(1)}, u32[]{:S(2)}, u32[]{:S(2)}) %collective-permute-start.7) | collective-permute-done | bytes 20512 | tf_op jit(solution)/shard_map/ppermute | solution.py:488
  48.0 3.6 %near_pairs.1 = (f32[4,2,64,1024]{3,2,1,0:T(8,128)}, f32[4,64,1024]{2,1,0:T(8,128)}, f32[64,1024]{1,0:T(8,128)S(1)}, bf16[2,192,128]{2,1,0:T(8,128)(2,1)S(1)}) custom-call(bf16[4,1024,256]{2,1,0:T(8,128)(2,1)S(1)} %get-tuple-element.26.bands, bf16[4,64,160]{2,1,0:T(8,128)(2,1)S(1)} %get-tuple-element.32.edge_bands, ...), custom_call_target="tpu_custom_call" | custom-call | tf_op jit(solution)/shard_map/near_pairs/pallas_call | solution.py:492
  51.6 1.9 %far_pair.1 = (f32[4,2,64,1024]{3,2,1,0:T(8,128)}, f32[4,64,1024]{2,1,0:T(8,128)}) custom-call(bf16[4,1024,256]{2,1,0:T(8,128)(2,1)S(1)} %get-tuple-element.26.bands, bf16[64,96]{1,0:T(8,128)(2,1)S(1)} %get-tuple-element.27.band, f32[4,8,256]{2,1,0:T(8,128)S(1)} %get-tuple-element.28.scale, ...), custom_call_target="tpu_custom_call", output_to_operand_aliasing={{0}: (8, {}), {1}: (9, {})} | custom-call | tf_op jit(solution)/shard_map/far_pair/pallas_call | solution.py:492
  (4 shorter events, 0.1 us)
Async XLA Ops:
  0.6 27.3 %collective-permute-start.1 = (bf16[2,2,64,1024]{3,2,1,0:T(8,128)(2,1)}, bf16[2,2,64,1024]{3,2,1,0:T(8,128)(2,1)S(1)}, u32[]{:S(2)}, u32[]{:S(2)}) collective-permute-start(bf16[2,2,64,1024]{3,2,1,0:T(8,128)(2,1)} %images.1), channel_id=1, source_target_pairs={{16,0},{32,16},{48,32},{64,48},{80,64},{96,80},{112,96},{128,112},... | collective-permute-start | bytes 1572872 | tf_op jit(solution)/shard_map/ppermute | solution.py:510
  3.3 1.0 %copy-start = (bf16[2,2,64,1024]{3,2,1,0:T(8,128)(2,1)S(1)}, bf16[2,2,64,1024]{3,2,1,0:T(8,128)(2,1)}, u32[]{:S(2)}) copy-start(bf16[2,2,64,1024]{3,2,1,0:T(8,128)(2,1)} %images.1) | copy-start | bytes 1572868
  5.0 23.0 %collective-permute-start.3 = (bf16[272,128]{1,0:T(8,128)(2,1)S(1)}, bf16[272,128]{1,0:T(8,128)(2,1)S(1)}, u32[]{:S(2)}, u32[]{:S(2)}) collective-permute-start(bf16[272,128]{1,0:T(8,128)(2,1)S(1)} %get-tuple-element.36), channel_id=1, source_target_pairs={{0,256},{16,272},{32,288},{48,304},{64,320},{80,336},{96,352},{112... | collective-permute-start | bytes 208904 | tf_op jit(solution)/shard_map/ppermute | solution.py:518
  20.2 7.7 %collective-permute-start.2 = (bf16[2,2,64,1024]{3,2,1,0:T(8,128)(2,1)S(1)}, bf16[2,2,64,1024]{3,2,1,0:T(8,128)(2,1)S(1)}, u32[]{:S(2)}, u32[]{:S(2)}) collective-permute-start(bf16[2,2,64,1024]{3,2,1,0:T(8,128)(2,1)S(1)} %get-tuple-element.25.images), channel_id=1, source_target_pairs={{480,496},{481,497},{482,498},{483,499},{484,500},{485,501},{486,5... | collective-permute-start | bytes 1572872 | tf_op jit(solution)/shard_map/ppermute | solution.py:550
  23.3 28.3 %collective-permute-start = (bf16[2,48,1024]{2,1,0:T(8,128)(2,1)S(1)}, bf16[2,48,1024]{2,1,0:T(8,128)(2,1)S(1)}, u32[]{:S(2)}, u32[]{:S(2)}) collective-permute-start(bf16[2,48,1024]{2,1,0:T(8,128)(2,1)S(1)} %get-tuple-element.31), channel_id=1, source_target_pairs={{0,256},{16,272},{32,288},{48,304},{64,320},{80,336},{96,352},{112... | collective-permute-start | bytes 589832 | tf_op jit(solution)/shard_map/ppermute | solution.py:549
  28.0 8.4 %collective-permute-start.4 = (bf16[80,1024]{1,0:T(8,128)(2,1)S(1)}, bf16[80,1024]{1,0:T(8,128)(2,1)S(1)}, u32[]{:S(2)}, u32[]{:S(2)}) collective-permute-start(bf16[80,1024]{1,0:T(8,128)(2,1)S(1)} %get-tuple-element.37), channel_id=1, source_target_pairs={{0,4},{4,8},{8,12},{1,5},{5,9},{9,13},{2,6},{6,10},{10,14},{3,7},{... | collective-permute-start | bytes 491528 | tf_op jit(solution)/shard_map/ppermute | solution.py:488
  31.4 7.2 %collective-permute-start.5 = (bf16[80,1024]{1,0:T(8,128)(2,1)S(1)}, bf16[80,1024]{1,0:T(8,128)(2,1)S(1)}, u32[]{:S(2)}, u32[]{:S(2)}) collective-permute-start(bf16[80,1024]{1,0:T(8,128)(2,1)S(1)} %get-tuple-element.38), channel_id=1, source_target_pairs={{4,0},{8,4},{12,8},{5,1},{9,5},{13,9},{6,2},{10,6},{14,10},{7,3},{... | collective-permute-start | bytes 491528 | tf_op jit(solution)/shard_map/ppermute | solution.py:488
  38.8 7.9 %collective-permute-start.6 = (bf16[80,128]{1,0:T(8,128)(2,1)S(1)}, bf16[80,128]{1,0:T(8,128)(2,1)S(1)}, u32[]{:S(2)}, u32[]{:S(2)}) collective-permute-start(bf16[80,128]{1,0:T(8,128)(2,1)S(1)} %get-tuple-element.41), channel_id=1, source_target_pairs={{0,1},{1,2},{2,3},{4,5},{5,6},{6,7},{8,9},{9,10},{10,11},{12,13},{... | collective-permute-start | bytes 61448 | tf_op jit(solution)/shard_map/ppermute | solution.py:488
  42.3 5.7 %collective-permute-start.7 = (bf16[80,128]{1,0:T(8,128)(2,1)S(1)}, bf16[80,128]{1,0:T(8,128)(2,1)S(1)}, u32[]{:S(2)}, u32[]{:S(2)}) collective-permute-start(bf16[80,128]{1,0:T(8,128)(2,1)S(1)} %get-tuple-element.42), channel_id=1, source_target_pairs={{1,0},{2,1},{3,2},{5,4},{6,5},{7,6},{9,8},{10,9},{11,10},{13,12},{... | collective-permute-start | bytes 61448 | tf_op jit(solution)/shard_map/ppermute | solution.py:488
